TPU v7x, 256 devices: a whole 4x4x8 slice. The times are simulated.
256 devices in a mesh: sub: 16 (over z_lo, y, core), col: 16 (over z_hi, x).
Axes of the slice: x: 4, y: 4, z: 8 (z_hi: 4, z_lo: 2; z = z_hi * 2 + z_lo), core: 2. Of those that a mesh axis runs over, the one named last changes fastest.
Arguments:
- initial_state: float32 [5, 64, 32768], P(None, None, ('sub', 'col')), may hold values from -6 to 6
- state_cotangent: float32 [5, 64, 32768], P(None, None, ('sub', 'col')), may hold values from -6 to 6
- element_order: int32 [256, 128], P(('sub', 'col')), may hold values from 0 to 127, each once within a row
- element_weight: float32 [32768], P(('sub', 'col')), may hold values from 1 to 3
- element_diffusivity: float32 [32768], P(('sub', 'col')), may hold values from 0.1 to 0.4
- in_weight: float32 [64, 5], replicated, may hold values from -2.5 to 2.5
- in_bias: float32 [64], replicated, may hold values from -3 to 3
- mid_weight: float32 [64, 64], replicated, may hold values from -0.75 to 0.75
- mid_bias: float32 [64], replicated, may hold values from -3 to 3
- out_weight: float32 [5, 64], replicated, may hold values from -0.75 to 0.75
- out_bias: float32 [5], replicated, may hold values from -6 to 6
Outputs:
- final_state: float32 [5, 64, 32768], P(None, None, ('sub', 'col'))
- initial_adjoint: float32 [5, 64, 32768], P(None, None, ('sub', 'col'))
- grad_in_weight: float32 [64, 5], replicated
- grad_in_bias: float32 [64], replicated
- grad_mid_weight: float32 [64, 64], replicated
- grad_mid_bias: float32 [64], replicated
- grad_out_weight: float32 [5, 64], replicated
- grad_out_bias: float32 [5], replicated
Inputs may be any that keep to these rules, and one draw needn't show every extreme that they name: `element_order`: each row is a permutation of the local element positions 0 .. 127.
All inputs are finite; a program needn't handle non-finite values.
Results may differ from a plain program's by a relative error of at most 0.00027.
Values sent between devices are 32-bit elements; how exact they have to be, the bound alone decides.
No kernel may reach another device: no remote copies, remote signals or barrier semaphores. Data moves between devices by JAX's collectives and lax.ppermute only.
A program may use at most 128 MiB of HBM per device.

v0:
```python
import math

import jax
import jax.numpy as jnp
import numpy as np
from jax import lax
from jax.experimental import pallas as pl
from jax.experimental.pallas import tpu as pltpu
from jax.sharding import PartitionSpec as P

F = 5
STEP = 0.05
CH = 16
NW = CH * 128
f32, bf16 = jnp.float32, jnp.bfloat16
VM = pl.BlockSpec(memory_space=pltpu.VMEM)


def stiffness_matrix():
    at = [-1.0, -math.sqrt(0.2), math.sqrt(0.2), 1.0]
    w = np.array([1.0 / 6.0, 5.0 / 6.0, 5.0 / 6.0, 1.0 / 6.0])
    prods = [np.prod([at[r] - at[p] for p in range(4) if p != r]) for r in range(4)]
    d = np.zeros((4, 4))
    for r in range(4):
        for c in range(4):
            if r == c:
                d[r, c] = sum(1.0 / (at[r] - at[p]) for p in range(4) if p != r)
            else:
                d[r, c] = prods[r] / (prods[c] * (at[r] - at[c]))
    s = d.T @ np.diag(w) @ d
    m = np.diag(w)
    k = np.kron(m, np.kron(s, m)) + np.kron(m, np.kron(m, s)) + np.kron(s, np.kron(m, m))
    k = k.astype(np.float32)
    hi = k.astype(bf16).astype(np.float32)
    lo = k - hi
    return np.concatenate([hi, hi, lo], axis=1).astype(bf16)


def iota(shape, dim):
    return lax.broadcasted_iota(jnp.int32, shape, dim)


def next_k(x):
    ax = x.ndim - 1
    lane = iota(x.shape, ax) & 63
    return jnp.where(lane == 63, pltpu.roll(x, 63, ax), pltpu.roll(x, 127, ax))


def prev_k(x):
    ax = x.ndim - 1
    lane = iota(x.shape, ax) & 63
    return jnp.where(lane == 0, pltpu.roll(x, 65, ax), pltpu.roll(x, 1, ax))


def zsum(v):
    n = v.shape[0]
    top = v[:, 48:64] + next_k(v[:, 0:16])
    return jnp.concatenate([v[:, 16:48], top], axis=1)


def zfill(w):
    return jnp.concatenate([prev_k(w[:, 32:48]), w], axis=1)


def sroll(x, s):
    return pltpu.roll(x, s % 8, x.ndim - 2) if s % 8 else x


def xpack(w):
    n = w.shape[0]
    h = n // 2
    t = w.reshape(n, 3, 2, 8, 128)
    v0, v1 = t[:, :, 0].reshape(n * 3, 8, 128), t[:, :, 1].reshape(n * 3, 8, 128)
    low = iota((h * 3, 8, 128), 1) < 4
    up = jnp.where(low, sroll(v1[: h * 3], 4), v1[h * 3 :])
    dn = jnp.where(low, v0[: h * 3], sroll(v0[h * 3 :], 4))
    return up, dn


def xadd(w, rp, rm):
    n = w.shape[0]
    h = n // 2
    t = w.reshape(n, 3, 2, 8, 128)
    v0, v1 = t[:, :, 0].reshape(n * 3, 8, 128), t[:, :, 1].reshape(n * 3, 8, 128)
    low = iota((h * 3, 8, 128), 1) < 4
    zero = jnp.zeros_like(rp)
    a0 = jnp.concatenate([jnp.where(low, rp, zero), jnp.where(low, sroll(rp, 4), zero)], axis=0)
    a1 = jnp.concatenate([jnp.where(low, zero, sroll(rm, 4)), jnp.where(low, zero, rm)], axis=0)
    v0, v1 = v0 + a0, v1 + a1
    return v0, v1


def ylocal(v):
    b = iota(v.shape, 1) & 3
    left = iota(v.shape, 2) < 64
    d = jnp.where(b == 0, sroll(v, 5), sroll(v, 3))
    d = pltpu.roll(d, 64, 2)
    zero = jnp.zeros_like(v)
    here = ((b == 0) & (~left)) | ((b == 3) & left)
    out = ((b == 0) & left) | ((b == 3) & (~left))
    return v + jnp.where(here, d, zero), jnp.where(out, d, zero)


def xy_body(n, w_ref, rp_ref, rm_ref, wo_ref, y_ref):
    w = w_ref[...]
    v0, v1 = xadd(w, rp_ref[...], rm_ref[...])
    for part, v in enumerate((v0, v1)):
        v, e = ylocal(v)
        wo_ref[:, :, part] = v.reshape(n, 3, 8, 128)
        e = e.reshape(n, 3, 8, 128)
        y_ref[:, part] = e[:, 0] + sroll(e[:, 1], 1) + sroll(e[:, 2], 2)


def yadd(w, yl, yr):
    n = w.shape[0]
    left = iota((n * 2, 8, 128), 2) < 64
    b = iota((n * 2, 8, 128), 1) & 3
    z = jnp.where(left, yl.reshape(n * 2, 8, 128), yr.reshape(n * 2, 8, 128))
    use = ((b == 0) & left) | ((b == 3) & (~left))
    parts = []
    for q in range(3):
        add = jnp.where(use, sroll(z, -q), jnp.zeros_like(z)).reshape(n, 2, 8, 128)
        parts.append((w[:, q] + add).reshape(n, 16, 128))
    return jnp.concatenate(parts, axis=1)


def one_hot(order):
    row = jnp.broadcast_to(order, (128, 128))
    return jnp.where(row == iota((128, 128), 0), 1.0, 0.0).astype(bf16)


def split3(x):
    h = x.astype(bf16)
    r = x - h.astype(f32)
    m = r.astype(bf16)
    l = (r - m.astype(f32)).astype(bf16)
    return h, m, l


def permute_nt(x, g):
    dims = (((1,), (1,)), ((), ()))
    h, m, l = (lax.dot_general(p, g, dims, preferred_element_type=f32) for p in split3(x))
    return h + m + l


def permute_nn(x, g):
    h, m, l = (jnp.dot(p, g, preferred_element_type=f32) for p in split3(x))
    return h + m + l


def quad(shape):
    r = iota(shape, 0)
    w = 1.0
    for i in (r >> 4, (r >> 2) & 3, r & 3):
        w = w * jnp.where((i == 0) | (i == 3), 1.0 / 6.0, 5.0 / 6.0)
    return w


def start_body(s_ref, c_ref, o_ref, ew_ref, ed_ref, w_ref, up_ref, dn_ref, mk_ref):
    g = one_hot(o_ref[...])
    rows = []
    for ref in (s_ref, c_ref):
        for f in range(F):
            for q in range(4):
                rows.append(ref[f, pl.ds(q, 16, stride=4), :])
    el = jnp.concatenate(
        [jnp.broadcast_to(ew_ref[...], (8, 128)), jnp.broadcast_to(ed_ref[...], (8, 128))], axis=0
    )
    x = permute_nt(jnp.concatenate(rows + [el], axis=0), g)
    mass = quad((64, 128)) * x[640:641]
    mk_ref[...] = x[640:656]
    s = x[:320].reshape(F, 64, 128) * mass[None]
    c = x[320:640].reshape(F, 64, 128)
    v = jnp.concatenate([s, mass[None], c, jnp.zeros((1, 64, 128), f32)], axis=0)
    w = zsum(v)
    w_ref[...] = w
    up_ref[...], dn_ref[...] = xpack(w)


def stiffness(v, kmat, kappa):
    n = v.shape[0]
    x = jnp.concatenate([v[i] for i in range(n)], axis=1)
    h = x.astype(bf16)
    l = (x - h.astype(f32)).astype(bf16)
    y = jnp.dot(kmat, jnp.concatenate([h, l, h], axis=0), preferred_element_type=f32)
    return jnp.stack([y[:, i * 128 : (i + 1) * 128] * kappa for i in range(n)], axis=0)


def state_body(w_ref, yl_ref, yr_ref, mk_ref, k_ref, sa_ref, im_ref, w2_ref, up_ref, dn_ref):
    v = zfill(yadd(w_ref[...], yl_ref[...], yr_ref[...]))
    im = 1.0 / v[F]
    im_ref[...] = im
    sa = jnp.concatenate([v[:F], v[F + 1 : 2 * F + 1]], axis=0) * im[None]
    sa_ref[...] = sa
    w = zsum(stiffness(sa, k_ref[...], mk_ref[8:9]))
    w2_ref[...] = w
    up_ref[...], dn_ref[...] = xpack(w)


def weights(p_ref):
    p = p_ref[...]
    h = p.astype(bf16)
    l = (p - h.astype(f32)).astype(bf16)
    hf, lf = h.astype(f32), l.astype(f32)
    col = iota((128, 256), 1)
    wide = (col < 128) | (col == 192)
    big = jnp.where(wide, hf[0:128], lf[0:128]).astype(bf16)
    thin = jnp.where(iota((128, 256), 1) < 16, hf[128:256], lf[128:256]).astype(bf16)
    wide16 = wide[:16]
    small = jnp.where(wide16, hf[256:272], lf[256:272]).astype(bf16)
    return dict(
        l2=big[0:64, 0:208],
        l2t=big[64:128, 0:192],
        l1=thin[0:64, 0:32],
        lot=thin[64:128, 0:32],
        lo=small[:, 0:208],
    )


def two(x):
    h = x.astype(bf16)
    return h, (x - h.astype(f32)).astype(bf16)


def stack8(x):
    h = x.astype(bf16).astype(f32)
    l = x - h
    return jnp.concatenate([h, l, h, l], axis=0).astype(bf16)


def mm(a, b):
    return jnp.dot(a, b, preferred_element_type=f32)


def nt(a, b):
    return lax.dot_general(a, b, (((1,), (1,)), ((), ())), preferred_element_type=f32)


def load8(ref, n0):
    return jnp.concatenate([ref[pl.ds(n0 + i, 8, stride=64), :] for i in range(CH)], axis=1)


def store8(ref, n0, x):
    for i in range(CH):
        ref[pl.ds(n0 + i, 8, stride=64), :] = x[:, i * 128 : (i + 1) * 128]


def put_fields(ref, x, ones):
    ref[0 : F * 64, :] = x.reshape(F * 64, 128)
    ref[F * 64 : F * 64 + 64, :] = jnp.full((64, 128), 1.0 if ones else 0.0, f32)
    ref[F * 64 + 64 :, :] = jnp.zeros((128, 128), f32)


def bias_rows():
    return jnp.where(iota((16, NW), 0) < 2, 1.0, 0.0).astype(bf16)


def forward(x8, w, ones):
    h1 = jnp.tanh(mm(w["l1"], stack8(x8)))
    h1h, h1l = two(h1)
    h2 = jnp.tanh(mm(w["l2"], jnp.concatenate([h1h, h1l, h1h, ones], axis=0)))
    return h1, h1h, h1l, h2


def closure_body(sa_ref, p_ref, c_ref, h1_ref, h2_ref, x_ref, o_ref):
    put_fields(x_ref, sa_ref[0:F], True)
    w = weights(p_ref)
    ones = bias_rows()

    def chunk(i, carry):
        n0 = i * CH
        h1, _, _, h2 = forward(load8(x_ref, n0), w, ones)
        lanes = pl.ds(pl.multiple_of(i * NW, NW), NW)
        h1_ref[:, lanes] = h1
        h2_ref[:, lanes] = h2
        h2h, h2l = two(h2)
        out = mm(w["lo"], jnp.concatenate([h2h, h2l, h2h, ones], axis=0))
        store8(o_ref, n0, out[0:8])
        return carry

    lax.fori_loop(0, 64 // CH, chunk, 0)
    c_ref[...] = o_ref[0 : F * 64].reshape(F, 64, 128)


def backward(x8, c8, h1, h1h, h1l, h2, h2h, h2l, w, acc):
    gw, gx, gc, gb = acc
    d2 = mm(w["lot"], stack8(c8)) * (1.0 - h2 * h2)
    d2h, d2l = two(d2)
    d1 = mm(w["l2t"], jnp.concatenate([d2h, d2l, d2h], axis=0)) * (1.0 - h1 * h1)
    d1h, d1l = two(d1)
    back = mm(w["lo"][:, 0:192], jnp.concatenate([d1h, d1l, d1h], axis=0))[8:16]
    gw = gw + nt(jnp.concatenate([d2h, d2l], axis=0), jnp.concatenate([h1h, h1l], axis=0))
    xh = x8.astype(bf16).astype(f32)
    ch = c8.astype(bf16).astype(f32)
    xs = jnp.concatenate([xh, x8 - xh], axis=0).astype(bf16)
    cs = jnp.concatenate([ch, c8 - ch], axis=0).astype(bf16)
    gx = gx + nt(xs, jnp.concatenate([d1h, d1l, d2h, d2l], axis=0))
    gc = gc + nt(cs, jnp.concatenate([h2h, h2l], axis=0))
    for i in range(CH):
        gb = gb + c8[:, i * 128 : (i + 1) * 128]
    return back, (gw, gx, gc, gb)


def no_grads():
    return (
        jnp.zeros((128, 128), f32),
        jnp.zeros((16, 256), f32),
        jnp.zeros((16, 128), f32),
        jnp.zeros((8, 128), f32),
    )


def second_body(
    w_ref, yl_ref, yr_ref, mk_ref, im_ref, sa_ref, c0_ref, p_ref, k_ref,
    part_ref, m1_ref, w2_ref, up_ref, dn_ref, gw_ref, gx_ref, gc_ref, gb_ref,
    x_ref, c_ref, o_ref, b_ref,
):
    im = im_ref[...] * STEP
    mass = quad((64, 128)) * mk_ref[0:1]
    v = zfill(yadd(w_ref[...], yl_ref[...], yr_ref[...])) * im[None]
    a2 = sa_ref[F:]
    s1 = sa_ref[0:F] + STEP * c0_ref[...] - v[0:F]
    put_fields(x_ref, s1, True)
    put_fields(c_ref, a2 * mass[None], False)
    w = weights(p_ref)
    ones = bias_rows()

    def chunk(i, acc):
        n0 = i * CH
        x8 = load8(x_ref, n0)
        c8 = load8(c_ref, n0)
        h1, h1h, h1l, h2 = forward(x8, w, ones)
        h2h, h2l = two(h2)
        out = mm(w["lo"], jnp.concatenate([h2h, h2l, h2h, ones], axis=0))
        store8(o_ref, n0, out[0:8])
        back, acc = backward(x8, c8, h1, h1h, h1l, h2, h2h, h2l, w, acc)
        store8(b_ref, n0, back)
        return acc

    acc = lax.fori_loop(0, 64 // CH, chunk, no_grads())
    gw_ref[...], gx_ref[...], gc_ref[...], gb_ref[...] = acc
    back = b_ref[0 : F * 64].reshape(F, 64, 128)
    a1 = a2 - v[F:] + (STEP / mass)[None] * back
    m1_ref[...] = a1 * mass[None]
    part_ref[0:F] = s1 + STEP * o_ref[0 : F * 64].reshape(F, 64, 128)
    part_ref[F:] = a1
    wz = zsum(stiffness(jnp.concatenate([s1, a1], axis=0), k_ref[...], mk_ref[8:9]))
    w2_ref[...] = wz
    up_ref[...], dn_ref[...] = xpack(wz)


def first_body(
    sa_ref, m1_ref, h1_ref, h2_ref, p_ref, gw_ref, gx_ref, gc_ref, gb_ref,
    back_ref, pay_ref, x_ref, c_ref, b_ref,
):
    put_fields(x_ref, sa_ref[0:F], True)
    put_fields(c_ref, m1_ref[...], False)
    w = weights(p_ref)

    def chunk(i, acc):
        n0 = i * CH
        lanes = pl.ds(pl.multiple_of(i * NW, NW), NW)
        h1, h2 = h1_ref[:, lanes], h2_ref[:, lanes]
        h1h, h1l = two(h1)
        h2h, h2l = two(h2)
        back, acc = backward(
            load8(x_ref, n0), load8(c_ref, n0), h1, h1h, h1l, h2, h2h, h2l, w, acc
        )
        store8(b_ref, n0, back)
        return acc

    gw, gx, gc, gb = lax.fori_loop(
        0, 64 // CH, chunk, (gw_ref[...], gx_ref[...], gc_ref[...], gb_ref[...])
    )
    back_ref[...] = b_ref[0 : F * 64].reshape(F, 64, 128)

    def fold(t):
        return t + pltpu.roll(t, 64, 1)

    gw = fold(gw[0:64] + gw[64:128])
    gx1 = fold(gx[0:8, 0:128] + gx[8:16, 0:128])
    gx2 = fold(gx[0:8, 128:256] + gx[8:16, 128:256])
    gc = fold(gc[0:8] + gc[8:16])
    gbs = jnp.broadcast_to(jnp.sum(gb, axis=1, keepdims=True), (8, 128))
    left = iota((32, 128), 1) < 64
    scale = STEP / 256.0
    pay_ref[0:32] = jnp.where(left, gw[0:32], gw[32:64]) * scale
    pay_ref[32:40] = jnp.where(left[:8], gx1, gx2) * scale
    pay_ref[40:48] = jnp.where(left[:8], gc, gbs) * scale


def finish_body(
    w_ref, yl_ref, yr_ref, mk_ref, im_ref, part_ref, back_ref, o_ref, s_ref, a_ref
):
    im = im_ref[...] * STEP
    mass = quad((64, 128)) * mk_ref[0:1]
    v = zfill(yadd(w_ref[...], yl_ref[...], yr_ref[...])) * im[None]
    s2 = part_ref[0:F] - v[0:F]
    a0 = (part_ref[F:] - v[F:]) * mass[None] + STEP * back_ref[...]
    x = jnp.concatenate([s2.reshape(320, 128), a0.reshape(320, 128)], axis=0)
    y = permute_nn(x, one_hot(o_ref[...]))
    for i, ref in enumerate((s_ref, a_ref)):
        for f in range(F):
            for q in range(4):
                r = (i * F + f) * 64 + q * 16
                ref[f, pl.ds(q, 16, stride=4), :] = y[r : r + 16]


def call(body, outs, args, scratch=(), flops=0, trans=0):
    shapes = [jax.ShapeDtypeStruct(s, f32) for s in outs]
    return pl.pallas_call(
        body,
        out_shape=shapes,
        in_specs=[VM] * len(args),
        out_specs=[VM] * len(shapes),
        scratch_shapes=[pltpu.VMEM(s, f32) for s in scratch],
        cost_estimate=pl.CostEstimate(
            flops=flops, bytes_accessed=2000000, transcendentals=trans
        ),
        compiler_params=pltpu.CompilerParams(vmem_limit_bytes=40 * 1024 * 1024),
    )(*args)


def shift(x, axis, step):
    n = lax.axis_size(axis)
    return lax.ppermute(x, axis, [(i, (i + step) % n) for i in range(n)])


def both_ways(up, dn, axis):
    return shift(up, axis, 1), shift(dn, axis, -1)


def partner_maps():
    maps = []
    for dim in range(4):
        group = []
        for k in (1, 2, 3):
            perm = []
            for d in range(256):
                s, c = d // 16, d % 16
                zl, y, core, zh, x = s // 8, (s // 2) % 4, s % 2, c // 4, c % 4
                if dim == 0:
                    v = (core * 2 + zl) ^ k
                    core, zl = v // 2, v % 2
                elif dim == 1:
                    y = (y + k) % 4
                elif dim == 2:
                    x = (x + k) % 4
                else:
                    zh = (zh + k) % 4
                perm.append((d, (zl * 8 + y * 2 + core) * 16 + zh * 4 + x))
            group.append(perm)
        maps.append(group)
    return maps


def all_sum(x):
    if (lax.axis_size("sub"), lax.axis_size("col")) != (16, 16):
        return lax.psum(x, ("sub", "col"))
    for group in partner_maps():
        others = [lax.ppermute(x, ("sub", "col"), perm) for perm in group]
        x = x + others[0] + others[1] + others[2]
    return x


def pack_weights(in_weight, in_bias, mid_weight, mid_bias, out_weight, out_bias):
    def wide(a):
        return jnp.pad(a, ((0, 0), (0, 256 - a.shape[1])))

    w1 = jnp.concatenate([in_weight, in_bias[:, None], jnp.zeros((64, 2), f32)], axis=1)
    wot = jnp.pad(out_weight.T, ((0, 0), (0, 3)))
    wo = jnp.concatenate([out_weight] * 3 + [out_bias[:, None]] * 2, axis=1)
    return jnp.concatenate(
        [
            wide(jnp.concatenate([mid_weight] * 3 + [mid_bias[:, None]] * 2, axis=1)),
            wide(jnp.concatenate([mid_weight.T] * 3, axis=1)),
            wide(jnp.concatenate([w1] * 4, axis=1)),
            wide(jnp.concatenate([wot] * 4, axis=1)),
            jnp.pad(wide(wo), ((0, 3), (0, 0))),
            jnp.pad(wide(jnp.concatenate([in_weight.T] * 3, axis=1)), ((0, 3), (0, 0))),
        ],
        axis=0,
    )


def on_device(
    initial_state,
    state_cotangent,
    element_order,
    element_weight,
    element_diffusivity,
    in_weight,
    in_bias,
    mid_weight,
    mid_bias,
    out_weight,
    out_bias,
):
    kmat = jnp.asarray(stiffness_matrix())
    pw = pack_weights(in_weight, in_bias, mid_weight, mid_bias, out_weight, out_bias)

    def faces(w, up, dn, n):
        rp, rm = both_ways(up, dn, "sub")
        w, y = call(
            lambda *r: xy_body(n, *r), [(n, 3, 2, 8, 128), (n, 2, 8, 128)], [w, rp, rm]
        )
        yl, yr = both_ways(y, y, "col")
        return w, yl, yr

    w, up, dn, mk = call(
        start_body,
        [(12, 48, 128), (18, 8, 128), (18, 8, 128), (16, 128)],
        [
            initial_state,
            state_cotangent,
            element_order,
            element_weight.reshape(1, 128),
            element_diffusivity.reshape(1, 128),
        ],
    )
    w, yl, yr = faces(w, up, dn, 12)
    ten = [(10, 48, 128), (15, 8, 128), (15, 8, 128)]
    sa, im, w, up, dn = call(
        state_body, [(10, 64, 128), (64, 128)] + ten, [w, yl, yr, mk, kmat]
    )
    c0, h1, h2 = call(
        closure_body,
        [(F, 64, 128), (64, 8192), (64, 8192)],
        [sa, pw],
        [(512, 128)] * 2,
        flops=300000000,
        trans=1000000,
    )
    w, yl, yr = faces(w, up, dn, 10)
    part, m1, w, up, dn, gw, gx, gc, gb = call(
        second_body,
        [(10, 64, 128), (F, 64, 128)] + ten + [(128, 128), (16, 256), (16, 128), (8, 128)],
        [w, yl, yr, mk, im, sa, c0, pw, kmat],
        [(512, 128)] * 4,
        flops=900000000,
        trans=1000000,
    )
    back, pay = call(
        first_body,
        [(F, 64, 128), (48, 128)],
        [sa, m1, h1, h2, pw, gw, gx, gc, gb],
        [(512, 128)] * 3,
        flops=600000000,
    )
    w, yl, yr = faces(w, up, dn, 10)
    pay = all_sum(pay)
    out_state, out_adj = call(
        finish_body,
        [(F, 64, 128), (F, 64, 128)],
        [w, yl, yr, mk, im, part, back, element_order],
    )
    return (
        out_state,
        out_adj,
        pay[32:37, 0:64].T,
        pay[37, 0:64],
        jnp.concatenate([pay[0:32, 0:64], pay[0:32, 64:128]], axis=0),
        pay[37, 64:128],
        pay[40:45, 0:64],
        pay[40:45, 64],
    )


def solution(mesh):
    split = P(None, None, ("sub", "col"))
    placed = (split, split, P(("sub", "col"), None), P(("sub", "col")), P(("sub", "col")))
    return jax.shard_map(
        on_device,
        mesh=mesh,
        in_specs=placed + (P(),) * 6,
        out_specs=(split, split) + (P(),) * 6,
        check_vma=False,
    )
```

profile of v0, /device:TPU:32, one launch (start us, length us, event | category | flops | bytes accessed | tf_op | source)
XLA Modules:
  0.0 99.2 jit_solution(14733448688547200980)
XLA Ops:
  5.1 3.8 %collective-permute-start.1 = (f32[18,8,128]{2,1,0:T(8,128)S(1)}, f32[18,8,128]{2,1,0:T(8,128)S(1)}, u32[]{:S(2)}, u32[]{:S(2)}) collective-permute-start(f32[18,8,128]{2,1,0:T(8,128)S(1)} %get-tuple-element.41), channel_id=1, source_target_pairs={{0,240},{16,0},{32,16},{48,32},{64,48},{80,64},{96,80},{112,96},{1... | collective-permute-start | bytes 221192 | tf_op jit(solution)/shard_map/ppermute | solution.py:426
  13.6 1.0 concatenate.26
  16.0 7.7 %collective-permute-start.3 = (f32[12,2,8,128]{3,2,1,0:T(8,128)S(1)}, f32[12,2,8,128]{3,2,1,0:T(8,128)S(1)}, u32[]{:S(2)}, u32[]{:S(2)}) collective-permute-start(f32[12,2,8,128]{3,2,1,0:T(8,128)S(1)} %get-tuple-element.43), channel_id=1, source_target_pairs={{0,15},{1,0},{2,1},{3,2},{4,3},{5,4},{6,5},{7,6},{8,7},{9,8},{10,9... | collective-permute-start | bytes 294920 | tf_op jit(solution)/shard_map/ppermute | solution.py:426
  23.7 2.1 %collective-permute-done.3.yr_ref = f32[12,2,8,128]{3,2,1,0:T(8,128)S(1)} collective-permute-done((f32[12,2,8,128]{3,2,1,0:T(8,128)S(1)}, f32[12,2,8,128]{3,2,1,0:T(8,128)S(1)}, u32[]{:S(2)}, u32[]{:S(2)}) %collective-permute-start.3) | collective-permute-done | bytes 98336 | tf_op jit(solution)/shard_map/ppermute | solution.py:426
  25.9 7.7 %collective-permute-done.2.yl_ref = f32[12,2,8,128]{3,2,1,0:T(8,128)S(1)} collective-permute-done((f32[12,2,8,128]{3,2,1,0:T(8,128)S(1)}, f32[12,2,8,128]{3,2,1,0:T(8,128)S(1)}, u32[]{:S(2)}, u32[]{:S(2)}) %collective-permute-start.2) | collective-permute-done | bytes 98336 | tf_op jit(solution)/shard_map/ppermute | solution.py:426
  34.0 3.8 %collective-permute-start.5 = (f32[15,8,128]{2,1,0:T(8,128)S(1)}, f32[15,8,128]{2,1,0:T(8,128)S(1)}, u32[]{:S(2)}, u32[]{:S(2)}) collective-permute-start(f32[15,8,128]{2,1,0:T(8,128)S(1)} %get-tuple-element.47), channel_id=1, source_target_pairs={{0,240},{16,0},{32,16},{48,32},{64,48},{80,64},{96,80},{112,96},{1... | collective-permute-start | bytes 184328 | tf_op jit(solution)/shard_map/ppermute | solution.py:426
  37.8 1.9 %collective-permute-done.4.r_1_ = f32[15,8,128]{2,1,0:T(8,128)S(1)} collective-permute-done((f32[15,8,128]{2,1,0:T(8,128)S(1)}, f32[15,8,128]{2,1,0:T(8,128)S(1)}, u32[]{:S(2)}, u32[]{:S(2)}) %collective-permute-start.4) | collective-permute-done | bytes 61472 | tf_op jit(solution)/shard_map/ppermute | solution.py:426
  40.4 2.0 %collective-permute-start.6 = (f32[10,2,8,128]{3,2,1,0:T(8,128)S(1)}, f32[10,2,8,128]{3,2,1,0:T(8,128)S(1)}, u32[]{:S(2)}, u32[]{:S(2)}) collective-permute-start(f32[10,2,8,128]{3,2,1,0:T(8,128)S(1)} %get-tuple-element.49), channel_id=1, source_target_pairs={{0,1},{1,2},{2,3},{3,4},{4,5},{5,6},{6,7},{7,8},{8,9},{9,10},{10,1... | collective-permute-start | bytes 245768 | tf_op jit(solution)/shard_map/ppermute | solution.py:426
  42.4 2.4 %shard_map.183 = (f32[5,64,128]{2,1,0:T(8,128)S(1)}, f32[64,8192]{1,0:T(8,128)S(1)}, f32[64,8192]{1,0:T(8,128)S(1)}) custom-call(f32[10,64,128]{2,1,0:T(8,128)S(1)} %get-tuple-element.51.sa_ref, f32[272,256]{1,0:T(8,128)S(1)} %constant_dynamic-update-slice_fusion.p_ref), custom_call_target="tpu_custom_call" | custom-call | flops 300000000 | bytes 2000000 | tf_op jit(solution)/shard_map/pallas_call | solution.py:411
  44.8 5.2 %collective-permute-done.6.yl_ref = f32[10,2,8,128]{3,2,1,0:T(8,128)S(1)} collective-permute-done((f32[10,2,8,128]{3,2,1,0:T(8,128)S(1)}, f32[10,2,8,128]{3,2,1,0:T(8,128)S(1)}, u32[]{:S(2)}, u32[]{:S(2)}) %collective-permute-start.6) | collective-permute-done | bytes 81952 | tf_op jit(solution)/shard_map/ppermute | solution.py:426
  50.0 6.9 %shard_map.184 = (f32[10,64,128]{2,1,0:T(8,128)S(1)}, f32[5,64,128]{2,1,0:T(8,128)S(1)}, f32[10,48,128]{2,1,0:T(8,128)S(1)}, f32[15,8,128]{2,1,0:T(8,128)S(1)}, ...) custom-call(f32[10,3,2,8,128]{4,3,2,1,0:T(8,128)S(1)} %get-tuple-ele, ...), custom_call_target="tpu_custom_call" | custom-call | flops 900000000 | bytes 2000000 | tf_op jit(solution)/shard_map/pallas_call | solution.py:411
  56.9 4.8 %shard_map.186 = (f32[5,64,128]{2,1,0:T(8,128)S(1)}, f32[48,128]{1,0:T(8,128)S(1)}) custom-call(f32[10,64,128]{2,1,0:T(8,128)S(1)} %get-tuple-element.51.sa_ref, f32[5,64,128]{2,1,0:T(8,128)S(1)} %get-tuple-element.59.m1_ref, f32[64,8192]{1,0:T(8,128)S(1)} %get-tuple-element.60.h1_ref, f32[64,8192]{1,0:T(8,128)S(1)} %get-tuple-element.61.h2_ref, ...), custom_call_target="tpu_custom_call" | custom-call | flops 600000000 | bytes 2000000 | tf_op jit(solution)/shard_map/pallas_call | solution.py:411
  61.9 2.0 %collective-permute-start.12 = (f32[48,128]{1,0:T(8,128)S(1)}, f32[48,128]{1,0:T(8,128)S(1)}, u32[]{:S(2)}, u32[]{:S(2)}) collective-permute-start(f32[48,128]{1,0:T(8,128)S(1)} %get-tuple-element.69), channel_id=1, source_target_pairs={{0,128},{1,129},{2,130},{3,131},{4,132},{5,133},{6,134},{7,135},{8... | collective-permute-start | bytes 73736 | tf_op jit(solution)/shard_map/ppermute | solution.py:461
  64.0 1.1 %collective-permute-done.14 = f32[48,128]{1,0:T(8,128)S(1)} collective-permute-done((f32[48,128]{1,0:T(8,128)S(1)}, f32[48,128]{1,0:T(8,128)S(1)}, u32[]{:S(2)}, u32[]{:S(2)}) %collective-permute-start.14) | collective-permute-done | bytes 24608 | tf_op jit(solution)/shard_map/ppermute | solution.py:461
  66.0 2.3 %collective-permute-start.17 = (f32[48,128]{1,0:T(8,128)S(1)}, f32[48,128]{1,0:T(8,128)S(1)}, u32[]{:S(2)}, u32[]{:S(2)}) collective-permute-start(f32[48,128]{1,0:T(8,128)S(1)} %add_add_fusion.3), channel_id=1, source_target_pairs={{0,96},{1,97},{2,98},{3,99},{4,100},{5,101},{6,102},{7,103},{8,104... | collective-permute-start | bytes 73736 | tf_op jit(solution)/shard_map/ppermute | solution.py:461
  68.3 1.0 collective-permute-start.15
  70.0 3.7 %collective-permute-done.16 = f32[48,128]{1,0:T(8,128)S(1)} collective-permute-done((f32[48,128]{1,0:T(8,128)S(1)}, f32[48,128]{1,0:T(8,128)S(1)}, u32[]{:S(2)}, u32[]{:S(2)}) %collective-permute-start.16) | collective-permute-done | bytes 24608 | tf_op jit(solution)/shard_map/ppermute | solution.py:461
  73.9 1.9 %collective-permute-start.18 = (f32[48,128]{1,0:T(8,128)S(1)}, f32[48,128]{1,0:T(8,128)S(1)}, u32[]{:S(2)}, u32[]{:S(2)}) collective-permute-start(f32[48,128]{1,0:T(8,128)S(1)} %add_add_fusion.2), channel_id=1, source_target_pairs={{0,1},{1,2},{2,3},{3,0},{4,5},{5,6},{6,7},{7,4},{8,9},{9,10},{10,1... | collective-permute-start | bytes 73736 | tf_op jit(solution)/shard_map/ppermute | solution.py:461
  75.8 3.9 %collective-permute-start.9 = (f32[15,8,128]{2,1,0:T(8,128)S(1)}, f32[15,8,128]{2,1,0:T(8,128)S(1)}, u32[]{:S(2)}, u32[]{:S(2)}) collective-permute-start(f32[15,8,128]{2,1,0:T(8,128)S(1)} %get-tuple-element.55), channel_id=1, source_target_pairs={{0,240},{16,0},{32,16},{48,32},{64,48},{80,64},{96,80},{112,96},{1... | collective-permute-start | bytes 184328 | tf_op jit(solution)/shard_map/ppermute | solution.py:426
  80.6 1.9 %collective-permute-start.22 = (f32[48,128]{1,0:T(8,128)S(1)}, f32[48,128]{1,0:T(8,128)S(1)}, u32[]{:S(2)}, u32[]{:S(2)}) collective-permute-start(f32[48,128]{1,0:T(8,128)S(1)} %add_add_fusion.1), channel_id=1, source_target_pairs={{0,8},{1,9},{2,10},{3,11},{4,12},{5,13},{6,14},{7,15},{8,0},{9,1},... | collective-permute-start | bytes 73736 | tf_op jit(solution)/shard_map/ppermute | solution.py:461
  82.5 2.6 %collective-permute-start.21 = (f32[48,128]{1,0:T(8,128)S(1)}, f32[48,128]{1,0:T(8,128)S(1)}, u32[]{:S(2)}, u32[]{:S(2)}) collective-permute-start(f32[48,128]{1,0:T(8,128)S(1)} %add_add_fusion.1), channel_id=1, source_target_pairs={{0,4},{1,5},{2,6},{3,7},{4,8},{5,9},{6,10},{7,11},{8,12},{9,13},{1... | collective-permute-start | bytes 73736 | tf_op jit(solution)/shard_map/ppermute | solution.py:461
  85.3 3.2 %collective-permute-start.11 = (f32[10,2,8,128]{3,2,1,0:T(8,128)S(1)}, f32[10,2,8,128]{3,2,1,0:T(8,128)S(1)}, u32[]{:S(2)}, u32[]{:S(2)}) collective-permute-start(f32[10,2,8,128]{3,2,1,0:T(8,128)S(1)} %get-tuple-element.57), channel_id=1, source_target_pairs={{0,15},{1,0},{2,1},{3,2},{4,3},{5,4},{6,5},{7,6},{8,7},{9,8},{10,9... | collective-permute-start | bytes 245768 | tf_op jit(solution)/shard_map/ppermute | solution.py:426
  91.2 6.9 %collective-permute-done.10.yl_ref = f32[10,2,8,128]{3,2,1,0:T(8,128)S(1)} collective-permute-done((f32[10,2,8,128]{3,2,1,0:T(8,128)S(1)}, f32[10,2,8,128]{3,2,1,0:T(8,128)S(1)}, u32[]{:S(2)}, u32[]{:S(2)}) %collective-permute-start.10) | collective-permute-done | bytes 81952 | tf_op jit(solution)/shard_map/ppermute | solution.py:426
  98.1 1.1 %shard_map.187 = (f32[5,64,128]{2,1,0:T(8,128)}, f32[5,64,128]{2,1,0:T(8,128)}) custom-call(f32[10,3,2,8,128]{4,3,2,1,0:T(8,128)S(1)} %get-tuple-element.56.w_ref, f32[10,2,8,128]{3,2,1,0:T(8,128)S(1)} %collective-permute-done.10.yl_ref, f32[10,2,8,128]{3,2,1,0:T(8,128)S(1)} %collective-permute-done.11.yr_ref, f32[16,128]{1,0:T(8,128)S(1)} %get-tuple-element.44.mk_ref, ...), custom_call_target="tpu_custom_call" | custom-call | bytes 2000000 | tf_op jit(solution)/shard_map/pallas_call | solution.py:411
  (76 shorter events, 17.4 us)
Async XLA Ops:
  5.0 10.8 %collective-permute-start = (f32[18,8,128]{2,1,0:T(8,128)S(1)}, f32[18,8,128]{2,1,0:T(8,128)S(1)}, u32[]{:S(2)}, u32[]{:S(2)}) collective-permute-start(f32[18,8,128]{2,1,0:T(8,128)S(1)} %get-tuple-element.40), channel_id=1, source_target_pairs={{0,16},{16,32},{32,48},{48,64},{64,80},{80,96},{96,112},{112,128},... | collective-permute-start | bytes 221192 | tf_op jit(solution)/shard_map/ppermute | solution.py:426
  5.1 10.7 %collective-permute-start.1 = (f32[18,8,128]{2,1,0:T(8,128)S(1)}, f32[18,8,128]{2,1,0:T(8,128)S(1)}, u32[]{:S(2)}, u32[]{:S(2)}) collective-permute-start(f32[18,8,128]{2,1,0:T(8,128)S(1)} %get-tuple-element.41), channel_id=1, source_target_pairs={{0,240},{16,0},{32,16},{48,32},{64,48},{80,64},{96,80},{112,96},{1... | collective-permute-start | bytes 221192 | tf_op jit(solution)/shard_map/ppermute | solution.py:426
  16.0 9.9 %collective-permute-start.3 = (f32[12,2,8,128]{3,2,1,0:T(8,128)S(1)}, f32[12,2,8,128]{3,2,1,0:T(8,128)S(1)}, u32[]{:S(2)}, u32[]{:S(2)}) collective-permute-start(f32[12,2,8,128]{3,2,1,0:T(8,128)S(1)} %get-tuple-element.43), channel_id=1, source_target_pairs={{0,15},{1,0},{2,1},{3,2},{4,3},{5,4},{6,5},{7,6},{8,7},{9,8},{10,9... | collective-permute-start | bytes 294920 | tf_op jit(solution)/shard_map/ppermute | solution.py:426
  23.6 9.9 %collective-permute-start.2 = (f32[12,2,8,128]{3,2,1,0:T(8,128)S(1)}, f32[12,2,8,128]{3,2,1,0:T(8,128)S(1)}, u32[]{:S(2)}, u32[]{:S(2)}) collective-permute-start(f32[12,2,8,128]{3,2,1,0:T(8,128)S(1)} %get-tuple-element.43), channel_id=1, source_target_pairs={{0,1},{1,2},{2,3},{3,4},{4,5},{5,6},{6,7},{7,8},{8,9},{9,10},{10,1... | collective-permute-start | bytes 294920 | tf_op jit(solution)/shard_map/ppermute | solution.py:426
  33.9 5.8 %collective-permute-start.4 = (f32[15,8,128]{2,1,0:T(8,128)S(1)}, f32[15,8,128]{2,1,0:T(8,128)S(1)}, u32[]{:S(2)}, u32[]{:S(2)}) collective-permute-start(f32[15,8,128]{2,1,0:T(8,128)S(1)} %get-tuple-element.46), channel_id=1, source_target_pairs={{0,16},{16,32},{32,48},{48,64},{64,80},{80,96},{96,112},{112,128},... | collective-permute-start | bytes 184328 | tf_op jit(solution)/shard_map/ppermute | solution.py:426
  34.0 6.2 %collective-permute-start.5 = (f32[15,8,128]{2,1,0:T(8,128)S(1)}, f32[15,8,128]{2,1,0:T(8,128)S(1)}, u32[]{:S(2)}, u32[]{:S(2)}) collective-permute-start(f32[15,8,128]{2,1,0:T(8,128)S(1)} %get-tuple-element.47), channel_id=1, source_target_pairs={{0,240},{16,0},{32,16},{48,32},{64,48},{80,64},{96,80},{112,96},{1... | collective-permute-start | bytes 184328 | tf_op jit(solution)/shard_map/ppermute | solution.py:426
  40.3 4.5 %collective-permute-start.7 = (f32[10,2,8,128]{3,2,1,0:T(8,128)S(1)}, f32[10,2,8,128]{3,2,1,0:T(8,128)S(1)}, u32[]{:S(2)}, u32[]{:S(2)}) collective-permute-start(f32[10,2,8,128]{3,2,1,0:T(8,128)S(1)} %get-tuple-element.49), channel_id=1, source_target_pairs={{0,15},{1,0},{2,1},{3,2},{4,3},{5,4},{6,5},{7,6},{8,7},{9,8},{10,9... | collective-permute-start | bytes 245768 | tf_op jit(solution)/shard_map/ppermute | solution.py:426
  40.4 9.6 %collective-permute-start.6 = (f32[10,2,8,128]{3,2,1,0:T(8,128)S(1)}, f32[10,2,8,128]{3,2,1,0:T(8,128)S(1)}, u32[]{:S(2)}, u32[]{:S(2)}) collective-permute-start(f32[10,2,8,128]{3,2,1,0:T(8,128)S(1)} %get-tuple-element.49), channel_id=1, source_target_pairs={{0,1},{1,2},{2,3},{3,4},{4,5},{5,6},{6,7},{7,8},{8,9},{9,10},{10,1... | collective-permute-start | bytes 245768 | tf_op jit(solution)/shard_map/ppermute | solution.py:426
  61.7 3.3 %collective-permute-start.14 = (f32[48,128]{1,0:T(8,128)S(1)}, f32[48,128]{1,0:T(8,128)S(1)}, u32[]{:S(2)}, u32[]{:S(2)}) collective-permute-start(f32[48,128]{1,0:T(8,128)S(1)} %get-tuple-element.69), channel_id=1, source_target_pairs={{0,144},{1,145},{2,146},{3,147},{4,148},{5,149},{6,150},{7,151},{8... | collective-permute-start | bytes 73736 | tf_op jit(solution)/shard_map/ppermute | solution.py:461
  61.8 3.2 %collective-permute-start.13 = (f32[48,128]{1,0:T(8,128)S(1)}, f32[48,128]{1,0:T(8,128)S(1)}, u32[]{:S(2)}, u32[]{:S(2)}) collective-permute-start(f32[48,128]{1,0:T(8,128)S(1)} %get-tuple-element.69), channel_id=1, source_target_pairs={{0,16},{1,17},{2,18},{3,19},{4,20},{5,21},{6,22},{7,23},{8,24},{9,... | collective-permute-start | bytes 73736 | tf_op jit(solution)/shard_map/ppermute | solution.py:461
  61.9 4.1 %collective-permute-start.12 = (f32[48,128]{1,0:T(8,128)S(1)}, f32[48,128]{1,0:T(8,128)S(1)}, u32[]{:S(2)}, u32[]{:S(2)}) collective-permute-start(f32[48,128]{1,0:T(8,128)S(1)} %get-tuple-element.69), channel_id=1, source_target_pairs={{0,128},{1,129},{2,130},{3,131},{4,132},{5,133},{6,134},{7,135},{8... | collective-permute-start | bytes 73736 | tf_op jit(solution)/shard_map/ppermute | solution.py:461
  66.0 3.9 %collective-permute-start.17 = (f32[48,128]{1,0:T(8,128)S(1)}, f32[48,128]{1,0:T(8,128)S(1)}, u32[]{:S(2)}, u32[]{:S(2)}) collective-permute-start(f32[48,128]{1,0:T(8,128)S(1)} %add_add_fusion.3), channel_id=1, source_target_pairs={{0,96},{1,97},{2,98},{3,99},{4,100},{5,101},{6,102},{7,103},{8,104... | collective-permute-start | bytes 73736 | tf_op jit(solution)/shard_map/ppermute | solution.py:461
  68.3 5.3 %collective-permute-start.16 = (f32[48,128]{1,0:T(8,128)S(1)}, f32[48,128]{1,0:T(8,128)S(1)}, u32[]{:S(2)}, u32[]{:S(2)}) collective-permute-start(f32[48,128]{1,0:T(8,128)S(1)} %add_add_fusion.3), channel_id=1, source_target_pairs={{0,64},{1,65},{2,66},{3,67},{4,68},{5,69},{6,70},{7,71},{8,72},{9,... | collective-permute-start | bytes 73736 | tf_op jit(solution)/shard_map/ppermute | solution.py:461
  68.3 5.3 %collective-permute-start.15 = (f32[48,128]{1,0:T(8,128)S(1)}, f32[48,128]{1,0:T(8,128)S(1)}, u32[]{:S(2)}, u32[]{:S(2)}) collective-permute-start(f32[48,128]{1,0:T(8,128)S(1)} %add_add_fusion.3), channel_id=1, source_target_pairs={{0,32},{1,33},{2,34},{3,35},{4,36},{5,37},{6,38},{7,39},{8,40},{9,... | collective-permute-start | bytes 73736 | tf_op jit(solution)/shard_map/ppermute | solution.py:461
  73.7 6.0 %collective-permute-start.20 = (f32[48,128]{1,0:T(8,128)S(1)}, f32[48,128]{1,0:T(8,128)S(1)}, u32[]{:S(2)}, u32[]{:S(2)}) collective-permute-start(f32[48,128]{1,0:T(8,128)S(1)} %add_add_fusion.2), channel_id=1, source_target_pairs={{0,3},{1,0},{2,1},{3,2},{4,7},{5,4},{6,5},{7,6},{8,11},{9,8},{10,9... | collective-permute-start | bytes 73736 | tf_op jit(solution)/shard_map/ppermute | solution.py:461
  73.8 5.9 %collective-permute-start.19 = (f32[48,128]{1,0:T(8,128)S(1)}, f32[48,128]{1,0:T(8,128)S(1)}, u32[]{:S(2)}, u32[]{:S(2)}) collective-permute-start(f32[48,128]{1,0:T(8,128)S(1)} %add_add_fusion.2), channel_id=1, source_target_pairs={{0,2},{1,3},{2,0},{3,1},{4,6},{5,7},{6,4},{7,5},{8,10},{9,11},{10,... | collective-permute-start | bytes 73736 | tf_op jit(solution)/shard_map/ppermute | solution.py:461
  73.9 6.4 %collective-permute-start.18 = (f32[48,128]{1,0:T(8,128)S(1)}, f32[48,128]{1,0:T(8,128)S(1)}, u32[]{:S(2)}, u32[]{:S(2)}) collective-permute-start(f32[48,128]{1,0:T(8,128)S(1)} %add_add_fusion.2), channel_id=1, source_target_pairs={{0,1},{1,2},{2,3},{3,0},{4,5},{5,6},{6,7},{7,4},{8,9},{9,10},{10,1... | collective-permute-start | bytes 73736 | tf_op jit(solution)/shard_map/ppermute | solution.py:461
  75.8 9.4 %collective-permute-start.8 = (f32[15,8,128]{2,1,0:T(8,128)S(1)}, f32[15,8,128]{2,1,0:T(8,128)S(1)}, u32[]{:S(2)}, u32[]{:S(2)}) collective-permute-start(f32[15,8,128]{2,1,0:T(8,128)S(1)} %get-tuple-element.54), channel_id=1, source_target_pairs={{0,16},{16,32},{32,48},{48,64},{64,80},{80,96},{96,112},{112,128},... | collective-permute-start | bytes 184328 | tf_op jit(solution)/shard_map/ppermute | solution.py:426
  75.8 9.4 %collective-permute-start.9 = (f32[15,8,128]{2,1,0:T(8,128)S(1)}, f32[15,8,128]{2,1,0:T(8,128)S(1)}, u32[]{:S(2)}, u32[]{:S(2)}) collective-permute-start(f32[15,8,128]{2,1,0:T(8,128)S(1)} %get-tuple-element.55), channel_id=1, source_target_pairs={{0,240},{16,0},{32,16},{48,32},{64,48},{80,64},{96,80},{112,96},{1... | collective-permute-start | bytes 184328 | tf_op jit(solution)/shard_map/ppermute | solution.py:426
  80.3 8.3 %collective-permute-start.23 = (f32[48,128]{1,0:T(8,128)S(1)}, f32[48,128]{1,0:T(8,128)S(1)}, u32[]{:S(2)}, u32[]{:S(2)}) collective-permute-start(f32[48,128]{1,0:T(8,128)S(1)} %add_add_fusion.1), channel_id=1, source_target_pairs={{0,12},{1,13},{2,14},{3,15},{4,0},{5,1},{6,2},{7,3},{8,4},{9,5},{1... | collective-permute-start | bytes 73736 | tf_op jit(solution)/shard_map/ppermute | solution.py:461
  80.6 8.0 %collective-permute-start.22 = (f32[48,128]{1,0:T(8,128)S(1)}, f32[48,128]{1,0:T(8,128)S(1)}, u32[]{:S(2)}, u32[]{:S(2)}) collective-permute-start(f32[48,128]{1,0:T(8,128)S(1)} %add_add_fusion.1), channel_id=1, source_target_pairs={{0,8},{1,9},{2,10},{3,11},{4,12},{5,13},{6,14},{7,15},{8,0},{9,1},... | collective-permute-start | bytes 73736 | tf_op jit(solution)/shard_map/ppermute | solution.py:461
  82.5 6.1 %collective-permute-start.21 = (f32[48,128]{1,0:T(8,128)S(1)}, f32[48,128]{1,0:T(8,128)S(1)}, u32[]{:S(2)}, u32[]{:S(2)}) collective-permute-start(f32[48,128]{1,0:T(8,128)S(1)} %add_add_fusion.1), channel_id=1, source_target_pairs={{0,4},{1,5},{2,6},{3,7},{4,8},{5,9},{6,10},{7,11},{8,12},{9,13},{1... | collective-permute-start | bytes 73736 | tf_op jit(solution)/shard_map/ppermute | solution.py:461
  85.3 5.9 %collective-permute-start.11 = (f32[10,2,8,128]{3,2,1,0:T(8,128)S(1)}, f32[10,2,8,128]{3,2,1,0:T(8,128)S(1)}, u32[]{:S(2)}, u32[]{:S(2)}) collective-permute-start(f32[10,2,8,128]{3,2,1,0:T(8,128)S(1)} %get-tuple-element.57), channel_id=1, source_target_pairs={{0,15},{1,0},{2,1},{3,2},{4,3},{5,4},{6,5},{7,6},{8,7},{9,8},{10,9... | collective-permute-start | bytes 245768 | tf_op jit(solution)/shard_map/ppermute | solution.py:426
  88.6 9.5 %collective-permute-start.10 = (f32[10,2,8,128]{3,2,1,0:T(8,128)S(1)}, f32[10,2,8,128]{3,2,1,0:T(8,128)S(1)}, u32[]{:S(2)}, u32[]{:S(2)}) collective-permute-start(f32[10,2,8,128]{3,2,1,0:T(8,128)S(1)} %get-tuple-element.57), channel_id=1, source_target_pairs={{0,1},{1,2},{2,3},{3,4},{4,5},{5,6},{6,7},{7,8},{8,9},{9,10},{10,1... | collective-permute-start | bytes 245768 | tf_op jit(solution)/shard_map/ppermute | solution.py:426
  (8 other events, 93.3 us)
where the time goes:
time: 99.6 us; the launch traced here: 99.2 us
  starting transfers between devices  37.2 us (37%)
  waiting for transfers between devices  31.3 us (31%)
  Pallas kernels  16.5 us (17%)
  local copies, waits for them, and re-layouts  12.4 us (12%)
    ppermute x12, starting transfers between devices, shift(): return lax.ppermute(x, axis, [(i, (i + step) % n) for i in range(n)])  24.7 us
    ppermute x12, waiting for transfers between devices, shift(): return lax.ppermute(x, axis, [(i, (i + step) % n) for i in range(n)])  24.2 us
    pallas_call x9, Pallas kernels, call(): pl.pallas_call(body, out_shape=shapes, in_specs=[VM] * len(args), out_spe...  16.5 us
    ppermute x12, starting transfers between devices, all_sum(): others = [lax.ppermute(x, ('sub', 'col'), perm) for perm in group]  12.5 us
    ppermute x12, waiting for transfers between devices, all_sum(): others = [lax.ppermute(x, ('sub', 'col'), perm) for perm in group]  7.12 us
    unnamed x22, local copies, waits for them, and re-layouts  6.21 us
  transfers between devices with their start and end apart: 24, of which 12 were waited for; matrix products, arithmetic and copies ran while one was open for 10% of the time, Pallas kernels for 3%

commit v1 on v0

--- a/solution.py
+++ b/solution.py
@@ -156,8 +156,19 @@
     return w
 
 
-def start_body(s_ref, c_ref, o_ref, ew_ref, ed_ref, w_ref, up_ref, dn_ref, mk_ref):
+def fetch(srcs, dsts, sems):
+    copies = [pltpu.make_async_copy(a, b, sems.at[i]) for i, (a, b) in enumerate(zip(srcs, dsts))]
+    for c in copies:
+        c.start()
+    for c in copies:
+        c.wait()
+
+
+def start_body(s_in, c_in, o_in, ew_in, ed_in, w_ref, up_ref, dn_ref, mk_ref, g_ref, *scratch):
+    s_ref, c_ref, o_ref, ew_ref, ed_ref, sems = scratch
+    fetch((s_in, c_in, o_in, ew_in, ed_in), scratch[:5], sems)
     g = one_hot(o_ref[...])
+    g_ref[...] = g
     rows = []
     for ref in (s_ref, c_ref):
         for f in range(F):
@@ -197,23 +208,48 @@
     up_ref[...], dn_ref[...] = xpack(w)
 
 
+def prepare_body(w1_in, b1_in, w2_in, b2_in, wo_in, bo_in, p_ref, *scratch):
+    fetch((w1_in, b1_in, w2_in, b2_in, wo_in, bo_in), scratch[:6], scratch[6])
+    w1, b1, w2, b2, wo, bo = (r[...] for r in scratch[:6])
+    z = jnp.zeros((64, 64), f32)
+    pad3 = jnp.zeros((3, 64), f32)
+    w1b = jnp.concatenate([w1, b1, jnp.zeros((2, 64), f32)], axis=0)
+    w1p = jnp.concatenate([w1, pad3], axis=0)
+    wop = jnp.concatenate([wo, pad3], axis=0)
+
+    def columns(parts, rows):
+        if rows < 256:
+            parts = parts + [jnp.zeros((256 - rows, 64), f32)]
+        return jnp.concatenate(parts, axis=0).T
+
+    l2 = columns([w2.T] * 3 + [jnp.broadcast_to(b2, (8, 64))], 200)
+    l2t = columns([w2] * 3, 192)
+    l1 = columns([w1b] * 4, 32)
+    lot = columns([wop] * 4, 32)
+    both = jnp.concatenate([wop, w1p], axis=0)
+    diag = iota((16, 5), 0) == iota((16, 5), 1)
+    bias = jnp.sum(jnp.where(diag, jnp.broadcast_to(bo, (16, 5)), 0.0), axis=1, keepdims=True)
+    bias = jnp.where(iota((16, 64), 1) < 2, jnp.broadcast_to(bias, (16, 64)), z[:16])
+    small = jnp.concatenate([both, both, both, bias], axis=1)
+
+    def parts(p, high):
+        h = p.astype(bf16).astype(f32)
+        return jnp.where(high, h, p - h).astype(bf16)
+
+    col = iota((128, 256), 1)
+    high = (col < 128) | (col == 192)
+    p_ref[0:128] = parts(jnp.concatenate([l2, l2t], axis=0), high)
+    p_ref[128:256] = parts(jnp.concatenate([l1, lot], axis=0), col < 16)
+    p_ref[256:272] = parts(small, high[:16])
+
+
 def weights(p_ref):
-    p = p_ref[...]
-    h = p.astype(bf16)
-    l = (p - h.astype(f32)).astype(bf16)
-    hf, lf = h.astype(f32), l.astype(f32)
-    col = iota((128, 256), 1)
-    wide = (col < 128) | (col == 192)
-    big = jnp.where(wide, hf[0:128], lf[0:128]).astype(bf16)
-    thin = jnp.where(iota((128, 256), 1) < 16, hf[128:256], lf[128:256]).astype(bf16)
-    wide16 = wide[:16]
-    small = jnp.where(wide16, hf[256:272], lf[256:272]).astype(bf16)
     return dict(
-        l2=big[0:64, 0:208],
-        l2t=big[64:128, 0:192],
-        l1=thin[0:64, 0:32],
-        lot=thin[64:128, 0:32],
-        lo=small[:, 0:208],
+        l2=p_ref[0:64, 0:208],
+        l2t=p_ref[64:128, 0:192],
+        l1=p_ref[128:192, 0:32],
+        lot=p_ref[192:256, 0:32],
+        lo=p_ref[256:272, 0:208],
     )
 
 
@@ -390,7 +426,8 @@
 
 
 def finish_body(
-    w_ref, yl_ref, yr_ref, mk_ref, im_ref, part_ref, back_ref, o_ref, s_ref, a_ref
+    w_ref, yl_ref, yr_ref, mk_ref, im_ref, part_ref, back_ref, g_ref, p_ref,
+    s_ref, a_ref, gw1_ref, gb1_ref, gw2_ref, gb2_ref, gwo_ref, gbo_ref,
 ):
     im = im_ref[...] * STEP
     mass = quad((64, 128)) * mk_ref[0:1]
@@ -398,22 +435,37 @@
     s2 = part_ref[0:F] - v[0:F]
     a0 = (part_ref[F:] - v[F:]) * mass[None] + STEP * back_ref[...]
     x = jnp.concatenate([s2.reshape(320, 128), a0.reshape(320, 128)], axis=0)
-    y = permute_nn(x, one_hot(o_ref[...]))
+    y = permute_nn(x, g_ref[...])
     for i, ref in enumerate((s_ref, a_ref)):
         for f in range(F):
             for q in range(4):
                 r = (i * F + f) * 64 + q * 16
                 ref[f, pl.ds(q, 16, stride=4), :] = y[r : r + 16]
-
-
-def call(body, outs, args, scratch=(), flops=0, trans=0):
-    shapes = [jax.ShapeDtypeStruct(s, f32) for s in outs]
+    pay = p_ref[0]
+    for i in range(1, 8):
+        pay = pay + p_ref[i]
+    gw2_ref[0:32] = pay[0:32, 0:64]
+    other = pltpu.roll(pay, 64, 1)
+    gw2_ref[32:64] = other[0:32, 0:64]
+    gw1_ref[...] = pay[32:37, 0:64]
+    gb1_ref[...] = pay[37:38, 0:64]
+    gb2_ref[...] = other[37:38, 0:64]
+    gwo_ref[...] = pay[40:45, 0:64]
+    diag = iota((8, 5), 0) == iota((8, 5), 1)
+    gbo_ref[...] = jnp.sum(jnp.where(diag, other[40:48, 0:5], 0.0), axis=0, keepdims=True)
+
+
+def call(body, outs, args, scratch=(), flops=0, trans=0, space=pltpu.VMEM):
+    if space == pltpu.HBM:
+        args = [pltpu.with_memory_space_constraint(x, pltpu.HBM) for x in args]
+    shapes = [s if hasattr(s, "dtype") else jax.ShapeDtypeStruct(s, f32) for s in outs]
+    scratch = [s if hasattr(s, "memory_space") or hasattr(s, "dtype") else pltpu.VMEM(s, f32) for s in scratch]
     return pl.pallas_call(
         body,
         out_shape=shapes,
-        in_specs=[VM] * len(args),
+        in_specs=[pl.BlockSpec(memory_space=space)] * len(args),
         out_specs=[VM] * len(shapes),
-        scratch_shapes=[pltpu.VMEM(s, f32) for s in scratch],
+        scratch_shapes=scratch,
         cost_estimate=pl.CostEstimate(
             flops=flops, bytes_accessed=2000000, transcendentals=trans
         ),
@@ -430,57 +482,31 @@
     return shift(up, axis, 1), shift(dn, axis, -1)
 
 
-def partner_maps():
-    maps = []
-    for dim in range(4):
-        group = []
-        for k in (1, 2, 3):
-            perm = []
-            for d in range(256):
-                s, c = d // 16, d % 16
-                zl, y, core, zh, x = s // 8, (s // 2) % 4, s % 2, c // 4, c % 4
-                if dim == 0:
-                    v = (core * 2 + zl) ^ k
-                    core, zl = v // 2, v % 2
-                elif dim == 1:
-                    y = (y + k) % 4
-                elif dim == 2:
-                    x = (x + k) % 4
-                else:
-                    zh = (zh + k) % 4
-                perm.append((d, (zl * 8 + y * 2 + core) * 16 + zh * 4 + x))
-            group.append(perm)
-        maps.append(group)
-    return maps
+def place(d):
+    s, c = d // 16, d % 16
+    return s // 8, (s // 2) % 4, s % 2, c // 4, c % 4
+
+
+def together(fixed):
+    groups = {}
+    for d in range(256):
+        groups.setdefault(tuple(place(d)[i] for i in fixed), []).append(d)
+    return [groups[k] for k in sorted(groups)]
+
+
+def send_to_all(x, groups):
+    n = len(groups[0])
+    y = jnp.broadcast_to(x[None], (n,) + x.shape)
+    return lax.all_to_all(y, ("sub", "col"), 0, 0, axis_index_groups=groups, tiled=True)
 
 
 def all_sum(x):
     if (lax.axis_size("sub"), lax.axis_size("col")) != (16, 16):
-        return lax.psum(x, ("sub", "col"))
-    for group in partner_maps():
-        others = [lax.ppermute(x, ("sub", "col"), perm) for perm in group]
-        x = x + others[0] + others[1] + others[2]
-    return x
-
-
-def pack_weights(in_weight, in_bias, mid_weight, mid_bias, out_weight, out_bias):
-    def wide(a):
-        return jnp.pad(a, ((0, 0), (0, 256 - a.shape[1])))
-
-    w1 = jnp.concatenate([in_weight, in_bias[:, None], jnp.zeros((64, 2), f32)], axis=1)
-    wot = jnp.pad(out_weight.T, ((0, 0), (0, 3)))
-    wo = jnp.concatenate([out_weight] * 3 + [out_bias[:, None]] * 2, axis=1)
-    return jnp.concatenate(
-        [
-            wide(jnp.concatenate([mid_weight] * 3 + [mid_bias[:, None]] * 2, axis=1)),
-            wide(jnp.concatenate([mid_weight.T] * 3, axis=1)),
-            wide(jnp.concatenate([w1] * 4, axis=1)),
-            wide(jnp.concatenate([wot] * 4, axis=1)),
-            jnp.pad(wide(wo), ((0, 3), (0, 0))),
-            jnp.pad(wide(jnp.concatenate([in_weight.T] * 3, axis=1)), ((0, 3), (0, 0))),
-        ],
-        axis=0,
-    )
+        x = lax.psum(x, ("sub", "col"))
+        return jnp.concatenate([x[None], jnp.zeros((7,) + x.shape, f32)], axis=0)
+    x = x + lax.ppermute(x, ("sub", "col"), [(d, d ^ 16) for d in range(256)])
+    x = send_to_all(x, together((0, 2, 3))).sum(0)
+    return send_to_all(x, together((1, 2, 4)))
 
 
 def on_device(
@@ -497,19 +523,22 @@
     out_bias,
 ):
     kmat = jnp.asarray(stiffness_matrix())
-    pw = pack_weights(in_weight, in_bias, mid_weight, mid_bias, out_weight, out_bias)
-
-    def faces(w, up, dn, n):
+    hot = jax.ShapeDtypeStruct((128, 128), bf16)
+
+    def in_device(w, up, dn, n):
         rp, rm = both_ways(up, dn, "sub")
-        w, y = call(
+        return call(
             lambda *r: xy_body(n, *r), [(n, 3, 2, 8, 128), (n, 2, 8, 128)], [w, rp, rm]
         )
+
+    def faces(w, up, dn, n):
+        w, y = in_device(w, up, dn, n)
         yl, yr = both_ways(y, y, "col")
         return w, yl, yr
 
-    w, up, dn, mk = call(
+    w, up, dn, mk, g = call(
         start_body,
-        [(12, 48, 128), (18, 8, 128), (18, 8, 128), (16, 128)],
+        [(12, 48, 128), (18, 8, 128), (18, 8, 128), (16, 128), hot],
         [
             initial_state,
             state_cotangent,
@@ -517,6 +546,24 @@
             element_weight.reshape(1, 128),
             element_diffusivity.reshape(1, 128),
         ],
+        [(F, 64, 128), (F, 64, 128), pltpu.VMEM((1, 128), jnp.int32), (1, 128), (1, 128)]
+        + [pltpu.SemaphoreType.DMA((5,))],
+        space=pltpu.HBM,
+    )
+    (pw,) = call(
+        prepare_body,
+        [jax.ShapeDtypeStruct((272, 256), bf16)],
+        [
+            in_weight.T,
+            in_bias.reshape(1, 64),
+            mid_weight,
+            mid_bias.reshape(1, 64),
+            out_weight,
+            out_bias.reshape(1, 5),
+        ],
+        [(5, 64), (1, 64), (64, 64), (1, 64), (5, 64), (1, 5), pltpu.SemaphoreType.DMA((6,))],
+        flops=2000000,
+        space=pltpu.HBM,
     )
     w, yl, yr = faces(w, up, dn, 12)
     ten = [(10, 48, 128), (15, 8, 128), (15, 8, 128)]
@@ -547,22 +594,24 @@
         [(512, 128)] * 3,
         flops=600000000,
     )
-    w, yl, yr = faces(w, up, dn, 10)
-    pay = all_sum(pay)
-    out_state, out_adj = call(
+    w, y = in_device(w, up, dn, 10)
+    pay, y = lax.optimization_barrier((pay, y))
+    yl, yr = both_ways(y, y, "col")
+    terms = all_sum(pay)
+    out_state, out_adj, gw1, gb1, gw2, gb2, gwo, gbo = call(
         finish_body,
-        [(F, 64, 128), (F, 64, 128)],
-        [w, yl, yr, mk, im, part, back, element_order],
+        [(F, 64, 128), (F, 64, 128), (5, 64), (1, 64), (64, 64), (1, 64), (5, 64), (1, 5)],
+        [w, yl, yr, mk, im, part, back, g, terms],
     )
     return (
         out_state,
         out_adj,
-        pay[32:37, 0:64].T,
-        pay[37, 0:64],
-        jnp.concatenate([pay[0:32, 0:64], pay[0:32, 64:128]], axis=0),
-        pay[37, 64:128],
-        pay[40:45, 0:64],
-        pay[40:45, 64],
+        gw1.T,
+        gb1.reshape(64),
+        gw2,
+        gb2.reshape(64),
+        gwo,
+        gbo.reshape(5),
     )
 
 

time: 99.6 us -> 91.9 us (0.923)
  the two profiles are of different devices: /device:TPU:32 before, /device:TPU:1 now
where the time goes in v1:
time: 91.9 us; the launch traced here: 91 us
  starting transfers between devices  29.9 us (33%)
  waiting for transfers between devices  28.1 us (31%)
  Pallas kernels  18.6 us (20%)
  blocking collectives  12.2 us (13%)
  local copies, waits for them, and re-layouts  1.47 us (2%)
    ppermute x12, waiting for transfers between devices, shift(): return lax.ppermute(x, axis, [(i, (i + step) % n) for i in range(n)])  27.3 us
    ppermute x12, starting transfers between devices, shift(): return lax.ppermute(x, axis, [(i, (i + step) % n) for i in range(n)])  22.6 us
    pallas_call x10, Pallas kernels, call(): pl.pallas_call(body, out_shape=shapes, in_specs=[pl.BlockSpec(memory_spac...  18.6 us
    all_to_all x1, blocking collectives, send_to_all(): lax.all_to_all(y, ('sub', 'col'), 0, 0, axis_index_groups=groups, tiled=T...  12.2 us
    ppermute x1, starting transfers between devices, all_sum(): x = x + lax.ppermute(x, ('sub', 'col'), [(d, d ^ 16) for d in range(256)])  3.85 us
    all_to_all x1, starting transfers between devices, send_to_all(): lax.all_to_all(y, ('sub', 'col'), 0, 0, axis_index_groups=groups, tiled=T...  3.39 us
  transfers between devices with their start and end apart: 14, of which 10 were waited for; matrix products, arithmetic and copies ran while one was open for 0% of the time, Pallas kernels for 9%

profile of v1, /device:TPU:1, one launch (start us, length us, event | category | flops | bytes accessed | tf_op | source)
XLA Modules:
  0.0 91.0 jit_solution(6205563182862189689)
XLA Ops:
  0.6 1.6 %shard_map.179 = (f32[12,48,128]{2,1,0:T(8,128)S(1)}, f32[18,8,128]{2,1,0:T(8,128)S(1)}, f32[18,8,128]{2,1,0:T(8,128)S(1)}, f32[16,128]{1,0:T(8,128)S(1)}, bf16[128,128]{1,0:T(8,128)(2,1)S(1)}) custom-call(f32[5,64,128]{2,1,0:T(8,128)} %s_in.1, f32[5,64,128]{2,1,0:T(8,128)} %c_in.1, s32[1,128]{1,0:T(1,128)} %o_in.1, f32[1,128]{1,0:T(1,128)} %bitcast.11, ...), custom_call_target="tpu_custom_call" | custom-call | bytes 2000000 | tf_op jit(solution)/shard_map/pallas_call | solution.py:463
  2.2 2.8 %collective-permute-start = (f32[18,8,128]{2,1,0:T(8,128)S(1)}, f32[18,8,128]{2,1,0:T(8,128)S(1)}, u32[]{:S(2)}, u32[]{:S(2)}) collective-permute-start(f32[18,8,128]{2,1,0:T(8,128)S(1)} %get-tuple-element.49), channel_id=1, source_target_pairs={{0,16},{16,32},{32,48},{48,64},{64,80},{80,96},{96,112},{112,128},... | collective-permute-start | bytes 221192 | tf_op jit(solution)/shard_map/ppermute | solution.py:478
  6.4 2.4 %collective-permute-done.1.r_2_ = f32[18,8,128]{2,1,0:T(8,128)S(1)} collective-permute-done((f32[18,8,128]{2,1,0:T(8,128)S(1)}, f32[18,8,128]{2,1,0:T(8,128)S(1)}, u32[]{:S(2)}, u32[]{:S(2)}) %collective-permute-start.1) | collective-permute-done | bytes 73760 | tf_op jit(solution)/shard_map/ppermute | solution.py:478
  8.9 8.6 %collective-permute-start.3 = (f32[12,2,8,128]{3,2,1,0:T(8,128)S(1)}, f32[12,2,8,128]{3,2,1,0:T(8,128)S(1)}, u32[]{:S(2)}, u32[]{:S(2)}) collective-permute-start(f32[12,2,8,128]{3,2,1,0:T(8,128)S(1)} %get-tuple-element.52), channel_id=1, source_target_pairs={{0,15},{1,0},{2,1},{3,2},{4,3},{5,4},{6,5},{7,6},{8,7},{9,8},{10,9... | collective-permute-start | bytes 294920 | tf_op jit(solution)/shard_map/ppermute | solution.py:478
  17.5 4.0 %collective-permute-done.3.yr_ref = f32[12,2,8,128]{3,2,1,0:T(8,128)S(1)} collective-permute-done((f32[12,2,8,128]{3,2,1,0:T(8,128)S(1)}, f32[12,2,8,128]{3,2,1,0:T(8,128)S(1)}, u32[]{:S(2)}, u32[]{:S(2)}) %collective-permute-start.3) | collective-permute-done | bytes 98336 | tf_op jit(solution)/shard_map/ppermute | solution.py:478
  21.5 5.7 %collective-permute-done.2.yl_ref = f32[12,2,8,128]{3,2,1,0:T(8,128)S(1)} collective-permute-done((f32[12,2,8,128]{3,2,1,0:T(8,128)S(1)}, f32[12,2,8,128]{3,2,1,0:T(8,128)S(1)}, u32[]{:S(2)}, u32[]{:S(2)}) %collective-permute-start.2) | collective-permute-done | bytes 98336 | tf_op jit(solution)/shard_map/ppermute | solution.py:478
  28.3 1.6 %collective-permute-start.4 = (f32[15,8,128]{2,1,0:T(8,128)S(1)}, f32[15,8,128]{2,1,0:T(8,128)S(1)}, u32[]{:S(2)}, u32[]{:S(2)}) collective-permute-start(f32[15,8,128]{2,1,0:T(8,128)S(1)} %get-tuple-element.55), channel_id=1, source_target_pairs={{0,16},{16,32},{32,48},{48,64},{64,80},{80,96},{96,112},{112,128},... | collective-permute-start | bytes 184328 | tf_op jit(solution)/shard_map/ppermute | solution.py:478
  29.9 1.3 %collective-permute-done.4.r_1_ = f32[15,8,128]{2,1,0:T(8,128)S(1)} collective-permute-done((f32[15,8,128]{2,1,0:T(8,128)S(1)}, f32[15,8,128]{2,1,0:T(8,128)S(1)}, u32[]{:S(2)}, u32[]{:S(2)}) %collective-permute-start.4) | collective-permute-done | bytes 61472 | tf_op jit(solution)/shard_map/ppermute | solution.py:478
  31.2 2.4 %collective-permute-done.5.r_2_ = f32[15,8,128]{2,1,0:T(8,128)S(1)} collective-permute-done((f32[15,8,128]{2,1,0:T(8,128)S(1)}, f32[15,8,128]{2,1,0:T(8,128)S(1)}, u32[]{:S(2)}, u32[]{:S(2)}) %collective-permute-start.5) | collective-permute-done | bytes 61472 | tf_op jit(solution)/shard_map/ppermute | solution.py:478
  33.8 1.5 %collective-permute-start.6 = (f32[10,2,8,128]{3,2,1,0:T(8,128)S(1)}, f32[10,2,8,128]{3,2,1,0:T(8,128)S(1)}, u32[]{:S(2)}, u32[]{:S(2)}) collective-permute-start(f32[10,2,8,128]{3,2,1,0:T(8,128)S(1)} %get-tuple-element.58), channel_id=1, source_target_pairs={{0,1},{1,2},{2,3},{3,4},{4,5},{5,6},{6,7},{7,8},{8,9},{9,10},{10,1... | collective-permute-start | bytes 245768 | tf_op jit(solution)/shard_map/ppermute | solution.py:478
  35.2 1.1 %shard_map.183.p_ref = bf16[272,256]{1,0:T(8,128)(2,1)S(1)} custom-call(f32[5,64]{1,0:T(8,128)} %bitcast.10, f32[1,64]{1,0:T(1,128)} %bitcast.13, f32[64,64]{1,0:T(8,128)} %w2_in.1, f32[1,64]{1,0:T(1,128)} %bitcast.14, f32[5,64]{1,0:T(8,128)} %wo_in.1, f32[1,5]{1,0:T(1,128)} %bitcast.15), custom_call_target="tpu_custom_call" | custom-call | flops 2000000 | bytes 2000000 | tf_op jit(solution)/shard_map/pallas_call | solution.py:463
  36.3 2.4 %shard_map.184 = (f32[5,64,128]{2,1,0:T(8,128)S(1)}, f32[64,8192]{1,0:T(8,128)S(1)}, f32[64,8192]{1,0:T(8,128)S(1)}) custom-call(f32[10,64,128]{2,1,0:T(8,128)S(1)} %get-tuple-element.60.sa_ref, bf16[272,256]{1,0:T(8,128)(2,1)S(1)} %shard_map.183.p_ref), custom_call_target="tpu_custom_call" | custom-call | flops 300000000 | bytes 2000000 | tf_op jit(solution)/shard_map/pallas_call | solution.py:463
  38.7 2.6 %collective-permute-done.6.yl_ref = f32[10,2,8,128]{3,2,1,0:T(8,128)S(1)} collective-permute-done((f32[10,2,8,128]{3,2,1,0:T(8,128)S(1)}, f32[10,2,8,128]{3,2,1,0:T(8,128)S(1)}, u32[]{:S(2)}, u32[]{:S(2)}) %collective-permute-start.6) | collective-permute-done | bytes 81952 | tf_op jit(solution)/shard_map/ppermute | solution.py:478
  41.4 6.9 %shard_map.185 = (f32[10,64,128]{2,1,0:T(8,128)S(1)}, f32[5,64,128]{2,1,0:T(8,128)S(1)}, f32[10,48,128]{2,1,0:T(8,128)S(1)}, f32[15,8,128]{2,1,0:T(8,128)S(1)}, ...) custom-call(f32[10,3,2,8,128]{4,3,2,1,0:T(8,128)S(1)} %get-tuple-ele, ...), custom_call_target="tpu_custom_call" | custom-call | flops 900000000 | bytes 2000000 | tf_op jit(solution)/shard_map/pallas_call | solution.py:463
  48.3 1.7 %collective-permute-start.8 = (f32[15,8,128]{2,1,0:T(8,128)S(1)}, f32[15,8,128]{2,1,0:T(8,128)S(1)}, u32[]{:S(2)}, u32[]{:S(2)}) collective-permute-start(f32[15,8,128]{2,1,0:T(8,128)S(1)} %get-tuple-element.63), channel_id=1, source_target_pairs={{0,16},{16,32},{32,48},{48,64},{64,80},{80,96},{96,112},{112,128},... | collective-permute-start | bytes 184328 | tf_op jit(solution)/shard_map/ppermute | solution.py:478
  50.0 2.3 %collective-permute-start.9 = (f32[15,8,128]{2,1,0:T(8,128)S(1)}, f32[15,8,128]{2,1,0:T(8,128)S(1)}, u32[]{:S(2)}, u32[]{:S(2)}) collective-permute-start(f32[15,8,128]{2,1,0:T(8,128)S(1)} %get-tuple-element.64), channel_id=1, source_target_pairs={{0,240},{16,0},{32,16},{48,32},{64,48},{80,64},{96,80},{112,96},{1... | collective-permute-start | bytes 184328 | tf_op jit(solution)/shard_map/ppermute | solution.py:478
  52.3 4.8 %shard_map.187 = (f32[5,64,128]{2,1,0:T(8,128)S(1)}, f32[48,128]{1,0:T(8,128)S(1)}) custom-call(f32[10,64,128]{2,1,0:T(8,128)S(1)} %get-tuple-element.60.sa_ref, f32[5,64,128]{2,1,0:T(8,128)S(1)} %get-tuple-element.66.m1_ref, f32[64,8192]{1,0:T(8,128)S(1)} %get-tuple-element.67.h1_ref, f32[64,8192]{1,0:T(8,128)S(1)} %get-tuple-element.68.h2_ref, ...), custom_call_target="tpu_custom_call" | custom-call | flops 600000000 | bytes 2000000 | tf_op jit(solution)/shard_map/pallas_call | solution.py:463
  57.3 3.9 %collective-permute-start.12 = (f32[48,128]{1,0:T(8,128)S(1)}, f32[48,128]{1,0:T(8,128)S(1)}, u32[]{:S(2)}, u32[]{:S(2)}) collective-permute-start(f32[48,128]{1,0:T(8,128)S(1)} %get-tuple-element.79), channel_id=1, source_target_pairs={{0,16},{1,17},{2,18},{3,19},{4,20},{5,21},{6,22},{7,23},{8,24},{9,... | collective-permute-start | bytes 73736 | tf_op jit(solution)/shard_map/ppermute | solution.py:507
  62.0 12.2 %all_to_all.10 = f32[16,48,128]{2,1,0:T(8,128)S(1)} all-to-all(f32[16,48,128]{2,1,0:T(8,128)S(1)} %broadcast_in_dim.4), channel_id=1, replica_groups={{0,1,2,3,32,33,34,35,64,65,66,67,96,97,98,99},{4,5,6,7,36,37,38,39,68,6..., dimensions={0} | all-to-all | bytes 786432 | tf_op jit(solution)/shard_map/all_to_all | solution.py:500
  74.9 3.4 %all-to-all-start.1 = ((f32[8,48,128]{2,1,0:T(8,128)}), f32[8,48,128]{2,1,0:T(8,128)S(1)}, u32[]{:S(2)}, u32[]{:S(2)}) async-start(f32[8,48,128]{2,1,0:T(8,128)} %broadcast_in_dim.5), calls=%async_computation.1 | async-start | bytes 393216 | tf_op jit(solution)/shard_map/all_to_all | solution.py:500
  78.3 3.4 %collective-permute-start.11 = (f32[10,2,8,128]{3,2,1,0:T(8,128)S(1)}, f32[10,2,8,128]{3,2,1,0:T(8,128)S(1)}, u32[]{:S(2)}, u32[]{:S(2)}) collective-permute-start(f32[10,2,8,128]{3,2,1,0:T(8,128)S(1)} %get-tuple-element.75), channel_id=1, source_target_pairs={{0,15},{1,0},{2,1},{3,2},{4,3},{5,4},{6,5},{7,6},{8,7},{9,8},{10,9... | collective-permute-start | bytes 245768 | tf_op jit(solution)/shard_map/ppermute | solution.py:478
  81.7 2.8 %collective-permute-done.11.yr_ref = f32[10,2,8,128]{3,2,1,0:T(8,128)S(1)} collective-permute-done((f32[10,2,8,128]{3,2,1,0:T(8,128)S(1)}, f32[10,2,8,128]{3,2,1,0:T(8,128)S(1)}, u32[]{:S(2)}, u32[]{:S(2)}) %collective-permute-start.11) | collective-permute-done | bytes 81952 | tf_op jit(solution)/shard_map/ppermute | solution.py:478
  84.5 5.4 %collective-permute-done.10.yl_ref = f32[10,2,8,128]{3,2,1,0:T(8,128)S(1)} collective-permute-done((f32[10,2,8,128]{3,2,1,0:T(8,128)S(1)}, f32[10,2,8,128]{3,2,1,0:T(8,128)S(1)}, u32[]{:S(2)}, u32[]{:S(2)}) %collective-permute-start.10) | collective-permute-done | bytes 81952 | tf_op jit(solution)/shard_map/ppermute | solution.py:478
  89.9 1.1 %shard_map.188 = (f32[5,64,128]{2,1,0:T(8,128)}, f32[5,64,128]{2,1,0:T(8,128)}, f32[5,64]{1,0:T(8,128)}, f32[1,64]{1,0:T(1,128)}, f32[64,64]{1,0:T(8,128)}, /*in...) custom-call(f32[10,3,2,8,128]{4,3,2,1,0:T(8,128)S(1)} %get-tuple-element.65.w_ref, ...), custom_call_target="tpu_custom_call" | custom-call | bytes 2000000 | tf_op jit(solution)/shard_map/pallas_call | solution.py:463
  (21 shorter events, 4.7 us)
Async XLA Ops:
  2.2 4.2 %collective-permute-start = (f32[18,8,128]{2,1,0:T(8,128)S(1)}, f32[18,8,128]{2,1,0:T(8,128)S(1)}, u32[]{:S(2)}, u32[]{:S(2)}) collective-permute-start(f32[18,8,128]{2,1,0:T(8,128)S(1)} %get-tuple-element.49), channel_id=1, source_target_pairs={{0,16},{16,32},{32,48},{48,64},{64,80},{80,96},{96,112},{112,128},... | collective-permute-start | bytes 221192 | tf_op jit(solution)/shard_map/ppermute | solution.py:478
  5.0 3.8 %collective-permute-start.1 = (f32[18,8,128]{2,1,0:T(8,128)S(1)}, f32[18,8,128]{2,1,0:T(8,128)S(1)}, u32[]{:S(2)}, u32[]{:S(2)}) collective-permute-start(f32[18,8,128]{2,1,0:T(8,128)S(1)} %get-tuple-element.50), channel_id=1, source_target_pairs={{0,240},{16,0},{32,16},{48,32},{64,48},{80,64},{96,80},{112,96},{1... | collective-permute-start | bytes 221192 | tf_op jit(solution)/shard_map/ppermute | solution.py:478
  8.9 12.6 %collective-permute-start.3 = (f32[12,2,8,128]{3,2,1,0:T(8,128)S(1)}, f32[12,2,8,128]{3,2,1,0:T(8,128)S(1)}, u32[]{:S(2)}, u32[]{:S(2)}) collective-permute-start(f32[12,2,8,128]{3,2,1,0:T(8,128)S(1)} %get-tuple-element.52), channel_id=1, source_target_pairs={{0,15},{1,0},{2,1},{3,2},{4,3},{5,4},{6,5},{7,6},{8,7},{9,8},{10,9... | collective-permute-start | bytes 294920 | tf_op jit(solution)/shard_map/ppermute | solution.py:478
  17.5 9.7 %collective-permute-start.2 = (f32[12,2,8,128]{3,2,1,0:T(8,128)S(1)}, f32[12,2,8,128]{3,2,1,0:T(8,128)S(1)}, u32[]{:S(2)}, u32[]{:S(2)}) collective-permute-start(f32[12,2,8,128]{3,2,1,0:T(8,128)S(1)} %get-tuple-element.52), channel_id=1, source_target_pairs={{0,1},{1,2},{2,3},{3,4},{4,5},{5,6},{6,7},{7,8},{8,9},{9,10},{10,1... | collective-permute-start | bytes 294920 | tf_op jit(solution)/shard_map/ppermute | solution.py:478
  27.2 0.8 copy-start
  28.3 2.9 %collective-permute-start.4 = (f32[15,8,128]{2,1,0:T(8,128)S(1)}, f32[15,8,128]{2,1,0:T(8,128)S(1)}, u32[]{:S(2)}, u32[]{:S(2)}) collective-permute-start(f32[15,8,128]{2,1,0:T(8,128)S(1)} %get-tuple-element.55), channel_id=1, source_target_pairs={{0,16},{16,32},{32,48},{48,64},{64,80},{80,96},{96,112},{112,128},... | collective-permute-start | bytes 184328 | tf_op jit(solution)/shard_map/ppermute | solution.py:478
  29.9 3.6 %collective-permute-start.5 = (f32[15,8,128]{2,1,0:T(8,128)S(1)}, f32[15,8,128]{2,1,0:T(8,128)S(1)}, u32[]{:S(2)}, u32[]{:S(2)}) collective-permute-start(f32[15,8,128]{2,1,0:T(8,128)S(1)} %get-tuple-element.56), channel_id=1, source_target_pairs={{0,240},{16,0},{32,16},{48,32},{64,48},{80,64},{96,80},{112,96},{1... | collective-permute-start | bytes 184328 | tf_op jit(solution)/shard_map/ppermute | solution.py:478
  33.7 5.0 %collective-permute-start.7 = (f32[10,2,8,128]{3,2,1,0:T(8,128)S(1)}, f32[10,2,8,128]{3,2,1,0:T(8,128)S(1)}, u32[]{:S(2)}, u32[]{:S(2)}) collective-permute-start(f32[10,2,8,128]{3,2,1,0:T(8,128)S(1)} %get-tuple-element.58), channel_id=1, source_target_pairs={{0,15},{1,0},{2,1},{3,2},{4,3},{5,4},{6,5},{7,6},{8,7},{9,8},{10,9... | collective-permute-start | bytes 245768 | tf_op jit(solution)/shard_map/ppermute | solution.py:478
  33.8 7.6 %collective-permute-start.6 = (f32[10,2,8,128]{3,2,1,0:T(8,128)S(1)}, f32[10,2,8,128]{3,2,1,0:T(8,128)S(1)}, u32[]{:S(2)}, u32[]{:S(2)}) collective-permute-start(f32[10,2,8,128]{3,2,1,0:T(8,128)S(1)} %get-tuple-element.58), channel_id=1, source_target_pairs={{0,1},{1,2},{2,3},{3,4},{4,5},{5,6},{6,7},{7,8},{8,9},{9,10},{10,1... | collective-permute-start | bytes 245768 | tf_op jit(solution)/shard_map/ppermute | solution.py:478
  48.3 8.8 %collective-permute-start.8 = (f32[15,8,128]{2,1,0:T(8,128)S(1)}, f32[15,8,128]{2,1,0:T(8,128)S(1)}, u32[]{:S(2)}, u32[]{:S(2)}) collective-permute-start(f32[15,8,128]{2,1,0:T(8,128)S(1)} %get-tuple-element.63), channel_id=1, source_target_pairs={{0,16},{16,32},{32,48},{48,64},{64,80},{80,96},{96,112},{112,128},... | collective-permute-start | bytes 184328 | tf_op jit(solution)/shard_map/ppermute | solution.py:478
  50.0 7.1 %collective-permute-start.9 = (f32[15,8,128]{2,1,0:T(8,128)S(1)}, f32[15,8,128]{2,1,0:T(8,128)S(1)}, u32[]{:S(2)}, u32[]{:S(2)}) collective-permute-start(f32[15,8,128]{2,1,0:T(8,128)S(1)} %get-tuple-element.64), channel_id=1, source_target_pairs={{0,240},{16,0},{32,16},{48,32},{64,48},{80,64},{96,80},{112,96},{1... | collective-permute-start | bytes 184328 | tf_op jit(solution)/shard_map/ppermute | solution.py:478
  57.3 4.7 %collective-permute-start.12 = (f32[48,128]{1,0:T(8,128)S(1)}, f32[48,128]{1,0:T(8,128)S(1)}, u32[]{:S(2)}, u32[]{:S(2)}) collective-permute-start(f32[48,128]{1,0:T(8,128)S(1)} %get-tuple-element.79), channel_id=1, source_target_pairs={{0,16},{1,17},{2,18},{3,19},{4,20},{5,21},{6,22},{7,23},{8,24},{9,... | collective-permute-start | bytes 73736 | tf_op jit(solution)/shard_map/ppermute | solution.py:507
  74.9 15.0 %all-to-all-start.1 = ((f32[8,48,128]{2,1,0:T(8,128)}), f32[8,48,128]{2,1,0:T(8,128)S(1)}, u32[]{:S(2)}, u32[]{:S(2)}) async-start(f32[8,48,128]{2,1,0:T(8,128)} %broadcast_in_dim.5), calls=%async_computation.1 | async-start | bytes 393216 | tf_op jit(solution)/shard_map/all_to_all | solution.py:500
  78.3 6.2 %collective-permute-start.11 = (f32[10,2,8,128]{3,2,1,0:T(8,128)S(1)}, f32[10,2,8,128]{3,2,1,0:T(8,128)S(1)}, u32[]{:S(2)}, u32[]{:S(2)}) collective-permute-start(f32[10,2,8,128]{3,2,1,0:T(8,128)S(1)} %get-tuple-element.75), channel_id=1, source_target_pairs={{0,15},{1,0},{2,1},{3,2},{4,3},{5,4},{6,5},{7,6},{8,7},{9,8},{10,9... | collective-permute-start | bytes 245768 | tf_op jit(solution)/shard_map/ppermute | solution.py:478
  81.7 8.2 %collective-permute-start.10 = (f32[10,2,8,128]{3,2,1,0:T(8,128)S(1)}, f32[10,2,8,128]{3,2,1,0:T(8,128)S(1)}, u32[]{:S(2)}, u32[]{:S(2)}) collective-permute-start(f32[10,2,8,128]{3,2,1,0:T(8,128)S(1)} %get-tuple-element.75), channel_id=1, source_target_pairs={{0,1},{1,2},{2,3},{3,4},{4,5},{5,6},{6,7},{7,8},{8,9},{9,10},{10,1... | collective-permute-start | bytes 245768 | tf_op jit(solution)/shard_map/ppermute | solution.py:478

commit v2 on v1

--- a/solution.py
+++ b/solution.py
@@ -10,7 +10,7 @@
 
 F = 5
 STEP = 0.05
-CH = 16
+CH = 32
 NW = CH * 128
 f32, bf16 = jnp.float32, jnp.bfloat16
 VM = pl.BlockSpec(memory_space=pltpu.VMEM)
@@ -30,10 +30,7 @@
     s = d.T @ np.diag(w) @ d
     m = np.diag(w)
     k = np.kron(m, np.kron(s, m)) + np.kron(m, np.kron(m, s)) + np.kron(s, np.kron(m, m))
-    k = k.astype(np.float32)
-    hi = k.astype(bf16).astype(np.float32)
-    lo = k - hi
-    return np.concatenate([hi, hi, lo], axis=1).astype(bf16)
+    return k.astype(np.float32)
 
 
 def iota(shape, dim):
@@ -164,9 +161,13 @@
         c.wait()
 
 
-def start_body(s_in, c_in, o_in, ew_in, ed_in, w_ref, up_ref, dn_ref, mk_ref, g_ref, *scratch):
-    s_ref, c_ref, o_ref, ew_ref, ed_ref, sems = scratch
-    fetch((s_in, c_in, o_in, ew_in, ed_in), scratch[:5], sems)
+def start_body(
+    s_in, c_in, o_in, ew_in, ed_in, k_in, w_ref, up_ref, dn_ref, mk_ref, g_ref, k_ref, *scratch
+):
+    s_ref, c_ref, o_ref, ew_ref, ed_ref, kf_ref, sems = scratch
+    fetch((s_in, c_in, o_in, ew_in, ed_in, k_in), scratch[:6], sems)
+    kh, kl = two(kf_ref[...])
+    k_ref[...] = jnp.concatenate([kh, kh, kl], axis=1)
     g = one_hot(o_ref[...])
     g_ref[...] = g
     rows = []
@@ -295,21 +296,30 @@
     h1 = jnp.tanh(mm(w["l1"], stack8(x8)))
     h1h, h1l = two(h1)
     h2 = jnp.tanh(mm(w["l2"], jnp.concatenate([h1h, h1l, h1h, ones], axis=0)))
-    return h1, h1h, h1l, h2
-
-
-def closure_body(sa_ref, p_ref, c_ref, h1_ref, h2_ref, x_ref, o_ref):
+    h2h, h2l = two(h2)
+    return h1, h1h, h1l, h2, h2h, h2l
+
+
+def lanes_of(i):
+    return pl.ds(pl.multiple_of(i * NW, NW), NW)
+
+
+def put4(ref, i, parts):
+    for k, p in enumerate(parts):
+        ref[k * 64 : k * 64 + 64, lanes_of(i)] = p
+
+
+def closure_body(sa_ref, p_ref, c_ref, x_ref, hh_ref, t_ref, o_ref):
     put_fields(x_ref, sa_ref[0:F], True)
     w = weights(p_ref)
     ones = bias_rows()
 
     def chunk(i, carry):
         n0 = i * CH
-        h1, _, _, h2 = forward(load8(x_ref, n0), w, ones)
-        lanes = pl.ds(pl.multiple_of(i * NW, NW), NW)
-        h1_ref[:, lanes] = h1
-        h2_ref[:, lanes] = h2
-        h2h, h2l = two(h2)
+        h1, h1h, h1l, h2, h2h, h2l = forward(load8(x_ref, n0), w, ones)
+        put4(hh_ref, i, (h1h, h1l, h2h, h2l))
+        t_ref[0:64, lanes_of(i)] = 1.0 - h1 * h1
+        t_ref[64:128, lanes_of(i)] = 1.0 - h2 * h2
         out = mm(w["lo"], jnp.concatenate([h2h, h2l, h2h, ones], axis=0))
         store8(o_ref, n0, out[0:8])
         return carry
@@ -318,38 +328,35 @@
     c_ref[...] = o_ref[0 : F * 64].reshape(F, 64, 128)
 
 
-def backward(x8, c8, h1, h1h, h1l, h2, h2h, h2l, w, acc):
-    gw, gx, gc, gb = acc
-    d2 = mm(w["lot"], stack8(c8)) * (1.0 - h2 * h2)
-    d2h, d2l = two(d2)
-    d1 = mm(w["l2t"], jnp.concatenate([d2h, d2l, d2h], axis=0)) * (1.0 - h1 * h1)
-    d1h, d1l = two(d1)
+def backward(c8, t1, t2, w):
+    d2h, d2l = two(mm(w["lot"], stack8(c8)) * t2)
+    d1h, d1l = two(mm(w["l2t"], jnp.concatenate([d2h, d2l, d2h], axis=0)) * t1)
     back = mm(w["lo"][:, 0:192], jnp.concatenate([d1h, d1l, d1h], axis=0))[8:16]
-    gw = gw + nt(jnp.concatenate([d2h, d2l], axis=0), jnp.concatenate([h1h, h1l], axis=0))
-    xh = x8.astype(bf16).astype(f32)
-    ch = c8.astype(bf16).astype(f32)
-    xs = jnp.concatenate([xh, x8 - xh], axis=0).astype(bf16)
-    cs = jnp.concatenate([ch, c8 - ch], axis=0).astype(bf16)
-    gx = gx + nt(xs, jnp.concatenate([d1h, d1l, d2h, d2l], axis=0))
-    gc = gc + nt(cs, jnp.concatenate([h2h, h2l], axis=0))
+    return back, d2h, d2l, d1h, d1l
+
+
+def stack2(x):
+    h = x.astype(bf16).astype(f32)
+    return jnp.concatenate([h, x - h], axis=0).astype(bf16)
+
+
+def add_grads(acc, x8, c8, h1, h2, d2, d1):
+    gw, gb = acc
+    right = jnp.concatenate([h1, stack2(x8), stack2(c8)], axis=0)
+    gw = gw + nt(jnp.concatenate([d2, d1, h2], axis=0), right)
     for i in range(CH):
         gb = gb + c8[:, i * 128 : (i + 1) * 128]
-    return back, (gw, gx, gc, gb)
+    return gw, gb
 
 
 def no_grads():
-    return (
-        jnp.zeros((128, 128), f32),
-        jnp.zeros((16, 256), f32),
-        jnp.zeros((16, 128), f32),
-        jnp.zeros((8, 128), f32),
-    )
+    return jnp.zeros((384, 160), f32), jnp.zeros((8, 128), f32)
 
 
 def second_body(
     w_ref, yl_ref, yr_ref, mk_ref, im_ref, sa_ref, c0_ref, p_ref, k_ref,
-    part_ref, m1_ref, w2_ref, up_ref, dn_ref, gw_ref, gx_ref, gc_ref, gb_ref,
-    x_ref, c_ref, o_ref, b_ref,
+    part_ref, m1_ref, w2_ref, up_ref, dn_ref, x_ref, c_ref, hh_ref, dd_ref,
+    o_ref, b_ref,
 ):
     im = im_ref[...] * STEP
     mass = quad((64, 128)) * mk_ref[0:1]
@@ -361,20 +368,18 @@
     w = weights(p_ref)
     ones = bias_rows()
 
-    def chunk(i, acc):
+    def chunk(i, carry):
         n0 = i * CH
-        x8 = load8(x_ref, n0)
-        c8 = load8(c_ref, n0)
-        h1, h1h, h1l, h2 = forward(x8, w, ones)
-        h2h, h2l = two(h2)
+        h1, h1h, h1l, h2, h2h, h2l = forward(load8(x_ref, n0), w, ones)
+        put4(hh_ref, i, (h1h, h1l, h2h, h2l))
         out = mm(w["lo"], jnp.concatenate([h2h, h2l, h2h, ones], axis=0))
         store8(o_ref, n0, out[0:8])
-        back, acc = backward(x8, c8, h1, h1h, h1l, h2, h2h, h2l, w, acc)
+        back, *ds = backward(load8(c_ref, n0), 1.0 - h1 * h1, 1.0 - h2 * h2, w)
+        put4(dd_ref, i, ds)
         store8(b_ref, n0, back)
-        return acc
-
-    acc = lax.fori_loop(0, 64 // CH, chunk, no_grads())
-    gw_ref[...], gx_ref[...], gc_ref[...], gb_ref[...] = acc
+        return carry
+
+    lax.fori_loop(0, 64 // CH, chunk, 0)
     back = b_ref[0 : F * 64].reshape(F, 64, 128)
     a1 = a2 - v[F:] + (STEP / mass)[None] * back
     m1_ref[...] = a1 * mass[None]
@@ -385,38 +390,46 @@
     up_ref[...], dn_ref[...] = xpack(wz)
 
 
+def grads_body(x_ref, c_ref, hh_ref, dd_ref, gw_ref, gb_ref):
+    def chunk(i, acc):
+        n0 = i * CH
+        at = lanes_of(i)
+        return add_grads(
+            acc, load8(x_ref, n0), load8(c_ref, n0),
+            hh_ref[0:128, at], hh_ref[128:256, at], dd_ref[0:128, at], dd_ref[128:256, at],
+        )
+
+    gw_ref[...], gb_ref[...] = lax.fori_loop(0, 64 // CH, chunk, no_grads())
+
+
 def first_body(
-    sa_ref, m1_ref, h1_ref, h2_ref, p_ref, gw_ref, gx_ref, gc_ref, gb_ref,
-    back_ref, pay_ref, x_ref, c_ref, b_ref,
+    x_ref, m1_ref, hh_ref, t_ref, p_ref, gw_ref, gb_ref, back_ref, pay_ref, c_ref, b_ref
 ):
-    put_fields(x_ref, sa_ref[0:F], True)
     put_fields(c_ref, m1_ref[...], False)
     w = weights(p_ref)
 
     def chunk(i, acc):
         n0 = i * CH
-        lanes = pl.ds(pl.multiple_of(i * NW, NW), NW)
-        h1, h2 = h1_ref[:, lanes], h2_ref[:, lanes]
-        h1h, h1l = two(h1)
-        h2h, h2l = two(h2)
-        back, acc = backward(
-            load8(x_ref, n0), load8(c_ref, n0), h1, h1h, h1l, h2, h2h, h2l, w, acc
+        at = lanes_of(i)
+        c8 = load8(c_ref, n0)
+        back, d2h, d2l, d1h, d1l = backward(c8, t_ref[0:64, at], t_ref[64:128, at], w)
+        store8(b_ref, n0, back)
+        return add_grads(
+            acc, load8(x_ref, n0), c8, hh_ref[0:128, at], hh_ref[128:256, at],
+            jnp.concatenate([d2h, d2l], axis=0), jnp.concatenate([d1h, d1l], axis=0),
         )
-        store8(b_ref, n0, back)
-        return acc
-
-    gw, gx, gc, gb = lax.fori_loop(
-        0, 64 // CH, chunk, (gw_ref[...], gx_ref[...], gc_ref[...], gb_ref[...])
-    )
+
+    g, gb = lax.fori_loop(0, 64 // CH, chunk, (gw_ref[...], gb_ref[...]))
     back_ref[...] = b_ref[0 : F * 64].reshape(F, 64, 128)
 
     def fold(t):
         return t + pltpu.roll(t, 64, 1)
 
-    gw = fold(gw[0:64] + gw[64:128])
-    gx1 = fold(gx[0:8, 0:128] + gx[8:16, 0:128])
-    gx2 = fold(gx[0:8, 128:256] + gx[8:16, 128:256])
-    gc = fold(gc[0:8] + gc[8:16])
+    gw = fold(g[0:64, 0:128] + g[64:128, 0:128])
+    gs = g[:, 128:160].T
+    gx2 = fold(gs[0:8, 0:128] + gs[8:16, 0:128])
+    gx1 = fold(gs[0:8, 128:256] + gs[8:16, 128:256])
+    gc = fold(gs[16:24, 256:384] + gs[24:32, 256:384])
     gbs = jnp.broadcast_to(jnp.sum(gb, axis=1, keepdims=True), (8, 128))
     left = iota((32, 128), 1) < 64
     scale = STEP / 256.0
@@ -426,8 +439,7 @@
 
 
 def finish_body(
-    w_ref, yl_ref, yr_ref, mk_ref, im_ref, part_ref, back_ref, g_ref, p_ref,
-    s_ref, a_ref, gw1_ref, gb1_ref, gw2_ref, gb2_ref, gwo_ref, gbo_ref,
+    w_ref, yl_ref, yr_ref, mk_ref, im_ref, part_ref, back_ref, g_ref, s_ref, a_ref
 ):
     im = im_ref[...] * STEP
     mass = quad((64, 128)) * mk_ref[0:1]
@@ -441,6 +453,9 @@
             for q in range(4):
                 r = (i * F + f) * 64 + q * 16
                 ref[f, pl.ds(q, 16, stride=4), :] = y[r : r + 16]
+
+
+def output_body(p_ref, gw1_ref, gb1_ref, gw2_ref, gb2_ref, gwo_ref, gbo_ref):
     pay = p_ref[0]
     for i in range(1, 8):
         pay = pay + p_ref[i]
@@ -522,8 +537,9 @@
     out_weight,
     out_bias,
 ):
-    kmat = jnp.asarray(stiffness_matrix())
     hot = jax.ShapeDtypeStruct((128, 128), bf16)
+    wide = jax.ShapeDtypeStruct((256, 8192), bf16)
+    khot = jax.ShapeDtypeStruct((64, 192), bf16)
 
     def in_device(w, up, dn, n):
         rp, rm = both_ways(up, dn, "sub")
@@ -536,18 +552,20 @@
         yl, yr = both_ways(y, y, "col")
         return w, yl, yr
 
-    w, up, dn, mk, g = call(
+    w, up, dn, mk, g, kmat = call(
         start_body,
-        [(12, 48, 128), (18, 8, 128), (18, 8, 128), (16, 128), hot],
+        [(12, 48, 128), (18, 8, 128), (18, 8, 128), (16, 128), hot, khot],
         [
             initial_state,
             state_cotangent,
             element_order,
             element_weight.reshape(1, 128),
             element_diffusivity.reshape(1, 128),
+            jnp.asarray(stiffness_matrix()),
         ],
         [(F, 64, 128), (F, 64, 128), pltpu.VMEM((1, 128), jnp.int32), (1, 128), (1, 128)]
-        + [pltpu.SemaphoreType.DMA((5,))],
+        + [(64, 64)]
+        + [pltpu.SemaphoreType.DMA((6,))],
         space=pltpu.HBM,
     )
     (pw,) = call(
@@ -566,42 +584,54 @@
         space=pltpu.HBM,
     )
     w, yl, yr = faces(w, up, dn, 12)
+    pw, yl, yr = lax.optimization_barrier((pw, yl, yr))
     ten = [(10, 48, 128), (15, 8, 128), (15, 8, 128)]
     sa, im, w, up, dn = call(
         state_body, [(10, 64, 128), (64, 128)] + ten, [w, yl, yr, mk, kmat]
     )
-    c0, h1, h2 = call(
+    c0, x0, hh0, t0 = call(
         closure_body,
-        [(F, 64, 128), (64, 8192), (64, 8192)],
+        [(F, 64, 128), (512, 128), wide, (128, 8192)],
         [sa, pw],
-        [(512, 128)] * 2,
+        [(512, 128)],
         flops=300000000,
         trans=1000000,
     )
     w, yl, yr = faces(w, up, dn, 10)
-    part, m1, w, up, dn, gw, gx, gc, gb = call(
+    part, m1, w, up, dn, x1, c1, hh1, dd1 = call(
         second_body,
-        [(10, 64, 128), (F, 64, 128)] + ten + [(128, 128), (16, 256), (16, 128), (8, 128)],
+        [(10, 64, 128), (F, 64, 128)] + ten + [(512, 128), (512, 128), wide, wide],
         [w, yl, yr, mk, im, sa, c0, pw, kmat],
-        [(512, 128)] * 4,
+        [(512, 128)] * 2,
         flops=900000000,
         trans=1000000,
     )
+    acc = call(
+        grads_body,
+        [(384, 160), (8, 128)],
+        [x1, c1, hh1, dd1],
+        flops=300000000,
+    )
+    w, y = in_device(w, up, dn, 10)
+    acc, y = lax.optimization_barrier((acc, y))
+    yl, yr = both_ways(y, y, "col")
     back, pay = call(
         first_body,
         [(F, 64, 128), (48, 128)],
-        [sa, m1, h1, h2, pw, gw, gx, gc, gb],
-        [(512, 128)] * 3,
+        [x0, m1, hh0, t0, pw, *acc],
+        [(512, 128)] * 2,
         flops=600000000,
     )
-    w, y = in_device(w, up, dn, 10)
-    pay, y = lax.optimization_barrier((pay, y))
-    yl, yr = both_ways(y, y, "col")
+    pay, yl, yr = lax.optimization_barrier((pay, yl, yr))
     terms = all_sum(pay)
-    out_state, out_adj, gw1, gb1, gw2, gb2, gwo, gbo = call(
+    out_state, out_adj = call(
         finish_body,
-        [(F, 64, 128), (F, 64, 128), (5, 64), (1, 64), (64, 64), (1, 64), (5, 64), (1, 5)],
-        [w, yl, yr, mk, im, part, back, g, terms],
+        [(F, 64, 128), (F, 64, 128)],
+        [w, yl, yr, mk, im, part, back, g],
+        flops=20000000,
+    )
+    gw1, gb1, gw2, gb2, gwo, gbo = call(
+        output_body, [(5, 64), (1, 64), (64, 64), (1, 64), (5, 64), (1, 5)], [terms]
     )
     return (
         out_state,

time: 91.9 us -> 91.5 us (level)
  Pallas kernels: 18.6 us -> 17 us
  waiting for transfers between devices: 28.1 us -> 29.7 us
    all_to_all x1, waiting for transfers between devices: 0.01 us -> 6.33 us  [send_to_all(): lax.all_to_all(y, ('sub', 'col'), 0, 0, axis_index_groups=groups, tiled=T...]
    ppermute x12, waiting for transfers between devices: 27.3 us -> 22.5 us  [shift(): return lax.ppermute(x, axis, [(i, (i + step) % n) for i in range(n)])]
    ppermute x12, starting transfers between devices: 22.6 us -> 20.9 us  [shift(): return lax.ppermute(x, axis, [(i, (i + step) % n) for i in range(n)])]
    pallas_call x10 -> x12, Pallas kernels: 18.6 us -> 17 us  [call(): pl.pallas_call(body, out_shape=shapes, in_specs=[pl.BlockSpec(memory_spac...]
    ppermute x1, starting transfers between devices: 3.85 us -> 5 us  [all_sum(): x = x + lax.ppermute(x, ('sub', 'col'), [(d, d ^ 16) for d in range(256)])]
  transfers between devices with their start and end apart: 14 -> 14, of which waited for: 10 -> 10; matrix products, arithmetic and copies ran while one was open for 0% -> 0% of each run, Pallas kernels for 9% -> 11%
where the time goes in v2:
time: 91.5 us; the launch traced here: 90.1 us
  waiting for transfers between devices  29.7 us (32%)
  starting transfers between devices  29.3 us (32%)
  Pallas kernels  17 us (19%)
  blocking collectives  12.6 us (14%)
    ppermute x12, waiting for transfers between devices, shift(): return lax.ppermute(x, axis, [(i, (i + step) % n) for i in range(n)])  22.5 us
    ppermute x12, starting transfers between devices, shift(): return lax.ppermute(x, axis, [(i, (i + step) % n) for i in range(n)])  20.9 us
    pallas_call x12, Pallas kernels, call(): pl.pallas_call(body, out_shape=shapes, in_specs=[pl.BlockSpec(memory_spac...  17 us
    all_to_all x1, blocking collectives, send_to_all(): lax.all_to_all(y, ('sub', 'col'), 0, 0, axis_index_groups=groups, tiled=T...  12.6 us
    all_to_all x1, waiting for transfers between devices, send_to_all(): lax.all_to_all(y, ('sub', 'col'), 0, 0, axis_index_groups=groups, tiled=T...  6.33 us
    ppermute x1, starting transfers between devices, all_sum(): x = x + lax.ppermute(x, ('sub', 'col'), [(d, d ^ 16) for d in range(256)])  5 us
    all_to_all x1, starting transfers between devices, send_to_all(): lax.all_to_all(y, ('sub', 'col'), 0, 0, axis_index_groups=groups, tiled=T...  3.39 us
  transfers between devices with their start and end apart: 14, of which 10 were waited for; matrix products, arithmetic and copies ran while one was open for 0% of the time, Pallas kernels for 11%

profile of v2, /device:TPU:1, one launch (start us, length us, event | category | flops | bytes accessed | tf_op | source)
XLA Modules:
  0.0 90.1 jit_solution(13486074231657540858)
XLA Ops:
  0.6 1.6 %shard_map.179 = (f32[12,48,128]{2,1,0:T(8,128)S(1)}, f32[18,8,128]{2,1,0:T(8,128)S(1)}, f32[18,8,128]{2,1,0:T(8,128)S(1)}, f32[16,128]{1,0:T(8,128)S(1)}, bf16[...) custom-call(f32[5,64,128]{2,1,0:T(8,128)} %s_in.1, f32[5,64,128]{2,1,0:T(8,128)} %c_in.1, s32[1,128]{1,0:T(1,128)} %o_in.1, ...), custom_call_target="tpu_custom_call" | custom-call | bytes 2000000 | tf_op jit(solution)/shard_map/pallas_call | solution.py:478
  2.2 2.8 %collective-permute-start = (f32[18,8,128]{2,1,0:T(8,128)S(1)}, f32[18,8,128]{2,1,0:T(8,128)S(1)}, u32[]{:S(2)}, u32[]{:S(2)}) collective-permute-start(f32[18,8,128]{2,1,0:T(8,128)S(1)} %get-tuple-element.60), channel_id=1, source_target_pairs={{0,16},{16,32},{32,48},{48,64},{64,80},{80,96},{96,112},{112,128},... | collective-permute-start | bytes 221192 | tf_op jit(solution)/shard_map/ppermute | solution.py:493
  6.4 2.4 %collective-permute-done.1.r_2_ = f32[18,8,128]{2,1,0:T(8,128)S(1)} collective-permute-done((f32[18,8,128]{2,1,0:T(8,128)S(1)}, f32[18,8,128]{2,1,0:T(8,128)S(1)}, u32[]{:S(2)}, u32[]{:S(2)}) %collective-permute-start.1) | collective-permute-done | bytes 73760 | tf_op jit(solution)/shard_map/ppermute | solution.py:493
  8.9 8.6 %collective-permute-start.3 = (f32[12,2,8,128]{3,2,1,0:T(8,128)S(1)}, f32[12,2,8,128]{3,2,1,0:T(8,128)S(1)}, u32[]{:S(2)}, u32[]{:S(2)}) collective-permute-start(f32[12,2,8,128]{3,2,1,0:T(8,128)S(1)} %get-tuple-element.63), channel_id=1, source_target_pairs={{0,15},{1,0},{2,1},{3,2},{4,3},{5,4},{6,5},{7,6},{8,7},{9,8},{10,9... | collective-permute-start | bytes 294920 | tf_op jit(solution)/shard_map/ppermute | solution.py:493
  17.5 1.1 %shard_map.181.p_ref = bf16[272,256]{1,0:T(8,128)(2,1)S(1)} custom-call(f32[5,64]{1,0:T(8,128)} %bitcast.10, f32[1,64]{1,0:T(1,128)} %bitcast.13, f32[64,64]{1,0:T(8,128)} %w2_in.1, f32[1,64]{1,0:T(1,128)} %bitcast.14, f32[5,64]{1,0:T(8,128)} %wo_in.1, f32[1,5]{1,0:T(1,128)} %bitcast.15), custom_call_target="tpu_custom_call" | custom-call | flops 2000000 | bytes 2000000 | tf_op jit(solution)/shard_map/pallas_call | solution.py:478
  18.6 2.9 %collective-permute-done.3.yr_ref = f32[12,2,8,128]{3,2,1,0:T(8,128)S(1)} collective-permute-done((f32[12,2,8,128]{3,2,1,0:T(8,128)S(1)}, f32[12,2,8,128]{3,2,1,0:T(8,128)S(1)}, u32[]{:S(2)}, u32[]{:S(2)}) %collective-permute-start.3) | collective-permute-done | bytes 98336 | tf_op jit(solution)/shard_map/ppermute | solution.py:493
  21.5 5.7 %collective-permute-done.2.yl_ref = f32[12,2,8,128]{3,2,1,0:T(8,128)S(1)} collective-permute-done((f32[12,2,8,128]{3,2,1,0:T(8,128)S(1)}, f32[12,2,8,128]{3,2,1,0:T(8,128)S(1)}, u32[]{:S(2)}, u32[]{:S(2)}) %collective-permute-start.2) | collective-permute-done | bytes 98336 | tf_op jit(solution)/shard_map/ppermute | solution.py:493
  27.6 1.6 %collective-permute-start.4 = (f32[15,8,128]{2,1,0:T(8,128)S(1)}, f32[15,8,128]{2,1,0:T(8,128)S(1)}, u32[]{:S(2)}, u32[]{:S(2)}) collective-permute-start(f32[15,8,128]{2,1,0:T(8,128)S(1)} %get-tuple-element.69), channel_id=1, source_target_pairs={{0,16},{16,32},{32,48},{48,64},{64,80},{80,96},{96,112},{112,128},... | collective-permute-start | bytes 184328 | tf_op jit(solution)/shard_map/ppermute | solution.py:493
  29.2 1.3 %collective-permute-done.4.r_1_ = f32[15,8,128]{2,1,0:T(8,128)S(1)} collective-permute-done((f32[15,8,128]{2,1,0:T(8,128)S(1)}, f32[15,8,128]{2,1,0:T(8,128)S(1)}, u32[]{:S(2)}, u32[]{:S(2)}) %collective-permute-start.4) | collective-permute-done | bytes 61472 | tf_op jit(solution)/shard_map/ppermute | solution.py:493
  30.4 2.4 %collective-permute-done.5.r_2_ = f32[15,8,128]{2,1,0:T(8,128)S(1)} collective-permute-done((f32[15,8,128]{2,1,0:T(8,128)S(1)}, f32[15,8,128]{2,1,0:T(8,128)S(1)}, u32[]{:S(2)}, u32[]{:S(2)}) %collective-permute-start.5) | collective-permute-done | bytes 61472 | tf_op jit(solution)/shard_map/ppermute | solution.py:493
  33.0 1.4 %collective-permute-start.6 = (f32[10,2,8,128]{3,2,1,0:T(8,128)S(1)}, f32[10,2,8,128]{3,2,1,0:T(8,128)S(1)}, u32[]{:S(2)}, u32[]{:S(2)}) collective-permute-start(f32[10,2,8,128]{3,2,1,0:T(8,128)S(1)} %get-tuple-element.72), channel_id=1, source_target_pairs={{0,1},{1,2},{2,3},{3,4},{4,5},{5,6},{6,7},{7,8},{8,9},{9,10},{10,1... | collective-permute-start | bytes 245768 | tf_op jit(solution)/shard_map/ppermute | solution.py:493
  34.5 2.0 %shard_map.184 = (f32[5,64,128]{2,1,0:T(8,128)S(1)}, f32[512,128]{1,0:T(8,128)S(1)}, bf16[256,8192]{1,0:T(8,128)(2,1)S(1)}, f32[128,8192]{1,0:T(8,128)S(1)}) custom-call(f32[10,64,128]{2,1,0:T(8,128)S(1)} %get-tuple-element.74.sa_ref, bf16[272,256]{1,0:T(8,128)(2,1)S(1)} %shard_map.181.p_ref), custom_call_target="tpu_custom_call" | custom-call | flops 300000000 | bytes 2000000 | tf_op jit(solution)/shard_map/pallas_call | solution.py:478
  36.5 4.2 %collective-permute-done.6.yl_ref = f32[10,2,8,128]{3,2,1,0:T(8,128)S(1)} collective-permute-done((f32[10,2,8,128]{3,2,1,0:T(8,128)S(1)}, f32[10,2,8,128]{3,2,1,0:T(8,128)S(1)}, u32[]{:S(2)}, u32[]{:S(2)}) %collective-permute-start.6) | collective-permute-done | bytes 81952 | tf_op jit(solution)/shard_map/ppermute | solution.py:493
  40.6 4.1 %shard_map.185 = (f32[10,64,128]{2,1,0:T(8,128)S(1)}, f32[5,64,128]{2,1,0:T(8,128)S(1)}, f32[10,48,128]{2,1,0:T(8,128)S(1)}, f32[15,8,128]{2,1,0:T(8,128)S(1)}, ...) custom-call(f32[10,3,2,8,128]{4,3,2,1,0:T(8,128)S(1)} %get-tuple-ele, ...), custom_call_target="tpu_custom_call" | custom-call | flops 900000000 | bytes 2000000 | tf_op jit(solution)/shard_map/pallas_call | solution.py:478
  44.7 1.7 %collective-permute-start.8 = (f32[15,8,128]{2,1,0:T(8,128)S(1)}, f32[15,8,128]{2,1,0:T(8,128)S(1)}, u32[]{:S(2)}, u32[]{:S(2)}) collective-permute-start(f32[15,8,128]{2,1,0:T(8,128)S(1)} %get-tuple-element.78), channel_id=1, source_target_pairs={{0,16},{16,32},{32,48},{48,64},{64,80},{80,96},{96,112},{112,128},... | collective-permute-start | bytes 184328 | tf_op jit(solution)/shard_map/ppermute | solution.py:493
  46.5 2.5 %collective-permute-start.9 = (f32[15,8,128]{2,1,0:T(8,128)S(1)}, f32[15,8,128]{2,1,0:T(8,128)S(1)}, u32[]{:S(2)}, u32[]{:S(2)}) collective-permute-start(f32[15,8,128]{2,1,0:T(8,128)S(1)} %get-tuple-element.79), channel_id=1, source_target_pairs={{0,240},{16,0},{32,16},{48,32},{64,48},{80,64},{96,80},{112,96},{1... | collective-permute-start | bytes 184328 | tf_op jit(solution)/shard_map/ppermute | solution.py:493
  49.0 2.1 %shard_map.187 = (f32[384,160]{1,0:T(8,128)S(1)}, f32[8,128]{1,0:T(8,128)S(1)}) custom-call(f32[512,128]{1,0:T(8,128)S(1)} %get-tuple-element.85.x_ref, f32[512,128]{1,0:T(8,128)S(1)} %get-tuple-element.86.c_ref, bf16[256,8192]{1,0:T(8,128)(2,1)S(1)} %get-tuple-element.87.hh_ref, bf16[256,8192]{1,0:T(8,128)(2,1)S(1)} %get-tuple-element.88.dd_ref), custom_call_target="tpu_custom_call" | custom-call | flops 300000000 | bytes 2000000 | tf_op jit(solution)/shard_map/pallas_call | solution.py:478
  52.8 3.6 %shard_map.188 = (f32[5,64,128]{2,1,0:T(8,128)S(1)}, f32[48,128]{1,0:T(8,128)S(1)}) custom-call(f32[512,128]{1,0:T(8,128)S(1)} %get-tuple-element.81.x_ref, f32[5,64,128]{2,1,0:T(8,128)S(1)} %get-tuple-element.82.m1_ref, bf16[256,8192]{1,0:T(8,128)(2,1)S(1)} %get-tuple-element.83.hh_ref, f32[128,8192]{1,0:T(8,128)S(1)} %get-tuple-element.84.t_ref, ...), custom_call_target="tpu_custom_call" | custom-call | flops 600000000 | bytes 2000000 | tf_op jit(solution)/shard_map/pallas_call | solution.py:478
  56.4 3.0 %collective-permute-done.10.yl_ref = f32[10,2,8,128]{3,2,1,0:T(8,128)S(1)} collective-permute-done((f32[10,2,8,128]{3,2,1,0:T(8,128)S(1)}, f32[10,2,8,128]{3,2,1,0:T(8,128)S(1)}, u32[]{:S(2)}, u32[]{:S(2)}) %collective-permute-start.10) | collective-permute-done | bytes 81952 | tf_op jit(solution)/shard_map/ppermute | solution.py:493
  59.4 5.0 %collective-permute-start.12 = (f32[48,128]{1,0:T(8,128)S(1)}, f32[48,128]{1,0:T(8,128)S(1)}, u32[]{:S(2)}, u32[]{:S(2)}) collective-permute-start(f32[48,128]{1,0:T(8,128)S(1)} %get-tuple-element.103), channel_id=1, source_target_pairs={{0,16},{1,17},{2,18},{3,19},{4,20},{5,21},{6,22},{7,23},{8,24},{9,... | collective-permute-start | bytes 73736 | tf_op jit(solution)/shard_map/ppermute | solution.py:522
  65.3 12.6 %all_to_all.10 = f32[16,48,128]{2,1,0:T(8,128)S(1)} all-to-all(f32[16,48,128]{2,1,0:T(8,128)S(1)} %broadcast_in_dim.4), channel_id=1, replica_groups={{0,1,2,3,32,33,34,35,64,65,66,67,96,97,98,99},{4,5,6,7,36,37,38,39,68,6..., dimensions={0} | all-to-all | bytes 786432 | tf_op jit(solution)/shard_map/all_to_all | solution.py:515
  78.6 3.4 %all-to-all-start.1 = ((f32[8,48,128]{2,1,0:T(8,128)}), f32[8,48,128]{2,1,0:T(8,128)S(1)}, u32[]{:S(2)}, u32[]{:S(2)}) async-start(f32[8,48,128]{2,1,0:T(8,128)} %broadcast_in_dim.5), calls=%async_computation.1 | async-start | bytes 393216 | tf_op jit(solution)/shard_map/all_to_all | solution.py:515
  82.0 1.0 %shard_map.189 = (f32[5,64,128]{2,1,0:T(8,128)}, f32[5,64,128]{2,1,0:T(8,128)}) custom-call(f32[10,3,2,8,128]{4,3,2,1,0:T(8,128)S(1)} %get-tuple-element.80.w_ref, f32[10,2,8,128]{3,2,1,0:T(8,128)S(1)} %collective-permute-done.10.yl_ref, f32[10,2,8,128]{3,2,1,0:T(8,128)S(1)} %collective-permute-done.11.yr_ref, f32[16,128]{1,0:T(8,128)S(1)} %get-tuple-element.66.mk_ref, ...), custom_call_target="tpu_custom_call" | custom-call | flops 20000000 | bytes 2000000 | tf_op jit(solution)/shard_map/pallas_call | solution.py:478
  83.0 6.3 %all-to-all-done.1.p_ref = f32[8,48,128]{2,1,0:T(8,128)S(1)} async-done(((f32[8,48,128]{2,1,0:T(8,128)}), f32[8,48,128]{2,1,0:T(8,128)S(1)}, u32[]{:S(2)}, u32[]{:S(2)}) %all-to-all-start.1) | async-done | bytes 196640 | tf_op jit(solution)/shard_map/all_to_all | solution.py:515
  (21 shorter events, 6.1 us)
Async XLA Ops:
  2.2 4.2 %collective-permute-start = (f32[18,8,128]{2,1,0:T(8,128)S(1)}, f32[18,8,128]{2,1,0:T(8,128)S(1)}, u32[]{:S(2)}, u32[]{:S(2)}) collective-permute-start(f32[18,8,128]{2,1,0:T(8,128)S(1)} %get-tuple-element.60), channel_id=1, source_target_pairs={{0,16},{16,32},{32,48},{48,64},{64,80},{80,96},{96,112},{112,128},... | collective-permute-start | bytes 221192 | tf_op jit(solution)/shard_map/ppermute | solution.py:493
  5.0 3.8 %collective-permute-start.1 = (f32[18,8,128]{2,1,0:T(8,128)S(1)}, f32[18,8,128]{2,1,0:T(8,128)S(1)}, u32[]{:S(2)}, u32[]{:S(2)}) collective-permute-start(f32[18,8,128]{2,1,0:T(8,128)S(1)} %get-tuple-element.61), channel_id=1, source_target_pairs={{0,240},{16,0},{32,16},{48,32},{64,48},{80,64},{96,80},{112,96},{1... | collective-permute-start | bytes 221192 | tf_op jit(solution)/shard_map/ppermute | solution.py:493
  8.9 12.6 %collective-permute-start.3 = (f32[12,2,8,128]{3,2,1,0:T(8,128)S(1)}, f32[12,2,8,128]{3,2,1,0:T(8,128)S(1)}, u32[]{:S(2)}, u32[]{:S(2)}) collective-permute-start(f32[12,2,8,128]{3,2,1,0:T(8,128)S(1)} %get-tuple-element.63), channel_id=1, source_target_pairs={{0,15},{1,0},{2,1},{3,2},{4,3},{5,4},{6,5},{7,6},{8,7},{9,8},{10,9... | collective-permute-start | bytes 294920 | tf_op jit(solution)/shard_map/ppermute | solution.py:493
  17.5 9.7 %collective-permute-start.2 = (f32[12,2,8,128]{3,2,1,0:T(8,128)S(1)}, f32[12,2,8,128]{3,2,1,0:T(8,128)S(1)}, u32[]{:S(2)}, u32[]{:S(2)}) collective-permute-start(f32[12,2,8,128]{3,2,1,0:T(8,128)S(1)} %get-tuple-element.63), channel_id=1, source_target_pairs={{0,1},{1,2},{2,3},{3,4},{4,5},{5,6},{6,7},{7,8},{8,9},{9,10},{10,1... | collective-permute-start | bytes 294920 | tf_op jit(solution)/shard_map/ppermute | solution.py:493
  27.6 2.9 %collective-permute-start.4 = (f32[15,8,128]{2,1,0:T(8,128)S(1)}, f32[15,8,128]{2,1,0:T(8,128)S(1)}, u32[]{:S(2)}, u32[]{:S(2)}) collective-permute-start(f32[15,8,128]{2,1,0:T(8,128)S(1)} %get-tuple-element.69), channel_id=1, source_target_pairs={{0,16},{16,32},{32,48},{48,64},{64,80},{80,96},{96,112},{112,128},... | collective-permute-start | bytes 184328 | tf_op jit(solution)/shard_map/ppermute | solution.py:493
  29.2 3.6 %collective-permute-start.5 = (f32[15,8,128]{2,1,0:T(8,128)S(1)}, f32[15,8,128]{2,1,0:T(8,128)S(1)}, u32[]{:S(2)}, u32[]{:S(2)}) collective-permute-start(f32[15,8,128]{2,1,0:T(8,128)S(1)} %get-tuple-element.70), channel_id=1, source_target_pairs={{0,240},{16,0},{32,16},{48,32},{64,48},{80,64},{96,80},{112,96},{1... | collective-permute-start | bytes 184328 | tf_op jit(solution)/shard_map/ppermute | solution.py:493
  32.9 3.5 %collective-permute-start.7 = (f32[10,2,8,128]{3,2,1,0:T(8,128)S(1)}, f32[10,2,8,128]{3,2,1,0:T(8,128)S(1)}, u32[]{:S(2)}, u32[]{:S(2)}) collective-permute-start(f32[10,2,8,128]{3,2,1,0:T(8,128)S(1)} %get-tuple-element.72), channel_id=1, source_target_pairs={{0,15},{1,0},{2,1},{3,2},{4,3},{5,4},{6,5},{7,6},{8,7},{9,8},{10,9... | collective-permute-start | bytes 245768 | tf_op jit(solution)/shard_map/ppermute | solution.py:493
  33.0 7.6 %collective-permute-start.6 = (f32[10,2,8,128]{3,2,1,0:T(8,128)S(1)}, f32[10,2,8,128]{3,2,1,0:T(8,128)S(1)}, u32[]{:S(2)}, u32[]{:S(2)}) collective-permute-start(f32[10,2,8,128]{3,2,1,0:T(8,128)S(1)} %get-tuple-element.72), channel_id=1, source_target_pairs={{0,1},{1,2},{2,3},{3,4},{4,5},{5,6},{6,7},{7,8},{8,9},{9,10},{10,1... | collective-permute-start | bytes 245768 | tf_op jit(solution)/shard_map/ppermute | solution.py:493
  44.7 6.3 %collective-permute-start.8 = (f32[15,8,128]{2,1,0:T(8,128)S(1)}, f32[15,8,128]{2,1,0:T(8,128)S(1)}, u32[]{:S(2)}, u32[]{:S(2)}) collective-permute-start(f32[15,8,128]{2,1,0:T(8,128)S(1)} %get-tuple-element.78), channel_id=1, source_target_pairs={{0,16},{16,32},{32,48},{48,64},{64,80},{80,96},{96,112},{112,128},... | collective-permute-start | bytes 184328 | tf_op jit(solution)/shard_map/ppermute | solution.py:493
  46.5 4.6 %collective-permute-start.9 = (f32[15,8,128]{2,1,0:T(8,128)S(1)}, f32[15,8,128]{2,1,0:T(8,128)S(1)}, u32[]{:S(2)}, u32[]{:S(2)}) collective-permute-start(f32[15,8,128]{2,1,0:T(8,128)S(1)} %get-tuple-element.79), channel_id=1, source_target_pairs={{0,240},{16,0},{32,16},{48,32},{64,48},{80,64},{96,80},{112,96},{1... | collective-permute-start | bytes 184328 | tf_op jit(solution)/shard_map/ppermute | solution.py:493
  51.2 5.2 %collective-permute-start.11 = (f32[10,2,8,128]{3,2,1,0:T(8,128)S(1)}, f32[10,2,8,128]{3,2,1,0:T(8,128)S(1)}, u32[]{:S(2)}, u32[]{:S(2)}) collective-permute-start(f32[10,2,8,128]{3,2,1,0:T(8,128)S(1)} %get-tuple-element.95), channel_id=1, source_target_pairs={{0,15},{1,0},{2,1},{3,2},{4,3},{5,4},{6,5},{7,6},{8,7},{9,8},{10,9... | collective-permute-start | bytes 245768 | tf_op jit(solution)/shard_map/ppermute | solution.py:493
  51.8 7.6 %collective-permute-start.10 = (f32[10,2,8,128]{3,2,1,0:T(8,128)S(1)}, f32[10,2,8,128]{3,2,1,0:T(8,128)S(1)}, u32[]{:S(2)}, u32[]{:S(2)}) collective-permute-start(f32[10,2,8,128]{3,2,1,0:T(8,128)S(1)} %get-tuple-element.95), channel_id=1, source_target_pairs={{0,1},{1,2},{2,3},{3,4},{4,5},{5,6},{6,7},{7,8},{8,9},{9,10},{10,1... | collective-permute-start | bytes 245768 | tf_op jit(solution)/shard_map/ppermute | solution.py:493
  59.4 5.9 %collective-permute-start.12 = (f32[48,128]{1,0:T(8,128)S(1)}, f32[48,128]{1,0:T(8,128)S(1)}, u32[]{:S(2)}, u32[]{:S(2)}) collective-permute-start(f32[48,128]{1,0:T(8,128)S(1)} %get-tuple-element.103), channel_id=1, source_target_pairs={{0,16},{1,17},{2,18},{3,19},{4,20},{5,21},{6,22},{7,23},{8,24},{9,... | collective-permute-start | bytes 73736 | tf_op jit(solution)/shard_map/ppermute | solution.py:522
  78.6 10.8 %all-to-all-start.1 = ((f32[8,48,128]{2,1,0:T(8,128)}), f32[8,48,128]{2,1,0:T(8,128)S(1)}, u32[]{:S(2)}, u32[]{:S(2)}) async-start(f32[8,48,128]{2,1,0:T(8,128)} %broadcast_in_dim.5), calls=%async_computation.1 | async-start | bytes 393216 | tf_op jit(solution)/shard_map/all_to_all | solution.py:515

commit v3 on v2

--- a/solution.py
+++ b/solution.py
@@ -98,27 +98,35 @@
     return v + jnp.where(here, d, zero), jnp.where(out, d, zero)
 
 
-def xy_body(n, w_ref, rp_ref, rm_ref, wo_ref, y_ref):
+def xy_body(n, w_ref, rp_ref, rm_ref, wo_ref, yu_ref, yd_ref):
+    ys = []
     w = w_ref[...]
     v0, v1 = xadd(w, rp_ref[...], rm_ref[...])
     for part, v in enumerate((v0, v1)):
         v, e = ylocal(v)
         wo_ref[:, :, part] = v.reshape(n, 3, 8, 128)
         e = e.reshape(n, 3, 8, 128)
-        y_ref[:, part] = e[:, 0] + sroll(e[:, 1], 1) + sroll(e[:, 2], 2)
+        ys.append(e[:, 0] + sroll(e[:, 1], 1) + sroll(e[:, 2], 2))
+    left = iota((n, 8, 128), 2) < 64
+    m = yu_ref.shape[0]
+    yu_ref[...] = jnp.where(left, ys[0], pltpu.roll(ys[1], 64, 2))[:m]
+    yd_ref[...] = jnp.where(left, pltpu.roll(ys[0], 64, 2), ys[1])[:m]
 
 
 def yadd(w, yl, yr):
-    n = w.shape[0]
-    left = iota((n * 2, 8, 128), 2) < 64
-    b = iota((n * 2, 8, 128), 1) & 3
-    z = jnp.where(left, yl.reshape(n * 2, 8, 128), yr.reshape(n * 2, 8, 128))
+    m = yl.shape[0]
+    left = iota((m, 8, 128), 2) < 64
+    b = iota((m, 8, 128), 1) & 3
     use = ((b == 0) & left) | ((b == 3) & (~left))
-    parts = []
+    zs = (
+        jnp.where(left, yl, pltpu.roll(yr, 64, 2)),
+        jnp.where(left, pltpu.roll(yl, 64, 2), yr),
+    )
+    rows = []
     for q in range(3):
-        add = jnp.where(use, sroll(z, -q), jnp.zeros_like(z)).reshape(n, 2, 8, 128)
-        parts.append((w[:, q] + add).reshape(n, 16, 128))
-    return jnp.concatenate(parts, axis=1)
+        for part, z in enumerate(zs):
+            rows.append(w[:m, q, part] + jnp.where(use, sroll(z, -q), jnp.zeros_like(z)))
+    return jnp.concatenate(rows, axis=1)
 
 
 def one_hot(order):
@@ -390,21 +398,7 @@
     up_ref[...], dn_ref[...] = xpack(wz)
 
 
-def grads_body(x_ref, c_ref, hh_ref, dd_ref, gw_ref, gb_ref):
-    def chunk(i, acc):
-        n0 = i * CH
-        at = lanes_of(i)
-        return add_grads(
-            acc, load8(x_ref, n0), load8(c_ref, n0),
-            hh_ref[0:128, at], hh_ref[128:256, at], dd_ref[0:128, at], dd_ref[128:256, at],
-        )
-
-    gw_ref[...], gb_ref[...] = lax.fori_loop(0, 64 // CH, chunk, no_grads())
-
-
-def first_body(
-    x_ref, m1_ref, hh_ref, t_ref, p_ref, gw_ref, gb_ref, back_ref, pay_ref, c_ref, b_ref
-):
+def first_body(x_ref, m1_ref, hh_ref, t_ref, p_ref, back_ref, gw_ref, gb_ref, c_ref, b_ref):
     put_fields(c_ref, m1_ref[...], False)
     w = weights(p_ref)
 
@@ -419,8 +413,20 @@
             jnp.concatenate([d2h, d2l], axis=0), jnp.concatenate([d1h, d1l], axis=0),
         )
 
+    gw_ref[...], gb_ref[...] = lax.fori_loop(0, 64 // CH, chunk, no_grads())
+    back_ref[...] = b_ref[0 : F * 64].reshape(F, 64, 128)
+
+
+def grads_body(x_ref, c_ref, hh_ref, dd_ref, gw_ref, gb_ref, pay_ref):
+    def chunk(i, acc):
+        n0 = i * CH
+        at = lanes_of(i)
+        return add_grads(
+            acc, load8(x_ref, n0), load8(c_ref, n0),
+            hh_ref[0:128, at], hh_ref[128:256, at], dd_ref[0:128, at], dd_ref[128:256, at],
+        )
+
     g, gb = lax.fori_loop(0, 64 // CH, chunk, (gw_ref[...], gb_ref[...]))
-    back_ref[...] = b_ref[0 : F * 64].reshape(F, 64, 128)
 
     def fold(t):
         return t + pltpu.roll(t, 64, 1)
@@ -455,10 +461,8 @@
                 ref[f, pl.ds(q, 16, stride=4), :] = y[r : r + 16]
 
 
-def output_body(p_ref, gw1_ref, gb1_ref, gw2_ref, gb2_ref, gwo_ref, gbo_ref):
-    pay = p_ref[0]
-    for i in range(1, 8):
-        pay = pay + p_ref[i]
+def output_body(l_ref, h_ref, gw1_ref, gb1_ref, gw2_ref, gb2_ref, gwo_ref, gbo_ref):
+    pay = jnp.concatenate([l_ref[...], h_ref[...]], axis=0)
     gw2_ref[0:32] = pay[0:32, 0:64]
     other = pltpu.roll(pay, 64, 1)
     gw2_ref[32:64] = other[0:32, 0:64]
@@ -515,13 +519,32 @@
     return lax.all_to_all(y, ("sub", "col"), 0, 0, axis_index_groups=groups, tiled=True)
 
 
-def all_sum(x):
-    if (lax.axis_size("sub"), lax.axis_size("col")) != (16, 16):
-        x = lax.psum(x, ("sub", "col"))
-        return jnp.concatenate([x[None], jnp.zeros((7,) + x.shape, f32)], axis=0)
-    x = x + lax.ppermute(x, ("sub", "col"), [(d, d ^ 16) for d in range(256)])
-    x = send_to_all(x, together((0, 2, 3))).sum(0)
-    return send_to_all(x, together((1, 2, 4)))
+SWAP = [(d, d ^ 16) for d in range(256)]
+
+
+def grid_is_whole():
+    return (lax.axis_size("sub"), lax.axis_size("col")) == (16, 16)
+
+
+def on_first_core():
+    return lax.axis_index("sub") % 2 == 0
+
+
+def chip_sum(x):
+    core, low, high = on_first_core(), x[:24], x[24:]
+    mine = jnp.where(core, low, high)
+    return mine + lax.ppermute(jnp.where(core, high, low), ("sub", "col"), SWAP)
+
+
+def plane_sum(x):
+    return send_to_all(x, together((0, 2, 3))).sum(0)
+
+
+def rest_sum(x):
+    core = on_first_core()
+    x = send_to_all(x, together((1, 2, 4))).sum(0)
+    other = lax.ppermute(x, ("sub", "col"), SWAP)
+    return jnp.where(core, x, other), jnp.where(core, other, x)
 
 
 def on_device(
@@ -541,15 +564,15 @@
     wide = jax.ShapeDtypeStruct((256, 8192), bf16)
     khot = jax.ShapeDtypeStruct((64, 192), bf16)
 
-    def in_device(w, up, dn, n):
-        rp, rm = both_ways(up, dn, "sub")
+    def in_device(w, rp, rm, n):
+        m = 10 if n == 10 else 11
         return call(
-            lambda *r: xy_body(n, *r), [(n, 3, 2, 8, 128), (n, 2, 8, 128)], [w, rp, rm]
+            lambda *r: xy_body(n, *r), [(n, 3, 2, 8, 128), (m, 8, 128), (m, 8, 128)], [w, rp, rm]
         )
 
     def faces(w, up, dn, n):
-        w, y = in_device(w, up, dn, n)
-        yl, yr = both_ways(y, y, "col")
+        w, yu, yd = in_device(w, *both_ways(up, dn, "sub"), n)
+        yl, yr = both_ways(yu, yd, "col")
         return w, yl, yr
 
     w, up, dn, mk, g, kmat = call(
@@ -606,24 +629,28 @@
         flops=900000000,
         trans=1000000,
     )
-    acc = call(
-        grads_body,
-        [(384, 160), (8, 128)],
-        [x1, c1, hh1, dd1],
-        flops=300000000,
-    )
-    w, y = in_device(w, up, dn, 10)
-    acc, y = lax.optimization_barrier((acc, y))
-    yl, yr = both_ways(y, y, "col")
-    back, pay = call(
+    back, gw, gb = call(
         first_body,
-        [(F, 64, 128), (48, 128)],
-        [x0, m1, hh0, t0, pw, *acc],
+        [(F, 64, 128), (384, 160), (8, 128)],
+        [x0, m1, hh0, t0, pw],
         [(512, 128)] * 2,
         flops=600000000,
     )
-    pay, yl, yr = lax.optimization_barrier((pay, yl, yr))
-    terms = all_sum(pay)
+    rp, rm = both_ways(up, dn, "sub")
+    gw, rp, rm = lax.optimization_barrier((gw, rp, rm))
+    (pay,) = call(grads_body, [(48, 128)], [x1, c1, hh1, dd1, gw, gb], flops=300000000)
+    w, yu, yd = in_device(w, rp, rm, 10)
+    if grid_is_whole():
+        pay = chip_sum(pay)
+        pay, yu, yd = lax.optimization_barrier((pay, yu, yd))
+        yl, yr = both_ways(yu, yd, "col")
+        pay = plane_sum(pay)
+        pay, yl, yr = lax.optimization_barrier((pay, yl, yr))
+        terms = list(rest_sum(pay))
+    else:
+        yl, yr = both_ways(yu, yd, "col")
+        pay = lax.psum(pay, ("sub", "col"))
+        terms = [pay[:24], pay[24:]]
     out_state, out_adj = call(
         finish_body,
         [(F, 64, 128), (F, 64, 128)],
@@ -631,7 +658,7 @@
         flops=20000000,
     )
     gw1, gb1, gw2, gb2, gwo, gbo = call(
-        output_body, [(5, 64), (1, 64), (64, 64), (1, 64), (5, 64), (1, 5)], [terms]
+        output_body, [(5, 64), (1, 64), (64, 64), (1, 64), (5, 64), (1, 5)], terms
     )
     return (
         out_state,

time: 91.5 us -> 92.9 us (1.015); the launches traced: 90.1 us -> 92.5 us
  waiting for transfers between devices: 29.7 us -> 8.66 us
  local copies, waits for them, and re-layouts: 0.71 us -> 13 us
  starting transfers between devices: 29.3 us -> 40 us
    ppermute x12, waiting for transfers between devices: 22.5 us -> 6.11 us  [shift(): return lax.ppermute(x, axis, [(i, (i + step) % n) for i in range(n)])]
    unnamed x0 -> x16, local copies, waits for them, and re-layouts: none -> 12.3 us
    ppermute x12, starting transfers between devices: 20.9 us -> 29.5 us  [shift(): return lax.ppermute(x, axis, [(i, (i + step) % n) for i in range(n)])]
    all_to_all x1, waiting for transfers between devices: 6.33 us -> 1.94 us  [send_to_all(): lax.all_to_all(y, ('sub', 'col'), 0, 0, axis_index_groups=groups, tiled=T...]
    ppermute x1 -> x2, starting transfers between devices: 5 us -> 6.96 us  [the longest x1 3.93 us: chip_sum(): return mine + lax.ppermute(jnp.where(core, high, low), ('sub', 'col'), SWAP)]
  transfers between devices with their start and end apart: 14 -> 15, of which waited for: 10 -> 7; matrix products, arithmetic and copies ran while one was open for 0% -> 0% of each run, Pallas kernels for 11% -> 9%
where the time goes in v3:
time: 92.9 us; the launch traced here: 92.5 us
  starting transfers between devices  40 us (43%)
  Pallas kernels  17.5 us (19%)
  local copies, waits for them, and re-layouts  13 us (14%)
  blocking collectives  12.5 us (13%)
  waiting for transfers between devices  8.66 us (9%)
    ppermute x12, starting transfers between devices, shift(): return lax.ppermute(x, axis, [(i, (i + step) % n) for i in range(n)])  29.5 us
    pallas_call x12, Pallas kernels, call(): pl.pallas_call(body, out_shape=shapes, in_specs=[pl.BlockSpec(memory_spac...  17.5 us
    all_to_all x1, blocking collectives, send_to_all(): lax.all_to_all(y, ('sub', 'col'), 0, 0, axis_index_groups=groups, tiled=T...  12.5 us
    unnamed x16, local copies, waits for them, and re-layouts  12.3 us
    ppermute x12, waiting for transfers between devices, shift(): return lax.ppermute(x, axis, [(i, (i + step) % n) for i in range(n)])  6.11 us
    ppermute x1, starting transfers between devices, chip_sum(): return mine + lax.ppermute(jnp.where(core, high, low), ('sub', 'col'), SWAP)  3.93 us
    all_to_all x1, starting transfers between devices, send_to_all(): lax.all_to_all(y, ('sub', 'col'), 0, 0, axis_index_groups=groups, tiled=T...  3.52 us
    ppermute x1, starting transfers between devices, rest_sum(): other = lax.ppermute(x, ('sub', 'col'), SWAP)  3.03 us
  transfers between devices with their start and end apart: 15, of which 7 were waited for; matrix products, arithmetic and copies ran while one was open for 0% of the time, Pallas kernels for 9%

profile of v3, /device:TPU:1, one launch (start us, length us, event | category | flops | bytes accessed | tf_op | source)
XLA Modules:
  0.0 92.5 jit_solution(13825060638617218874)
XLA Ops:
  0.6 1.6 %shard_map.179 = (f32[12,48,128]{2,1,0:T(8,128)S(1)}, f32[18,8,128]{2,1,0:T(8,128)S(1)}, f32[18,8,128]{2,1,0:T(8,128)S(1)}, f32[16,128]{1,0:T(8,128)S(1)}, bf16[...) custom-call(f32[5,64,128]{2,1,0:T(8,128)} %s_in.1, f32[5,64,128]{2,1,0:T(8,128)} %c_in.1, s32[1,128]{1,0:T(1,128)} %o_in.1, ...), custom_call_target="tpu_custom_call" | custom-call | bytes 2000000 | tf_op jit(solution)/shard_map/pallas_call | solution.py:482
  2.2 2.8 %collective-permute-start = (f32[18,8,128]{2,1,0:T(8,128)S(1)}, f32[18,8,128]{2,1,0:T(8,128)S(1)}, u32[]{:S(2)}, u32[]{:S(2)}) collective-permute-start(f32[18,8,128]{2,1,0:T(8,128)S(1)} %get-tuple-element.65), channel_id=1, source_target_pairs={{0,16},{16,32},{32,48},{48,64},{64,80},{80,96},{96,112},{112,128},... | collective-permute-start | bytes 221192 | tf_op jit(solution)/shard_map/ppermute | solution.py:497
  6.4 2.4 %collective-permute-done.1.r_2_ = f32[18,8,128]{2,1,0:T(8,128)S(1)} collective-permute-done((f32[18,8,128]{2,1,0:T(8,128)S(1)}, f32[18,8,128]{2,1,0:T(8,128)S(1)}, u32[]{:S(2)}, u32[]{:S(2)}) %collective-permute-start.1) | collective-permute-done | bytes 73760 | tf_op jit(solution)/shard_map/ppermute | solution.py:497
  9.0 1.6 %collective-permute-start.2 = (f32[11,8,128]{2,1,0:T(8,128)S(1)}, f32[11,8,128]{2,1,0:T(8,128)S(1)}, u32[]{:S(2)}, u32[]{:S(2)}) collective-permute-start(f32[11,8,128]{2,1,0:T(8,128)S(1)} %get-tuple-element.68), channel_id=1, source_target_pairs={{0,1},{1,2},{2,3},{3,4},{4,5},{5,6},{6,7},{7,8},{8,9},{9,10},{10,1... | collective-permute-start | bytes 135176 | tf_op jit(solution)/shard_map/ppermute | solution.py:497
  10.6 7.1 %collective-permute-start.3 = (f32[11,8,128]{2,1,0:T(8,128)S(1)}, f32[11,8,128]{2,1,0:T(8,128)S(1)}, u32[]{:S(2)}, u32[]{:S(2)}) collective-permute-start(f32[11,8,128]{2,1,0:T(8,128)S(1)} %get-tuple-element.69), channel_id=1, source_target_pairs={{0,15},{1,0},{2,1},{3,2},{4,3},{5,4},{6,5},{7,6},{8,7},{9,8},{10,9... | collective-permute-start | bytes 135176 | tf_op jit(solution)/shard_map/ppermute | solution.py:497
  21.9 2.0 %collective-permute-done.5.r_2_ = f32[15,8,128]{2,1,0:T(8,128)S(1)} collective-permute-done((f32[15,8,128]{2,1,0:T(8,128)S(1)}, f32[15,8,128]{2,1,0:T(8,128)S(1)}, u32[]{:S(2)}, u32[]{:S(2)}) %collective-permute-start.5) | collective-permute-done | bytes 61472 | tf_op jit(solution)/shard_map/ppermute | solution.py:497
  24.2 6.2 %collective-permute-start.7 = (f32[10,8,128]{2,1,0:T(8,128)S(1)}, f32[10,8,128]{2,1,0:T(8,128)S(1)}, u32[]{:S(2)}, u32[]{:S(2)}) collective-permute-start(f32[10,8,128]{2,1,0:T(8,128)S(1)} %get-tuple-element.79), channel_id=1, source_target_pairs={{0,15},{1,0},{2,1},{3,2},{4,3},{5,4},{6,5},{7,6},{8,7},{9,8},{10,9... | collective-permute-start | bytes 122888 | tf_op jit(solution)/shard_map/ppermute | solution.py:497
  30.4 2.0 %shard_map.184 = (f32[5,64,128]{2,1,0:T(8,128)S(1)}, f32[512,128]{1,0:T(8,128)S(1)}, bf16[256,8192]{1,0:T(8,128)(2,1)S(1)}, f32[128,8192]{1,0:T(8,128)S(1)}) custom-call(f32[10,64,128]{2,1,0:T(8,128)S(1)} %get-tuple-element.81.sa_ref, bf16[272,256]{1,0:T(8,128)(2,1)S(1)} %shard_map.181.p_ref), custom_call_target="tpu_custom_call" | custom-call | flops 300000000 | bytes 2000000 | tf_op jit(solution)/shard_map/pallas_call | solution.py:482
  32.4 1.9 %copy-done = bf16[256,8192]{1,0:T(8,128)(2,1)} copy-done((bf16[256,8192]{1,0:T(8,128)(2,1)}, bf16[256,8192]{1,0:T(8,128)(2,1)S(1)}, u32[]{:S(2)}) %copy-start) | copy-done | bytes 4194328
  34.3 2.0 %copy-done.2 = f32[128,8192]{1,0:T(8,128)} copy-done((f32[128,8192]{1,0:T(8,128)}, f32[128,8192]{1,0:T(8,128)S(1)}, u32[]{:S(2)}) %copy-start.2) | copy-done | bytes 4194328
  36.3 4.1 %shard_map.185 = (f32[10,64,128]{2,1,0:T(8,128)S(1)}, f32[5,64,128]{2,1,0:T(8,128)S(1)}, f32[10,48,128]{2,1,0:T(8,128)S(1)}, f32[15,8,128]{2,1,0:T(8,128)S(1)}, ...) custom-call(f32[10,3,2,8,128]{4,3,2,1,0:T(8,128)S(1)} %get-tuple-ele, ...), custom_call_target="tpu_custom_call" | custom-call | flops 900000000 | bytes 2000000 | tf_op jit(solution)/shard_map/pallas_call | solution.py:482
  40.5 2.0 %copy-done.4 = bf16[256,8192]{1,0:T(8,128)(2,1)} copy-done((bf16[256,8192]{1,0:T(8,128)(2,1)}, bf16[256,8192]{1,0:T(8,128)(2,1)S(1)}, u32[]{:S(2)}) %copy-start.4) | copy-done | bytes 4194328
  42.5 1.9 %copy-done.6 = bf16[256,8192]{1,0:T(8,128)(2,1)} copy-done((bf16[256,8192]{1,0:T(8,128)(2,1)}, bf16[256,8192]{1,0:T(8,128)(2,1)S(1)}, u32[]{:S(2)}) %copy-start.6) | copy-done | bytes 4194328
  44.7 3.5 %collective-permute-start.9 = (f32[15,8,128]{2,1,0:T(8,128)S(1)}, f32[15,8,128]{2,1,0:T(8,128)S(1)}, u32[]{:S(2)}, u32[]{:S(2)}) collective-permute-start(f32[15,8,128]{2,1,0:T(8,128)S(1)} %get-tuple-element.91), channel_id=1, source_target_pairs={{0,240},{16,0},{32,16},{48,32},{64,48},{80,64},{96,80},{112,96},{1... | collective-permute-start | bytes 184328 | tf_op jit(solution)/shard_map/ppermute | solution.py:497
  48.2 2.2 %copy-done.1 = bf16[256,8192]{1,0:T(8,128)(2,1)S(1)} copy-done((bf16[256,8192]{1,0:T(8,128)(2,1)S(1)}, bf16[256,8192]{1,0:T(8,128)(2,1)}, u32[]{:S(2)}) %copy-start.1) | copy-done | bytes 4194328
  50.4 2.2 %copy-done.3 = f32[128,8192]{1,0:T(8,128)S(1)} copy-done((f32[128,8192]{1,0:T(8,128)S(1)}, f32[128,8192]{1,0:T(8,128)}, u32[]{:S(2)}) %copy-start.3) | copy-done | bytes 4194328
  52.6 3.5 %shard_map.186 = (f32[5,64,128]{2,1,0:T(8,128)S(1)}, f32[384,160]{1,0:T(8,128)S(1)}, f32[8,128]{1,0:T(8,128)S(1)}) custom-call(f32[512,128]{1,0:T(8,128)S(1)} %get-tuple-element.85.x_ref, f32[5,64,128]{2,1,0:T(8,128)S(1)} %get-tuple-element.86.m1_ref, bf16[256,8192]{1,0:T(8,128)(2,1)S(1)} %copy-done.1, f32[128,8192]{1,0:T(8,128)S(1)} %copy-done.3, ...), custom_call_target="tpu_custom_call" | custom-call | flops 600000000 | bytes 2000000 | tf_op jit(solution)/shard_map/pallas_call | solution.py:482
  56.1 2.3 %shard_map.188 = f32[48,128]{1,0:T(8,128)S(1)} custom-call(f32[512,128]{1,0:T(8,128)S(1)} %get-tuple-element.95.x_ref, f32[512,128]{1,0:T(8,128)S(1)} %get-tuple-element.96.c_ref, bf16[256,8192]{1,0:T(8,128)(2,1)S(1)} %copy-done.5, bf16[256,8192]{1,0:T(8,128)(2,1)S(1)} %copy-done.7, f32[384,160]{1,0:T(8,128)S(1)} %get-tuple-element.99.gw_ref, ...), custom_call_target="tpu_custom_call" | custom-call | flops 300000000 | bytes 2000000 | tf_op jit(solution)/shard_map/pallas_call | solution.py:482
  58.4 3.9 %collective-permute-start.10 = (f32[24,128]{1,0:T(8,128)S(1)}, f32[24,128]{1,0:T(8,128)S(1)}, u32[]{:S(2)}, u32[]{:S(2)}) collective-permute-start(f32[24,128]{1,0:T(8,128)S(1)} %slice_select_fusion), channel_id=1, source_target_pairs={{0,16},{1,17},{2,18},{3,19},{4,20},{5,21},{6,22},{7,23},{8,24},{9,... | collective-permute-start | bytes 36872 | tf_op jit(solution)/shard_map/ppermute | solution.py:536
  63.9 3.5 %all-to-all-start = ((f32[16,24,128]{2,1,0:T(8,128)}), f32[16,24,128]{2,1,0:T(8,128)S(1)}, u32[]{:S(2)}, u32[]{:S(2)}) async-start(f32[16,24,128]{2,1,0:T(8,128)} %broadcast_in_dim.4), calls=%async_computation | async-start | bytes 393216 | tf_op jit(solution)/shard_map/all_to_all | solution.py:519
  68.7 4.5 %collective-permute-start.12 = (f32[10,8,128]{2,1,0:T(8,128)S(1)}, f32[10,8,128]{2,1,0:T(8,128)S(1)}, u32[]{:S(2)}, u32[]{:S(2)}) collective-permute-start(f32[10,8,128]{2,1,0:T(8,128)S(1)} %get-tuple-element.105), channel_id=1, source_target_pairs={{0,15},{1,0},{2,1},{3,2},{4,3},{5,4},{6,5},{7,6},{8,7},{9,8},{10,9... | collective-permute-start | bytes 122888 | tf_op jit(solution)/shard_map/ppermute | solution.py:497
  73.2 1.9 %all-to-all-done = f32[16,24,128]{2,1,0:T(8,128)S(1)} async-done(((f32[16,24,128]{2,1,0:T(8,128)}), f32[16,24,128]{2,1,0:T(8,128)S(1)}, u32[]{:S(2)}, u32[]{:S(2)}) %all-to-all-start) | async-done | bytes 196640 | tf_op jit(solution)/shard_map/all_to_all | solution.py:519
  75.2 12.5 %all_to_all.10 = f32[8,24,128]{2,1,0:T(8,128)S(1)} all-to-all(f32[8,24,128]{2,1,0:T(8,128)S(1)} %broadcast_in_dim.5), channel_id=1, replica_groups={{0,4,8,12,128,132,136,140},{1,5,9,13,129,133,137,141},{2,6,10,14,130,13..., dimensions={0} | all-to-all | bytes 196608 | tf_op jit(solution)/shard_map/all_to_all | solution.py:519
  87.6 3.0 %collective-permute-start.13 = (f32[24,128]{1,0:T(8,128)S(1)}, f32[24,128]{1,0:T(8,128)S(1)}, u32[]{:S(2)}, u32[]{:S(2)}) collective-permute-start(f32[24,128]{1,0:T(8,128)S(1)} %reduce_sum.19), channel_id=1, source_target_pairs={{0,16},{1,17},{2,18},{3,19},{4,20},{5,21},{6,22},{7,23},{8,24},{9,... | collective-permute-start | bytes 36872 | tf_op jit(solution)/shard_map/ppermute | solution.py:546
  (42 shorter events, 11.0 us)
Async XLA Ops:
  2.2 4.2 %collective-permute-start = (f32[18,8,128]{2,1,0:T(8,128)S(1)}, f32[18,8,128]{2,1,0:T(8,128)S(1)}, u32[]{:S(2)}, u32[]{:S(2)}) collective-permute-start(f32[18,8,128]{2,1,0:T(8,128)S(1)} %get-tuple-element.65), channel_id=1, source_target_pairs={{0,16},{16,32},{32,48},{48,64},{64,80},{80,96},{96,112},{112,128},... | collective-permute-start | bytes 221192 | tf_op jit(solution)/shard_map/ppermute | solution.py:497
  5.0 3.8 %collective-permute-start.1 = (f32[18,8,128]{2,1,0:T(8,128)S(1)}, f32[18,8,128]{2,1,0:T(8,128)S(1)}, u32[]{:S(2)}, u32[]{:S(2)}) collective-permute-start(f32[18,8,128]{2,1,0:T(8,128)S(1)} %get-tuple-element.66), channel_id=1, source_target_pairs={{0,240},{16,0},{32,16},{48,32},{64,48},{80,64},{96,80},{112,96},{1... | collective-permute-start | bytes 221192 | tf_op jit(solution)/shard_map/ppermute | solution.py:497
  9.0 10.1 %collective-permute-start.2 = (f32[11,8,128]{2,1,0:T(8,128)S(1)}, f32[11,8,128]{2,1,0:T(8,128)S(1)}, u32[]{:S(2)}, u32[]{:S(2)}) collective-permute-start(f32[11,8,128]{2,1,0:T(8,128)S(1)} %get-tuple-element.68), channel_id=1, source_target_pairs={{0,1},{1,2},{2,3},{3,4},{4,5},{5,6},{6,7},{7,8},{8,9},{9,10},{10,1... | collective-permute-start | bytes 135176 | tf_op jit(solution)/shard_map/ppermute | solution.py:497
  10.6 8.5 %collective-permute-start.3 = (f32[11,8,128]{2,1,0:T(8,128)S(1)}, f32[11,8,128]{2,1,0:T(8,128)S(1)}, u32[]{:S(2)}, u32[]{:S(2)}) collective-permute-start(f32[11,8,128]{2,1,0:T(8,128)S(1)} %get-tuple-element.69), channel_id=1, source_target_pairs={{0,15},{1,0},{2,1},{3,2},{4,3},{5,4},{6,5},{7,6},{8,7},{9,8},{10,9... | collective-permute-start | bytes 135176 | tf_op jit(solution)/shard_map/ppermute | solution.py:497
  19.6 2.3 %collective-permute-start.4 = (f32[15,8,128]{2,1,0:T(8,128)S(1)}, f32[15,8,128]{2,1,0:T(8,128)S(1)}, u32[]{:S(2)}, u32[]{:S(2)}) collective-permute-start(f32[15,8,128]{2,1,0:T(8,128)S(1)} %get-tuple-element.75), channel_id=1, source_target_pairs={{0,16},{16,32},{32,48},{48,64},{64,80},{80,96},{96,112},{112,128},... | collective-permute-start | bytes 184328 | tf_op jit(solution)/shard_map/ppermute | solution.py:497
  20.2 3.6 %collective-permute-start.5 = (f32[15,8,128]{2,1,0:T(8,128)S(1)}, f32[15,8,128]{2,1,0:T(8,128)S(1)}, u32[]{:S(2)}, u32[]{:S(2)}) collective-permute-start(f32[15,8,128]{2,1,0:T(8,128)S(1)} %get-tuple-element.76), channel_id=1, source_target_pairs={{0,240},{16,0},{32,16},{48,32},{64,48},{80,64},{96,80},{112,96},{1... | collective-permute-start | bytes 184328 | tf_op jit(solution)/shard_map/ppermute | solution.py:497
  24.1 12.2 %collective-permute-start.6 = (f32[10,8,128]{2,1,0:T(8,128)S(1)}, f32[10,8,128]{2,1,0:T(8,128)S(1)}, u32[]{:S(2)}, u32[]{:S(2)}) collective-permute-start(f32[10,8,128]{2,1,0:T(8,128)S(1)} %get-tuple-element.78), channel_id=1, source_target_pairs={{0,1},{1,2},{2,3},{3,4},{4,5},{5,6},{6,7},{7,8},{8,9},{9,10},{10,1... | collective-permute-start | bytes 122888 | tf_op jit(solution)/shard_map/ppermute | solution.py:497
  24.2 12.1 %collective-permute-start.7 = (f32[10,8,128]{2,1,0:T(8,128)S(1)}, f32[10,8,128]{2,1,0:T(8,128)S(1)}, u32[]{:S(2)}, u32[]{:S(2)}) collective-permute-start(f32[10,8,128]{2,1,0:T(8,128)S(1)} %get-tuple-element.79), channel_id=1, source_target_pairs={{0,15},{1,0},{2,1},{3,2},{4,3},{5,4},{6,5},{7,6},{8,7},{9,8},{10,9... | collective-permute-start | bytes 122888 | tf_op jit(solution)/shard_map/ppermute | solution.py:497
  32.3 2.0 %copy-start = (bf16[256,8192]{1,0:T(8,128)(2,1)}, bf16[256,8192]{1,0:T(8,128)(2,1)S(1)}, u32[]{:S(2)}) copy-start(bf16[256,8192]{1,0:T(8,128)(2,1)S(1)} %get-tuple-element.87.hh_ref) | copy-start | bytes 12582916
  34.3 2.0 %copy-start.2 = (f32[128,8192]{1,0:T(8,128)}, f32[128,8192]{1,0:T(8,128)S(1)}, u32[]{:S(2)}) copy-start(f32[128,8192]{1,0:T(8,128)S(1)} %get-tuple-element.88.t_ref) | copy-start | bytes 12582916
  40.5 2.0 %copy-start.4 = (bf16[256,8192]{1,0:T(8,128)(2,1)}, bf16[256,8192]{1,0:T(8,128)(2,1)S(1)}, u32[]{:S(2)}) copy-start(bf16[256,8192]{1,0:T(8,128)(2,1)S(1)} %get-tuple-element.97.hh_ref) | copy-start | bytes 12582916
  42.5 1.9 %copy-start.6 = (bf16[256,8192]{1,0:T(8,128)(2,1)}, bf16[256,8192]{1,0:T(8,128)(2,1)S(1)}, u32[]{:S(2)}) copy-start(bf16[256,8192]{1,0:T(8,128)(2,1)S(1)} %get-tuple-element.98.dd_ref) | copy-start | bytes 12582916
  44.4 11.7 %collective-permute-start.8 = (f32[15,8,128]{2,1,0:T(8,128)S(1)}, f32[15,8,128]{2,1,0:T(8,128)S(1)}, u32[]{:S(2)}, u32[]{:S(2)}) collective-permute-start(f32[15,8,128]{2,1,0:T(8,128)S(1)} %get-tuple-element.90), channel_id=1, source_target_pairs={{0,16},{16,32},{32,48},{48,64},{64,80},{80,96},{96,112},{112,128},... | collective-permute-start | bytes 184328 | tf_op jit(solution)/shard_map/ppermute | solution.py:497
  44.7 11.4 %collective-permute-start.9 = (f32[15,8,128]{2,1,0:T(8,128)S(1)}, f32[15,8,128]{2,1,0:T(8,128)S(1)}, u32[]{:S(2)}, u32[]{:S(2)}) collective-permute-start(f32[15,8,128]{2,1,0:T(8,128)S(1)} %get-tuple-element.91), channel_id=1, source_target_pairs={{0,240},{16,0},{32,16},{48,32},{64,48},{80,64},{96,80},{112,96},{1... | collective-permute-start | bytes 184328 | tf_op jit(solution)/shard_map/ppermute | solution.py:497
  48.2 2.2 %copy-start.1 = (bf16[256,8192]{1,0:T(8,128)(2,1)S(1)}, bf16[256,8192]{1,0:T(8,128)(2,1)}, u32[]{:S(2)}) copy-start(bf16[256,8192]{1,0:T(8,128)(2,1)} %copy-done) | copy-start | bytes 12582916
  50.4 2.2 %copy-start.3 = (f32[128,8192]{1,0:T(8,128)S(1)}, f32[128,8192]{1,0:T(8,128)}, u32[]{:S(2)}) copy-start(f32[128,8192]{1,0:T(8,128)} %copy-done.2) | copy-start | bytes 12582916
  52.6 3.5 %copy-start.5 = (bf16[256,8192]{1,0:T(8,128)(2,1)S(1)}, bf16[256,8192]{1,0:T(8,128)(2,1)}, u32[]{:S(2)}) copy-start(bf16[256,8192]{1,0:T(8,128)(2,1)} %copy-done.4) | copy-start | bytes 12582916
  52.6 3.5 %copy-start.7 = (bf16[256,8192]{1,0:T(8,128)(2,1)S(1)}, bf16[256,8192]{1,0:T(8,128)(2,1)}, u32[]{:S(2)}) copy-start(bf16[256,8192]{1,0:T(8,128)(2,1)} %copy-done.6) | copy-start | bytes 12582916
  58.4 4.8 %collective-permute-start.10 = (f32[24,128]{1,0:T(8,128)S(1)}, f32[24,128]{1,0:T(8,128)S(1)}, u32[]{:S(2)}, u32[]{:S(2)}) collective-permute-start(f32[24,128]{1,0:T(8,128)S(1)} %slice_select_fusion), channel_id=1, source_target_pairs={{0,16},{1,17},{2,18},{3,19},{4,20},{5,21},{6,22},{7,23},{8,24},{9,... | collective-permute-start | bytes 36872 | tf_op jit(solution)/shard_map/ppermute | solution.py:536
  63.9 11.2 %all-to-all-start = ((f32[16,24,128]{2,1,0:T(8,128)}), f32[16,24,128]{2,1,0:T(8,128)S(1)}, u32[]{:S(2)}, u32[]{:S(2)}) async-start(f32[16,24,128]{2,1,0:T(8,128)} %broadcast_in_dim.4), calls=%async_computation | async-start | bytes 393216 | tf_op jit(solution)/shard_map/all_to_all | solution.py:519
  67.4 7.7 %collective-permute-start.11 = (f32[10,8,128]{2,1,0:T(8,128)S(1)}, f32[10,8,128]{2,1,0:T(8,128)S(1)}, u32[]{:S(2)}, u32[]{:S(2)}) collective-permute-start(f32[10,8,128]{2,1,0:T(8,128)S(1)} %get-tuple-element.104), channel_id=1, source_target_pairs={{0,1},{1,2},{2,3},{3,4},{4,5},{5,6},{6,7},{7,8},{8,9},{9,10},{10,1... | collective-permute-start | bytes 122888 | tf_op jit(solution)/shard_map/ppermute | solution.py:497
  68.7 6.5 %collective-permute-start.12 = (f32[10,8,128]{2,1,0:T(8,128)S(1)}, f32[10,8,128]{2,1,0:T(8,128)S(1)}, u32[]{:S(2)}, u32[]{:S(2)}) collective-permute-start(f32[10,8,128]{2,1,0:T(8,128)S(1)} %get-tuple-element.105), channel_id=1, source_target_pairs={{0,15},{1,0},{2,1},{3,2},{4,3},{5,4},{6,5},{7,6},{8,7},{9,8},{10,9... | collective-permute-start | bytes 122888 | tf_op jit(solution)/shard_map/ppermute | solution.py:497
  87.6 4.2 %collective-permute-start.13 = (f32[24,128]{1,0:T(8,128)S(1)}, f32[24,128]{1,0:T(8,128)S(1)}, u32[]{:S(2)}, u32[]{:S(2)}) collective-permute-start(f32[24,128]{1,0:T(8,128)S(1)} %reduce_sum.19), channel_id=1, source_target_pairs={{0,16},{1,17},{2,18},{3,19},{4,20},{5,21},{6,22},{7,23},{8,24},{9,... | collective-permute-start | bytes 36872 | tf_op jit(solution)/shard_map/ppermute | solution.py:546

commit v4 on v3

--- a/solution.py
+++ b/solution.py
@@ -530,8 +530,8 @@
     return lax.axis_index("sub") % 2 == 0
 
 
-def chip_sum(x):
-    core, low, high = on_first_core(), x[:24], x[24:]
+def chip_sum(x, core):
+    low, high = x[:24], x[24:]
     mine = jnp.where(core, low, high)
     return mine + lax.ppermute(jnp.where(core, high, low), ("sub", "col"), SWAP)
 
@@ -540,8 +540,7 @@
     return send_to_all(x, together((0, 2, 3))).sum(0)
 
 
-def rest_sum(x):
-    core = on_first_core()
+def rest_sum(x, core):
     x = send_to_all(x, together((1, 2, 4))).sum(0)
     other = lax.ppermute(x, ("sub", "col"), SWAP)
     return jnp.where(core, x, other), jnp.where(core, other, x)
@@ -560,6 +559,7 @@
     out_weight,
     out_bias,
 ):
+    core, element_weight = lax.optimization_barrier((on_first_core(), element_weight))
     hot = jax.ShapeDtypeStruct((128, 128), bf16)
     wide = jax.ShapeDtypeStruct((256, 8192), bf16)
     khot = jax.ShapeDtypeStruct((64, 192), bf16)
@@ -641,12 +641,12 @@
     (pay,) = call(grads_body, [(48, 128)], [x1, c1, hh1, dd1, gw, gb], flops=300000000)
     w, yu, yd = in_device(w, rp, rm, 10)
     if grid_is_whole():
-        pay = chip_sum(pay)
+        pay = chip_sum(pay, core)
         pay, yu, yd = lax.optimization_barrier((pay, yu, yd))
         yl, yr = both_ways(yu, yd, "col")
         pay = plane_sum(pay)
         pay, yl, yr = lax.optimization_barrier((pay, yl, yr))
-        terms = list(rest_sum(pay))
+        terms = list(rest_sum(pay, core))
     else:
         yl, yr = both_ways(yu, yd, "col")
         pay = lax.psum(pay, ("sub", "col"))

time: 92.9 us -> 83.3 us (0.90)
  local copies, waits for them, and re-layouts: 13 us -> 0.68 us
  starting transfers between devices: 40 us -> 42.3 us
    unnamed x16 -> x0, local copies, waits for them, and re-layouts: 12.3 us -> none
    ppermute x12, starting transfers between devices: 29.5 us -> 31.6 us  [shift(): return lax.ppermute(x, axis, [(i, (i + step) % n) for i in range(n)])]
    all_to_all x1, waiting for transfers between devices: 1.94 us -> 0.27 us  [send_to_all(): lax.all_to_all(y, ('sub', 'col'), 0, 0, axis_index_groups=groups, tiled=T...]
    ppermute x12, waiting for transfers between devices: 6.11 us -> 7.4 us  [shift(): return lax.ppermute(x, axis, [(i, (i + step) % n) for i in range(n)])]
  transfers between devices with their start and end apart: 15 -> 15, of which waited for: 7 -> 8; matrix products, arithmetic and copies ran while one was open for 0% -> 0% of each run, Pallas kernels for 9% -> 10%
where the time goes in v4:
time: 83.3 us; the launch traced here: 83 us
  starting transfers between devices  42.3 us (51%)
  Pallas kernels  17.5 us (21%)
  blocking collectives  13.4 us (16%)
  waiting for transfers between devices  8.29 us (10%)
    ppermute x12, starting transfers between devices, shift(): return lax.ppermute(x, axis, [(i, (i + step) % n) for i in range(n)])  31.6 us
    pallas_call x12, Pallas kernels, call(): pl.pallas_call(body, out_shape=shapes, in_specs=[pl.BlockSpec(memory_spac...  17.5 us
    all_to_all x1, blocking collectives, send_to_all(): lax.all_to_all(y, ('sub', 'col'), 0, 0, axis_index_groups=groups, tiled=T...  13.4 us
    ppermute x12, waiting for transfers between devices, shift(): return lax.ppermute(x, axis, [(i, (i + step) % n) for i in range(n)])  7.4 us
    all_to_all x1, starting transfers between devices, send_to_all(): lax.all_to_all(y, ('sub', 'col'), 0, 0, axis_index_groups=groups, tiled=T...  3.88 us
    ppermute x1, starting transfers between devices, chip_sum(): return mine + lax.ppermute(jnp.where(core, high, low), ('sub', 'col'), SWAP)  3.68 us
    ppermute x1, starting transfers between devices, rest_sum(): other = lax.ppermute(x, ('sub', 'col'), SWAP)  3.12 us
  transfers between devices with their start and end apart: 15, of which 8 were waited for; matrix products, arithmetic and copies ran while one was open for 0% of the time, Pallas kernels for 10%

profile of v4, /device:TPU:1, one launch (start us, length us, event | category | flops | bytes accessed | tf_op | source)
XLA Modules:
  0.0 83.0 jit_solution(13148927906021270838)
XLA Ops:
  0.6 1.6 %shard_map.179 = (f32[12,48,128]{2,1,0:T(8,128)S(1)}, f32[18,8,128]{2,1,0:T(8,128)S(1)}, f32[18,8,128]{2,1,0:T(8,128)S(1)}, f32[16,128]{1,0:T(8,128)S(1)}, bf16[...) custom-call(f32[5,64,128]{2,1,0:T(8,128)} %s_in.1, f32[5,64,128]{2,1,0:T(8,128)} %c_in.1, s32[1,128]{1,0:T(1,128)} %o_in.1, ...), custom_call_target="tpu_custom_call" | custom-call | bytes 2000000 | tf_op jit(solution)/shard_map/pallas_call | solution.py:482
  2.3 2.8 %collective-permute-start = (f32[18,8,128]{2,1,0:T(8,128)S(1)}, f32[18,8,128]{2,1,0:T(8,128)S(1)}, u32[]{:S(2)}, u32[]{:S(2)}) collective-permute-start(f32[18,8,128]{2,1,0:T(8,128)S(1)} %get-tuple-element.68), channel_id=1, source_target_pairs={{0,16},{16,32},{32,48},{48,64},{64,80},{80,96},{96,112},{112,128},... | collective-permute-start | bytes 221192 | tf_op jit(solution)/shard_map/ppermute | solution.py:497
  5.7 0.8 collective-permute-done.r_1_
  6.4 2.4 %collective-permute-done.1.r_2_ = f32[18,8,128]{2,1,0:T(8,128)S(1)} collective-permute-done((f32[18,8,128]{2,1,0:T(8,128)S(1)}, f32[18,8,128]{2,1,0:T(8,128)S(1)}, u32[]{:S(2)}, u32[]{:S(2)}) %collective-permute-start.1) | collective-permute-done | bytes 73760 | tf_op jit(solution)/shard_map/ppermute | solution.py:497
  9.0 1.6 %collective-permute-start.2 = (f32[11,8,128]{2,1,0:T(8,128)S(1)}, f32[11,8,128]{2,1,0:T(8,128)S(1)}, u32[]{:S(2)}, u32[]{:S(2)}) collective-permute-start(f32[11,8,128]{2,1,0:T(8,128)S(1)} %get-tuple-element.71), channel_id=1, source_target_pairs={{0,1},{1,2},{2,3},{3,4},{4,5},{5,6},{6,7},{7,8},{8,9},{9,10},{10,1... | collective-permute-start | bytes 135176 | tf_op jit(solution)/shard_map/ppermute | solution.py:497
  10.6 7.1 %collective-permute-start.3 = (f32[11,8,128]{2,1,0:T(8,128)S(1)}, f32[11,8,128]{2,1,0:T(8,128)S(1)}, u32[]{:S(2)}, u32[]{:S(2)}) collective-permute-start(f32[11,8,128]{2,1,0:T(8,128)S(1)} %get-tuple-element.72), channel_id=1, source_target_pairs={{0,15},{1,0},{2,1},{3,2},{4,3},{5,4},{6,5},{7,6},{8,7},{9,8},{10,9... | collective-permute-start | bytes 135176 | tf_op jit(solution)/shard_map/ppermute | solution.py:497
  17.7 1.1 %shard_map.181.p_ref = bf16[272,256]{1,0:T(8,128)(2,1)S(1)} custom-call(f32[5,64]{1,0:T(8,128)} %bitcast.10, f32[1,64]{1,0:T(1,128)} %bitcast.13, f32[64,64]{1,0:T(8,128)} %w2_in.1, f32[1,64]{1,0:T(1,128)} %bitcast.14, f32[5,64]{1,0:T(8,128)} %wo_in.1, f32[1,5]{1,0:T(1,128)} %bitcast.15), custom_call_target="tpu_custom_call" | custom-call | flops 2000000 | bytes 2000000 | tf_op jit(solution)/shard_map/pallas_call | solution.py:482
  20.2 1.0 %collective-permute-start.5 = (f32[15,8,128]{2,1,0:T(8,128)S(1)}, f32[15,8,128]{2,1,0:T(8,128)S(1)}, u32[]{:S(2)}, u32[]{:S(2)}) collective-permute-start(f32[15,8,128]{2,1,0:T(8,128)S(1)} %get-tuple-element.79), channel_id=1, source_target_pairs={{0,240},{16,0},{32,16},{48,32},{64,48},{80,64},{96,80},{112,96},{1... | collective-permute-start | bytes 184328 | tf_op jit(solution)/shard_map/ppermute | solution.py:497
  21.9 2.0 %collective-permute-done.5.r_2_ = f32[15,8,128]{2,1,0:T(8,128)S(1)} collective-permute-done((f32[15,8,128]{2,1,0:T(8,128)S(1)}, f32[15,8,128]{2,1,0:T(8,128)S(1)}, u32[]{:S(2)}, u32[]{:S(2)}) %collective-permute-start.5) | collective-permute-done | bytes 61472 | tf_op jit(solution)/shard_map/ppermute | solution.py:497
  24.2 6.2 %collective-permute-start.7 = (f32[10,8,128]{2,1,0:T(8,128)S(1)}, f32[10,8,128]{2,1,0:T(8,128)S(1)}, u32[]{:S(2)}, u32[]{:S(2)}) collective-permute-start(f32[10,8,128]{2,1,0:T(8,128)S(1)} %get-tuple-element.82), channel_id=1, source_target_pairs={{0,15},{1,0},{2,1},{3,2},{4,3},{5,4},{6,5},{7,6},{8,7},{9,8},{10,9... | collective-permute-start | bytes 122888 | tf_op jit(solution)/shard_map/ppermute | solution.py:497
  30.4 2.0 %shard_map.184 = (f32[5,64,128]{2,1,0:T(8,128)S(1)}, f32[512,128]{1,0:T(8,128)S(1)}, bf16[256,8192]{1,0:T(8,128)(2,1)S(1)}, f32[128,8192]{1,0:T(8,128)S(1)}) custom-call(f32[10,64,128]{2,1,0:T(8,128)S(1)} %get-tuple-element.84.sa_ref, bf16[272,256]{1,0:T(8,128)(2,1)S(1)} %shard_map.181.p_ref), custom_call_target="tpu_custom_call" | custom-call | flops 300000000 | bytes 2000000 | tf_op jit(solution)/shard_map/pallas_call | solution.py:482
  32.4 4.1 %shard_map.185 = (f32[10,64,128]{2,1,0:T(8,128)S(1)}, f32[5,64,128]{2,1,0:T(8,128)S(1)}, f32[10,48,128]{2,1,0:T(8,128)S(1)}, f32[15,8,128]{2,1,0:T(8,128)S(1)}, ...) custom-call(f32[10,3,2,8,128]{4,3,2,1,0:T(8,128)S(1)} %get-tuple-ele, ...), custom_call_target="tpu_custom_call" | custom-call | flops 900000000 | bytes 2000000 | tf_op jit(solution)/shard_map/pallas_call | solution.py:482
  36.9 3.9 %collective-permute-start.9 = (f32[15,8,128]{2,1,0:T(8,128)S(1)}, f32[15,8,128]{2,1,0:T(8,128)S(1)}, u32[]{:S(2)}, u32[]{:S(2)}) collective-permute-start(f32[15,8,128]{2,1,0:T(8,128)S(1)} %get-tuple-element.94), channel_id=1, source_target_pairs={{0,240},{16,0},{32,16},{48,32},{64,48},{80,64},{96,80},{112,96},{1... | collective-permute-start | bytes 184328 | tf_op jit(solution)/shard_map/ppermute | solution.py:497
  40.8 3.5 %shard_map.186 = (f32[5,64,128]{2,1,0:T(8,128)S(1)}, f32[384,160]{1,0:T(8,128)S(1)}, f32[8,128]{1,0:T(8,128)S(1)}) custom-call(f32[512,128]{1,0:T(8,128)S(1)} %get-tuple-element.88.x_ref, f32[5,64,128]{2,1,0:T(8,128)S(1)} %get-tuple-element.89.m1_ref, bf16[256,8192]{1,0:T(8,128)(2,1)S(1)} %get-tuple-element.90.hh_ref, ...), custom_call_target="tpu_custom_call" | custom-call | flops 600000000 | bytes 2000000 | tf_op jit(solution)/shard_map/pallas_call | solution.py:482
  44.3 2.2 %shard_map.188 = f32[48,128]{1,0:T(8,128)S(1)} custom-call(f32[512,128]{1,0:T(8,128)S(1)} %get-tuple-element.99.x_ref, f32[512,128]{1,0:T(8,128)S(1)} %get-tuple-element.100.c_ref, bf16[256,8192]{1,0:T(8,128)(2,1)S(1)} %get-tuple-element.101.hh_ref, bf16[256,8192]{1,0:T(8,128)(2,1)S(1)} %get-tuple-element.102.dd_ref, ...), custom_call_target="tpu_custom_call" | custom-call | flops 300000000 | bytes 2000000 | tf_op jit(solution)/shard_map/pallas_call | solution.py:482
  46.6 3.7 %collective-permute-start.10 = (f32[24,128]{1,0:T(8,128)S(1)}, f32[24,128]{1,0:T(8,128)S(1)}, u32[]{:S(2)}, u32[]{:S(2)}) collective-permute-start(f32[24,128]{1,0:T(8,128)S(1)} %slice_select_fusion), channel_id=1, source_target_pairs={{0,16},{1,17},{2,18},{3,19},{4,20},{5,21},{6,22},{7,23},{8,24},{9,... | collective-permute-start | bytes 36872 | tf_op jit(solution)/shard_map/ppermute | solution.py:536
  51.7 3.9 %all-to-all-start = ((f32[16,24,128]{2,1,0:T(8,128)}), f32[16,24,128]{2,1,0:T(8,128)S(1)}, u32[]{:S(2)}, u32[]{:S(2)}) async-start(f32[16,24,128]{2,1,0:T(8,128)} %broadcast_in_dim.4), calls=%async_computation | async-start | bytes 393216 | tf_op jit(solution)/shard_map/all_to_all | solution.py:519
  55.6 1.4 %collective-permute-start.11 = (f32[10,8,128]{2,1,0:T(8,128)S(1)}, f32[10,8,128]{2,1,0:T(8,128)S(1)}, u32[]{:S(2)}, u32[]{:S(2)}) collective-permute-start(f32[10,8,128]{2,1,0:T(8,128)S(1)} %get-tuple-element.108), channel_id=1, source_target_pairs={{0,1},{1,2},{2,3},{3,4},{4,5},{5,6},{6,7},{7,8},{8,9},{9,10},{10,1... | collective-permute-start | bytes 122888 | tf_op jit(solution)/shard_map/ppermute | solution.py:497
  57.0 6.0 %collective-permute-start.12 = (f32[10,8,128]{2,1,0:T(8,128)S(1)}, f32[10,8,128]{2,1,0:T(8,128)S(1)}, u32[]{:S(2)}, u32[]{:S(2)}) collective-permute-start(f32[10,8,128]{2,1,0:T(8,128)S(1)} %get-tuple-element.109), channel_id=1, source_target_pairs={{0,15},{1,0},{2,1},{3,2},{4,3},{5,4},{6,5},{7,6},{8,7},{9,8},{10,9... | collective-permute-start | bytes 122888 | tf_op jit(solution)/shard_map/ppermute | solution.py:497
  63.3 1.3 %collective-permute-done.11.yl_ref = f32[10,8,128]{2,1,0:T(8,128)S(1)} collective-permute-done((f32[10,8,128]{2,1,0:T(8,128)S(1)}, f32[10,8,128]{2,1,0:T(8,128)S(1)}, u32[]{:S(2)}, u32[]{:S(2)}) %collective-permute-start.11) | collective-permute-done | bytes 40992 | tf_op jit(solution)/shard_map/ppermute | solution.py:497
  64.6 13.4 %all_to_all.10 = f32[8,24,128]{2,1,0:T(8,128)S(1)} all-to-all(f32[8,24,128]{2,1,0:T(8,128)S(1)} %broadcast_in_dim.5), channel_id=1, replica_groups={{0,4,8,12,128,132,136,140},{1,5,9,13,129,133,137,141},{2,6,10,14,130,13..., dimensions={0} | all-to-all | bytes 196608 | tf_op jit(solution)/shard_map/all_to_all | solution.py:519
  78.0 3.1 %collective-permute-start.13 = (f32[24,128]{1,0:T(8,128)S(1)}, f32[24,128]{1,0:T(8,128)S(1)}, u32[]{:S(2)}, u32[]{:S(2)}) collective-permute-start(f32[24,128]{1,0:T(8,128)S(1)} %reduce_sum.19), channel_id=1, source_target_pairs={{0,16},{1,17},{2,18},{3,19},{4,20},{5,21},{6,22},{7,23},{8,24},{9,... | collective-permute-start | bytes 36872 | tf_op jit(solution)/shard_map/ppermute | solution.py:545
  81.1 1.1 %shard_map.189 = (f32[5,64,128]{2,1,0:T(8,128)}, f32[5,64,128]{2,1,0:T(8,128)}) custom-call(f32[10,3,2,8,128]{4,3,2,1,0:T(8,128)S(1)} %get-tuple-element.97.w_ref, f32[10,8,128]{2,1,0:T(8,128)S(1)} %collective-permute-done.11.yl_ref, f32[10,8,128]{2,1,0:T(8,128)S(1)} %collective-permute-done.12.yr_ref, f32[16,128]{1,0:T(8,128)S(1)} %get-tuple-element.75.mk_ref, ...), custom_call_target="tpu_custom_call" | custom-call | flops 20000000 | bytes 2000000 | tf_op jit(solution)/shard_map/pallas_call | solution.py:482
  82.3 0.7 shard_map.190
  (26 shorter events, 5.4 us)
Async XLA Ops:
  2.3 4.2 %collective-permute-start = (f32[18,8,128]{2,1,0:T(8,128)S(1)}, f32[18,8,128]{2,1,0:T(8,128)S(1)}, u32[]{:S(2)}, u32[]{:S(2)}) collective-permute-start(f32[18,8,128]{2,1,0:T(8,128)S(1)} %get-tuple-element.68), channel_id=1, source_target_pairs={{0,16},{16,32},{32,48},{48,64},{64,80},{80,96},{96,112},{112,128},... | collective-permute-start | bytes 221192 | tf_op jit(solution)/shard_map/ppermute | solution.py:497
  5.0 3.8 %collective-permute-start.1 = (f32[18,8,128]{2,1,0:T(8,128)S(1)}, f32[18,8,128]{2,1,0:T(8,128)S(1)}, u32[]{:S(2)}, u32[]{:S(2)}) collective-permute-start(f32[18,8,128]{2,1,0:T(8,128)S(1)} %get-tuple-element.69), channel_id=1, source_target_pairs={{0,240},{16,0},{32,16},{48,32},{64,48},{80,64},{96,80},{112,96},{1... | collective-permute-start | bytes 221192 | tf_op jit(solution)/shard_map/ppermute | solution.py:497
  9.0 10.1 %collective-permute-start.2 = (f32[11,8,128]{2,1,0:T(8,128)S(1)}, f32[11,8,128]{2,1,0:T(8,128)S(1)}, u32[]{:S(2)}, u32[]{:S(2)}) collective-permute-start(f32[11,8,128]{2,1,0:T(8,128)S(1)} %get-tuple-element.71), channel_id=1, source_target_pairs={{0,1},{1,2},{2,3},{3,4},{4,5},{5,6},{6,7},{7,8},{8,9},{9,10},{10,1... | collective-permute-start | bytes 135176 | tf_op jit(solution)/shard_map/ppermute | solution.py:497
  10.6 8.5 %collective-permute-start.3 = (f32[11,8,128]{2,1,0:T(8,128)S(1)}, f32[11,8,128]{2,1,0:T(8,128)S(1)}, u32[]{:S(2)}, u32[]{:S(2)}) collective-permute-start(f32[11,8,128]{2,1,0:T(8,128)S(1)} %get-tuple-element.72), channel_id=1, source_target_pairs={{0,15},{1,0},{2,1},{3,2},{4,3},{5,4},{6,5},{7,6},{8,7},{9,8},{10,9... | collective-permute-start | bytes 135176 | tf_op jit(solution)/shard_map/ppermute | solution.py:497
  19.6 2.3 %collective-permute-start.4 = (f32[15,8,128]{2,1,0:T(8,128)S(1)}, f32[15,8,128]{2,1,0:T(8,128)S(1)}, u32[]{:S(2)}, u32[]{:S(2)}) collective-permute-start(f32[15,8,128]{2,1,0:T(8,128)S(1)} %get-tuple-element.78), channel_id=1, source_target_pairs={{0,16},{16,32},{32,48},{48,64},{64,80},{80,96},{96,112},{112,128},... | collective-permute-start | bytes 184328 | tf_op jit(solution)/shard_map/ppermute | solution.py:497
  20.2 3.6 %collective-permute-start.5 = (f32[15,8,128]{2,1,0:T(8,128)S(1)}, f32[15,8,128]{2,1,0:T(8,128)S(1)}, u32[]{:S(2)}, u32[]{:S(2)}) collective-permute-start(f32[15,8,128]{2,1,0:T(8,128)S(1)} %get-tuple-element.79), channel_id=1, source_target_pairs={{0,240},{16,0},{32,16},{48,32},{64,48},{80,64},{96,80},{112,96},{1... | collective-permute-start | bytes 184328 | tf_op jit(solution)/shard_map/ppermute | solution.py:497
  24.1 8.3 %collective-permute-start.6 = (f32[10,8,128]{2,1,0:T(8,128)S(1)}, f32[10,8,128]{2,1,0:T(8,128)S(1)}, u32[]{:S(2)}, u32[]{:S(2)}) collective-permute-start(f32[10,8,128]{2,1,0:T(8,128)S(1)} %get-tuple-element.81), channel_id=1, source_target_pairs={{0,1},{1,2},{2,3},{3,4},{4,5},{5,6},{6,7},{7,8},{8,9},{9,10},{10,1... | collective-permute-start | bytes 122888 | tf_op jit(solution)/shard_map/ppermute | solution.py:497
  24.2 8.2 %collective-permute-start.7 = (f32[10,8,128]{2,1,0:T(8,128)S(1)}, f32[10,8,128]{2,1,0:T(8,128)S(1)}, u32[]{:S(2)}, u32[]{:S(2)}) collective-permute-start(f32[10,8,128]{2,1,0:T(8,128)S(1)} %get-tuple-element.82), channel_id=1, source_target_pairs={{0,15},{1,0},{2,1},{3,2},{4,3},{5,4},{6,5},{7,6},{8,7},{9,8},{10,9... | collective-permute-start | bytes 122888 | tf_op jit(solution)/shard_map/ppermute | solution.py:497
  36.5 7.8 %collective-permute-start.8 = (f32[15,8,128]{2,1,0:T(8,128)S(1)}, f32[15,8,128]{2,1,0:T(8,128)S(1)}, u32[]{:S(2)}, u32[]{:S(2)}) collective-permute-start(f32[15,8,128]{2,1,0:T(8,128)S(1)} %get-tuple-element.93), channel_id=1, source_target_pairs={{0,16},{16,32},{32,48},{48,64},{64,80},{80,96},{96,112},{112,128},... | collective-permute-start | bytes 184328 | tf_op jit(solution)/shard_map/ppermute | solution.py:497
  36.9 7.5 %collective-permute-start.9 = (f32[15,8,128]{2,1,0:T(8,128)S(1)}, f32[15,8,128]{2,1,0:T(8,128)S(1)}, u32[]{:S(2)}, u32[]{:S(2)}) collective-permute-start(f32[15,8,128]{2,1,0:T(8,128)S(1)} %get-tuple-element.94), channel_id=1, source_target_pairs={{0,240},{16,0},{32,16},{48,32},{64,48},{80,64},{96,80},{112,96},{1... | collective-permute-start | bytes 184328 | tf_op jit(solution)/shard_map/ppermute | solution.py:497
  46.6 4.5 %collective-permute-start.10 = (f32[24,128]{1,0:T(8,128)S(1)}, f32[24,128]{1,0:T(8,128)S(1)}, u32[]{:S(2)}, u32[]{:S(2)}) collective-permute-start(f32[24,128]{1,0:T(8,128)S(1)} %slice_select_fusion), channel_id=1, source_target_pairs={{0,16},{1,17},{2,18},{3,19},{4,20},{5,21},{6,22},{7,23},{8,24},{9,... | collective-permute-start | bytes 36872 | tf_op jit(solution)/shard_map/ppermute | solution.py:536
  51.7 11.5 %all-to-all-start = ((f32[16,24,128]{2,1,0:T(8,128)}), f32[16,24,128]{2,1,0:T(8,128)S(1)}, u32[]{:S(2)}, u32[]{:S(2)}) async-start(f32[16,24,128]{2,1,0:T(8,128)} %broadcast_in_dim.4), calls=%async_computation | async-start | bytes 393216 | tf_op jit(solution)/shard_map/all_to_all | solution.py:519
  55.6 9.0 %collective-permute-start.11 = (f32[10,8,128]{2,1,0:T(8,128)S(1)}, f32[10,8,128]{2,1,0:T(8,128)S(1)}, u32[]{:S(2)}, u32[]{:S(2)}) collective-permute-start(f32[10,8,128]{2,1,0:T(8,128)S(1)} %get-tuple-element.108), channel_id=1, source_target_pairs={{0,1},{1,2},{2,3},{3,4},{4,5},{5,6},{6,7},{7,8},{8,9},{9,10},{10,1... | collective-permute-start | bytes 122888 | tf_op jit(solution)/shard_map/ppermute | solution.py:497
  57.0 7.6 %collective-permute-start.12 = (f32[10,8,128]{2,1,0:T(8,128)S(1)}, f32[10,8,128]{2,1,0:T(8,128)S(1)}, u32[]{:S(2)}, u32[]{:S(2)}) collective-permute-start(f32[10,8,128]{2,1,0:T(8,128)S(1)} %get-tuple-element.109), channel_id=1, source_target_pairs={{0,15},{1,0},{2,1},{3,2},{4,3},{5,4},{6,5},{7,6},{8,7},{9,8},{10,9... | collective-permute-start | bytes 122888 | tf_op jit(solution)/shard_map/ppermute | solution.py:497
  78.0 4.2 %collective-permute-start.13 = (f32[24,128]{1,0:T(8,128)S(1)}, f32[24,128]{1,0:T(8,128)S(1)}, u32[]{:S(2)}, u32[]{:S(2)}) collective-permute-start(f32[24,128]{1,0:T(8,128)S(1)} %reduce_sum.19), channel_id=1, source_target_pairs={{0,16},{1,17},{2,18},{3,19},{4,20},{5,21},{6,22},{7,23},{8,24},{9,... | collective-permute-start | bytes 36872 | tf_op jit(solution)/shard_map/ppermute | solution.py:545

commit v5 on v4

--- a/solution.py
+++ b/solution.py
@@ -281,12 +281,12 @@
     return lax.dot_general(a, b, (((1,), (1,)), ((), ())), preferred_element_type=f32)
 
 
-def load8(ref, n0):
-    return jnp.concatenate([ref[pl.ds(n0 + i, 8, stride=64), :] for i in range(CH)], axis=1)
+def load8(ref, n0, ch=CH):
+    return jnp.concatenate([ref[pl.ds(n0 + i, 8, stride=64), :] for i in range(ch)], axis=1)
 
 
 def store8(ref, n0, x):
-    for i in range(CH):
+    for i in range(x.shape[1] // 128):
         ref[pl.ds(n0 + i, 8, stride=64), :] = x[:, i * 128 : (i + 1) * 128]
 
 
@@ -352,7 +352,7 @@
     gw, gb = acc
     right = jnp.concatenate([h1, stack2(x8), stack2(c8)], axis=0)
     gw = gw + nt(jnp.concatenate([d2, d1, h2], axis=0), right)
-    for i in range(CH):
+    for i in range(c8.shape[1] // 128):
         gb = gb + c8[:, i * 128 : (i + 1) * 128]
     return gw, gb
 
@@ -402,31 +402,21 @@
     put_fields(c_ref, m1_ref[...], False)
     w = weights(p_ref)
 
-    def chunk(i, acc):
-        n0 = i * CH
-        at = lanes_of(i)
-        c8 = load8(c_ref, n0)
-        back, d2h, d2l, d1h, d1l = backward(c8, t_ref[0:64, at], t_ref[64:128, at], w)
-        store8(b_ref, n0, back)
-        return add_grads(
-            acc, load8(x_ref, n0), c8, hh_ref[0:128, at], hh_ref[128:256, at],
-            jnp.concatenate([d2h, d2l], axis=0), jnp.concatenate([d1h, d1l], axis=0),
-        )
-
-    gw_ref[...], gb_ref[...] = lax.fori_loop(0, 64 // CH, chunk, no_grads())
+    c8 = load8(c_ref, 0, 64)
+    back, d2h, d2l, d1h, d1l = backward(c8, t_ref[0:64], t_ref[64:128], w)
+    store8(b_ref, 0, back)
+    gw_ref[...], gb_ref[...] = add_grads(
+        no_grads(), load8(x_ref, 0, 64), c8, hh_ref[0:128], hh_ref[128:256],
+        jnp.concatenate([d2h, d2l], axis=0), jnp.concatenate([d1h, d1l], axis=0),
+    )
     back_ref[...] = b_ref[0 : F * 64].reshape(F, 64, 128)
 
 
 def grads_body(x_ref, c_ref, hh_ref, dd_ref, gw_ref, gb_ref, pay_ref):
-    def chunk(i, acc):
-        n0 = i * CH
-        at = lanes_of(i)
-        return add_grads(
-            acc, load8(x_ref, n0), load8(c_ref, n0),
-            hh_ref[0:128, at], hh_ref[128:256, at], dd_ref[0:128, at], dd_ref[128:256, at],
-        )
-
-    g, gb = lax.fori_loop(0, 64 // CH, chunk, (gw_ref[...], gb_ref[...]))
+    g, gb = add_grads(
+        (gw_ref[...], gb_ref[...]), load8(x_ref, 0, 64), load8(c_ref, 0, 64),
+        hh_ref[0:128], hh_ref[128:256], dd_ref[0:128], dd_ref[128:256],
+    )
 
     def fold(t):
         return t + pltpu.roll(t, 64, 1)
@@ -497,8 +487,13 @@
     return lax.ppermute(x, axis, [(i, (i + step) % n) for i in range(n)])
 
 
-def both_ways(up, dn, axis):
-    return shift(up, axis, 1), shift(dn, axis, -1)
+def both_ways(up, dn, axis, even):
+    n = lax.axis_size(axis)
+    in_pair = lax.ppermute(jnp.where(even, up, dn), axis, [(i, i ^ 1) for i in range(n)])
+    across = lax.ppermute(
+        jnp.where(even, dn, up), axis, [(i, (i + 1 if i % 2 else i - 1) % n) for i in range(n)]
+    )
+    return jnp.where(even, across, in_pair), jnp.where(even, in_pair, across)
 
 
 def place(d):
@@ -526,8 +521,8 @@
     return (lax.axis_size("sub"), lax.axis_size("col")) == (16, 16)
 
 
-def on_first_core():
-    return lax.axis_index("sub") % 2 == 0
+def even_at(axis):
+    return lax.axis_index(axis) % 2 == 0
 
 
 def chip_sum(x, core):
@@ -559,7 +554,8 @@
     out_weight,
     out_bias,
 ):
-    core, element_weight = lax.optimization_barrier((on_first_core(), element_weight))
+    flags = (even_at("sub"), even_at("col"), element_weight)
+    even_s, even_c, element_weight = lax.optimization_barrier(flags)
     hot = jax.ShapeDtypeStruct((128, 128), bf16)
     wide = jax.ShapeDtypeStruct((256, 8192), bf16)
     khot = jax.ShapeDtypeStruct((64, 192), bf16)
@@ -571,8 +567,8 @@
         )
 
     def faces(w, up, dn, n):
-        w, yu, yd = in_device(w, *both_ways(up, dn, "sub"), n)
-        yl, yr = both_ways(yu, yd, "col")
+        w, yu, yd = in_device(w, *both_ways(up, dn, "sub", even_s), n)
+        yl, yr = both_ways(yu, yd, "col", even_c)
         return w, yl, yr
 
     w, up, dn, mk, g, kmat = call(
@@ -636,27 +632,33 @@
         [(512, 128)] * 2,
         flops=600000000,
     )
-    rp, rm = both_ways(up, dn, "sub")
+    rp, rm = both_ways(up, dn, "sub", even_s)
     gw, rp, rm = lax.optimization_barrier((gw, rp, rm))
     (pay,) = call(grads_body, [(48, 128)], [x1, c1, hh1, dd1, gw, gb], flops=300000000)
     w, yu, yd = in_device(w, rp, rm, 10)
     if grid_is_whole():
-        pay = chip_sum(pay, core)
+        pay = chip_sum(pay, even_s)
         pay, yu, yd = lax.optimization_barrier((pay, yu, yd))
-        yl, yr = both_ways(yu, yd, "col")
+        yl, yr = both_ways(yu, yd, "col", even_c)
+        out_state, out_adj = call(
+            finish_body,
+            [(F, 64, 128), (F, 64, 128)],
+            [w, yl, yr, mk, im, part, back, g],
+            flops=20000000,
+        )
         pay = plane_sum(pay)
-        pay, yl, yr = lax.optimization_barrier((pay, yl, yr))
-        terms = list(rest_sum(pay, core))
+        pay, out_state, out_adj = lax.optimization_barrier((pay, out_state, out_adj))
+        terms = list(rest_sum(pay, even_s))
     else:
-        yl, yr = both_ways(yu, yd, "col")
+        yl, yr = both_ways(yu, yd, "col", even_c)
         pay = lax.psum(pay, ("sub", "col"))
+        out_state, out_adj = call(
+            finish_body,
+            [(F, 64, 128), (F, 64, 128)],
+            [w, yl, yr, mk, im, part, back, g],
+            flops=20000000,
+        )
         terms = [pay[:24], pay[24:]]
-    out_state, out_adj = call(
-        finish_body,
-        [(F, 64, 128), (F, 64, 128)],
-        [w, yl, yr, mk, im, part, back, g],
-        flops=20000000,
-    )
     gw1, gb1, gw2, gb2, gwo, gbo = call(
         output_body, [(5, 64), (1, 64), (64, 64), (1, 64), (5, 64), (1, 5)], terms
     )

time: 83.3 us -> 82 us (0.984)
  waiting for transfers between devices: 8.29 us -> 15.8 us
  starting transfers between devices: 42.3 us -> 37.8 us
  blocking collectives: 13.4 us -> 9.29 us
    all_to_all x1, waiting for transfers between devices: 0.27 us -> 6.28 us  [send_to_all(): lax.all_to_all(y, ('sub', 'col'), 0, 0, axis_index_groups=groups, tiled=T...]
    all_to_all x1, blocking collectives: 13.4 us -> 9.29 us  [send_to_all(): lax.all_to_all(y, ('sub', 'col'), 0, 0, axis_index_groups=groups, tiled=T...]
    ppermute x12, starting transfers between devices: 31.6 us -> 28.7 us  [the longest x6 19.1 us: both_ways(): lax.ppermute(jnp.where(even, dn, up), axis, [(i, (i + 1 if i % 2 else i -...]
    ppermute x1, starting transfers between devices: 3.68 us -> 2.48 us  [chip_sum(): return mine + lax.ppermute(jnp.where(core, high, low), ('sub', 'col'), SWAP)]
  transfers between devices with their start and end apart: 15 -> 15, of which waited for: 8 -> 9; matrix products, arithmetic and copies ran while one was open for 0% -> 1% of each run, Pallas kernels for 10% -> 9%
where the time goes in v5:
time: 82 us; the launch traced here: 81.7 us
  starting transfers between devices  37.8 us (46%)
  Pallas kernels  17.1 us (21%)
  waiting for transfers between devices  15.8 us (19%)
  blocking collectives  9.29 us (11%)
  between operations  0.91 us (1%)
    ppermute x6, starting transfers between devices, both_ways(): lax.ppermute(jnp.where(even, dn, up), axis, [(i, (i + 1 if i % 2 else i -...  19.1 us
    pallas_call x12, Pallas kernels, call(): pl.pallas_call(body, out_shape=shapes, in_specs=[pl.BlockSpec(memory_spac...  17.1 us
    ppermute x6, starting transfers between devices, both_ways(): lax.ppermute(jnp.where(even, up, dn), axis, [(i, i ^ 1) for i in range(n)])  9.64 us
    all_to_all x1, blocking collectives, send_to_all(): lax.all_to_all(y, ('sub', 'col'), 0, 0, axis_index_groups=groups, tiled=T...  9.29 us
    all_to_all x1, waiting for transfers between devices, send_to_all(): lax.all_to_all(y, ('sub', 'col'), 0, 0, axis_index_groups=groups, tiled=T...  6.28 us
    ppermute x6, waiting for transfers between devices, both_ways(): lax.ppermute(jnp.where(even, dn, up), axis, [(i, (i + 1 if i % 2 else i -...  6.24 us
    all_to_all x1, starting transfers between devices, send_to_all(): lax.all_to_all(y, ('sub', 'col'), 0, 0, axis_index_groups=groups, tiled=T...  3.52 us
    ppermute x1, starting transfers between devices, rest_sum(): other = lax.ppermute(x, ('sub', 'col'), SWAP)  3.07 us
  transfers between devices with their start and end apart: 15, of which 9 were waited for; matrix products, arithmetic and copies ran while one was open for 1% of the time, Pallas kernels for 9%

profile of v5, /device:TPU:1, one launch (start us, length us, event | category | flops | bytes accessed | tf_op | source)
XLA Modules:
  0.0 81.7 jit_solution(7757161605299713480)
XLA Ops:
  0.7 1.6 %shard_map.179 = (f32[12,48,128]{2,1,0:T(8,128)S(1)}, f32[18,8,128]{2,1,0:T(8,128)S(1)}, f32[18,8,128]{2,1,0:T(8,128)S(1)}, f32[16,128]{1,0:T(8,128)S(1)}, bf16[...) custom-call(f32[5,64,128]{2,1,0:T(8,128)} %s_in.1, f32[5,64,128]{2,1,0:T(8,128)} %c_in.1, s32[1,128]{1,0:T(1,128)} %o_in.1, ...), custom_call_target="tpu_custom_call" | custom-call | bytes 2000000 | tf_op jit(solution)/shard_map/pallas_call | solution.py:472
  2.3 3.3 %collective-permute-start.1 = (f32[18,8,128]{2,1,0:T(8,128)S(1)}, f32[18,8,128]{2,1,0:T(8,128)S(1)}, u32[]{:S(2)}, u32[]{:S(2)}) collective-permute-start(f32[18,8,128]{2,1,0:T(8,128)S(1)} %get-tuple-element.128), channel_id=1, source_target_pairs={{0,16},{16,0},{32,48},{48,32},{64,80},{80,64},{96,112},{112,96},{1... | collective-permute-start | bytes 221192 | tf_op jit(solution)/shard_map/ppermute | solution.py:492
  5.6 0.9 %collective-permute-done.1 = f32[18,8,128]{2,1,0:T(8,128)S(1)} collective-permute-done((f32[18,8,128]{2,1,0:T(8,128)S(1)}, f32[18,8,128]{2,1,0:T(8,128)S(1)}, u32[]{:S(2)}, u32[]{:S(2)}) %collective-permute-start.1) | collective-permute-done | bytes 73760 | tf_op jit(solution)/shard_map/ppermute | solution.py:492
  6.5 2.9 %collective-permute-done = f32[18,8,128]{2,1,0:T(8,128)S(1)} collective-permute-done((f32[18,8,128]{2,1,0:T(8,128)S(1)}, f32[18,8,128]{2,1,0:T(8,128)S(1)}, u32[]{:S(2)}, u32[]{:S(2)}) %collective-permute-start) | collective-permute-done | bytes 73760 | tf_op jit(solution)/shard_map/ppermute | solution.py:493
  9.8 7.0 %collective-permute-start.2 = (f32[11,8,128]{2,1,0:T(8,128)S(1)}, f32[11,8,128]{2,1,0:T(8,128)S(1)}, u32[]{:S(2)}, u32[]{:S(2)}) collective-permute-start(f32[11,8,128]{2,1,0:T(8,128)S(1)} %get-tuple-element.141), channel_id=1, source_target_pairs={{0,15},{1,2},{2,1},{3,4},{4,3},{5,6},{6,5},{7,8},{8,7},{9,10},{10,... | collective-permute-start | bytes 135176 | tf_op jit(solution)/shard_map/ppermute | solution.py:493
  16.8 1.1 %shard_map.181.p_ref = bf16[272,256]{1,0:T(8,128)(2,1)S(1)} custom-call(f32[5,64]{1,0:T(8,128)} %bitcast.10, f32[1,64]{1,0:T(1,128)} %bitcast.13, f32[64,64]{1,0:T(8,128)} %w2_in.1, f32[1,64]{1,0:T(1,128)} %bitcast.14, f32[5,64]{1,0:T(8,128)} %wo_in.1, f32[1,5]{1,0:T(1,128)} %bitcast.15), custom_call_target="tpu_custom_call" | custom-call | flops 2000000 | bytes 2000000 | tf_op jit(solution)/shard_map/pallas_call | solution.py:472
  18.8 3.4 %collective-permute-start.5 = (f32[15,8,128]{2,1,0:T(8,128)S(1)}, f32[15,8,128]{2,1,0:T(8,128)S(1)}, u32[]{:S(2)}, u32[]{:S(2)}) collective-permute-start(f32[15,8,128]{2,1,0:T(8,128)S(1)} %get-tuple-element.136), channel_id=1, source_target_pairs={{0,16},{16,0},{32,48},{48,32},{64,80},{80,64},{96,112},{112,96},{1... | collective-permute-start | bytes 184328 | tf_op jit(solution)/shard_map/ppermute | solution.py:492
  22.2 0.9 %collective-permute-done.5 = f32[15,8,128]{2,1,0:T(8,128)S(1)} collective-permute-done((f32[15,8,128]{2,1,0:T(8,128)S(1)}, f32[15,8,128]{2,1,0:T(8,128)S(1)}, u32[]{:S(2)}, u32[]{:S(2)}) %collective-permute-start.5) | collective-permute-done | bytes 61472 | tf_op jit(solution)/shard_map/ppermute | solution.py:492
  23.1 2.7 %collective-permute-done.4 = f32[15,8,128]{2,1,0:T(8,128)S(1)} collective-permute-done((f32[15,8,128]{2,1,0:T(8,128)S(1)}, f32[15,8,128]{2,1,0:T(8,128)S(1)}, u32[]{:S(2)}, u32[]{:S(2)}) %collective-permute-start.4) | collective-permute-done | bytes 61472 | tf_op jit(solution)/shard_map/ppermute | solution.py:493
  26.2 6.0 %collective-permute-start.6 = (f32[10,8,128]{2,1,0:T(8,128)S(1)}, f32[10,8,128]{2,1,0:T(8,128)S(1)}, u32[]{:S(2)}, u32[]{:S(2)}) collective-permute-start(f32[10,8,128]{2,1,0:T(8,128)S(1)} %get-tuple-element.149), channel_id=1, source_target_pairs={{0,15},{1,2},{2,1},{3,4},{4,3},{5,6},{6,5},{7,8},{8,7},{9,10},{10,... | collective-permute-start | bytes 122888 | tf_op jit(solution)/shard_map/ppermute | solution.py:493
  32.2 2.0 %shard_map.184 = (f32[5,64,128]{2,1,0:T(8,128)S(1)}, f32[512,128]{1,0:T(8,128)S(1)}, bf16[256,8192]{1,0:T(8,128)(2,1)S(1)}, f32[128,8192]{1,0:T(8,128)S(1)}) custom-call(f32[10,64,128]{2,1,0:T(8,128)S(1)} %get-tuple-element.87.sa_ref, bf16[272,256]{1,0:T(8,128)(2,1)S(1)} %shard_map.181.p_ref), custom_call_target="tpu_custom_call" | custom-call | flops 300000000 | bytes 2000000 | tf_op jit(solution)/shard_map/pallas_call | solution.py:472
  34.3 4.1 %shard_map.185 = (f32[10,64,128]{2,1,0:T(8,128)S(1)}, f32[5,64,128]{2,1,0:T(8,128)S(1)}, f32[10,48,128]{2,1,0:T(8,128)S(1)}, f32[15,8,128]{2,1,0:T(8,128)S(1)}, ...) custom-call(f32[10,3,2,8,128]{4,3,2,1,0:T(8,128)S(1)} %get-tuple-ele, ...), custom_call_target="tpu_custom_call" | custom-call | flops 900000000 | bytes 2000000 | tf_op jit(solution)/shard_map/pallas_call | solution.py:472
  38.4 2.6 %collective-permute-start.9 = (f32[15,8,128]{2,1,0:T(8,128)S(1)}, f32[15,8,128]{2,1,0:T(8,128)S(1)}, u32[]{:S(2)}, u32[]{:S(2)}) collective-permute-start(f32[15,8,128]{2,1,0:T(8,128)S(1)} %get-tuple-element.132), channel_id=1, source_target_pairs={{0,16},{16,0},{32,48},{48,32},{64,80},{80,64},{96,112},{112,96},{1... | collective-permute-start | bytes 184328 | tf_op jit(solution)/shard_map/ppermute | solution.py:492
  41.0 3.4 %shard_map.186 = (f32[5,64,128]{2,1,0:T(8,128)S(1)}, f32[384,160]{1,0:T(8,128)S(1)}, f32[8,128]{1,0:T(8,128)S(1)}) custom-call(f32[512,128]{1,0:T(8,128)S(1)} %get-tuple-element.94.x_ref, f32[5,64,128]{2,1,0:T(8,128)S(1)} %get-tuple-element.95.m1_ref, bf16[256,8192]{1,0:T(8,128)(2,1)S(1)} %get-tuple-element.96.hh_ref, ...), custom_call_target="tpu_custom_call" | custom-call | flops 600000000 | bytes 2000000 | tf_op jit(solution)/shard_map/pallas_call | solution.py:472
  44.7 2.0 %shard_map.187 = f32[48,128]{1,0:T(8,128)S(1)} custom-call(f32[512,128]{1,0:T(8,128)S(1)} %get-tuple-element.90.x_ref, f32[512,128]{1,0:T(8,128)S(1)} %get-tuple-element.91.c_ref, bf16[256,8192]{1,0:T(8,128)(2,1)S(1)} %get-tuple-element.92.hh_ref, bf16[256,8192]{1,0:T(8,128)(2,1)S(1)} %get-tuple-element.93.dd_ref, f32[384,160]{1,0:T(8,128)S(1)} %get-tuple-element.101.gw_ref, ...), custom_call_target="tpu_custom_call" | custom-call | flops 300000000 | bytes 2000000 | tf_op jit(solution)/shard_map/pallas_call | solution.py:472
  46.6 2.5 %collective-permute-start.10 = (f32[24,128]{1,0:T(8,128)S(1)}, f32[24,128]{1,0:T(8,128)S(1)}, u32[]{:S(2)}, u32[]{:S(2)}) collective-permute-start(f32[24,128]{1,0:T(8,128)S(1)} %slice_select_fusion), channel_id=1, source_target_pairs={{0,16},{1,17},{2,18},{3,19},{4,20},{5,21},{6,22},{7,23},{8,24},{9,... | collective-permute-start | bytes 36872 | tf_op jit(solution)/shard_map/ppermute | solution.py:531
  50.1 6.0 %collective-permute-start.11 = (f32[10,8,128]{2,1,0:T(8,128)S(1)}, f32[10,8,128]{2,1,0:T(8,128)S(1)}, u32[]{:S(2)}, u32[]{:S(2)}) collective-permute-start(f32[10,8,128]{2,1,0:T(8,128)S(1)} %get-tuple-element.145), channel_id=1, source_target_pairs={{0,15},{1,2},{2,1},{3,4},{4,3},{5,6},{6,5},{7,8},{8,7},{9,10},{10,... | collective-permute-start | bytes 122888 | tf_op jit(solution)/shard_map/ppermute | solution.py:493
  56.8 3.5 %all-to-all-start = ((f32[16,24,128]{2,1,0:T(8,128)}), f32[16,24,128]{2,1,0:T(8,128)S(1)}, u32[]{:S(2)}, u32[]{:S(2)}) async-start(f32[16,24,128]{2,1,0:T(8,128)} %broadcast_in_dim.4), calls=%async_computation | async-start | bytes 393216 | tf_op jit(solution)/shard_map/all_to_all | solution.py:514
  60.3 1.1 %shard_map.189 = (f32[5,64,128]{2,1,0:T(8,128)}, f32[5,64,128]{2,1,0:T(8,128)}) custom-call(f32[10,3,2,8,128]{4,3,2,1,0:T(8,128)S(1)} %get-tuple-element.109.w_ref, f32[10,8,128]{2,1,0:T(8,128)S(1)} %get-tuple-element.143.yl_ref, f32[10,8,128]{2,1,0:T(8,128)S(1)} %get-tuple-element.142.yr_ref, f32[16,128]{1,0:T(8,128)S(1)} %get-tuple-element.78.mk_ref, ...), custom_call_target="tpu_custom_call" | custom-call | flops 20000000 | bytes 2000000 | tf_op jit(solution)/shard_map/pallas_call | solution.py:472
  61.5 6.3 %all-to-all-done = f32[16,24,128]{2,1,0:T(8,128)S(1)} async-done(((f32[16,24,128]{2,1,0:T(8,128)}), f32[16,24,128]{2,1,0:T(8,128)S(1)}, u32[]{:S(2)}, u32[]{:S(2)}) %all-to-all-start) | async-done | bytes 196640 | tf_op jit(solution)/shard_map/all_to_all | solution.py:514
  67.8 9.3 %all_to_all.10 = f32[8,24,128]{2,1,0:T(8,128)S(1)} all-to-all(f32[8,24,128]{2,1,0:T(8,128)S(1)} %broadcast_in_dim.5), channel_id=1, replica_groups={{0,4,8,12,128,132,136,140},{1,5,9,13,129,133,137,141},{2,6,10,14,130,13..., dimensions={0} | all-to-all | bytes 196608 | tf_op jit(solution)/shard_map/all_to_all | solution.py:514
  77.1 3.1 %collective-permute-start.13 = (f32[24,128]{1,0:T(8,128)S(1)}, f32[24,128]{1,0:T(8,128)S(1)}, u32[]{:S(2)}, u32[]{:S(2)}) collective-permute-start(f32[24,128]{1,0:T(8,128)S(1)} %reduce_sum.19), channel_id=1, source_target_pairs={{0,16},{1,17},{2,18},{3,19},{4,20},{5,21},{6,22},{7,23},{8,24},{9,... | collective-permute-start | bytes 36872 | tf_op jit(solution)/shard_map/ppermute | solution.py:540
  80.2 0.8 %collective-permute-done.13 = f32[24,128]{1,0:T(8,128)S(1)} collective-permute-done((f32[24,128]{1,0:T(8,128)S(1)}, f32[24,128]{1,0:T(8,128)S(1)}, u32[]{:S(2)}, u32[]{:S(2)}) %collective-permute-start.13) | collective-permute-done | bytes 12320 | tf_op jit(solution)/shard_map/ppermute | solution.py:540
  81.0 0.7 shard_map.190
  (38 shorter events, 3.6 us)
Async XLA Ops:
  2.3 4.2 %collective-permute-start.1 = (f32[18,8,128]{2,1,0:T(8,128)S(1)}, f32[18,8,128]{2,1,0:T(8,128)S(1)}, u32[]{:S(2)}, u32[]{:S(2)}) collective-permute-start(f32[18,8,128]{2,1,0:T(8,128)S(1)} %get-tuple-element.128), channel_id=1, source_target_pairs={{0,16},{16,0},{32,48},{48,32},{64,80},{80,64},{96,112},{112,96},{1... | collective-permute-start | bytes 221192 | tf_op jit(solution)/shard_map/ppermute | solution.py:492
  5.6 3.8 %collective-permute-start = (f32[18,8,128]{2,1,0:T(8,128)S(1)}, f32[18,8,128]{2,1,0:T(8,128)S(1)}, u32[]{:S(2)}, u32[]{:S(2)}) collective-permute-start(f32[18,8,128]{2,1,0:T(8,128)S(1)} %get-tuple-element.129), channel_id=1, source_target_pairs={{0,240},{16,32},{32,16},{48,64},{64,48},{80,96},{96,80},{112,128},... | collective-permute-start | bytes 221192 | tf_op jit(solution)/shard_map/ppermute | solution.py:493
  9.7 8.2 %collective-permute-start.3 = (f32[11,8,128]{2,1,0:T(8,128)S(1)}, f32[11,8,128]{2,1,0:T(8,128)S(1)}, u32[]{:S(2)}, u32[]{:S(2)}) collective-permute-start(f32[11,8,128]{2,1,0:T(8,128)S(1)} %get-tuple-element.140), channel_id=1, source_target_pairs={{0,1},{1,0},{2,3},{3,2},{4,5},{5,4},{6,7},{7,6},{8,9},{9,8},{10,11... | collective-permute-start | bytes 135176 | tf_op jit(solution)/shard_map/ppermute | solution.py:492
  9.8 8.5 %collective-permute-start.2 = (f32[11,8,128]{2,1,0:T(8,128)S(1)}, f32[11,8,128]{2,1,0:T(8,128)S(1)}, u32[]{:S(2)}, u32[]{:S(2)}) collective-permute-start(f32[11,8,128]{2,1,0:T(8,128)S(1)} %get-tuple-element.141), channel_id=1, source_target_pairs={{0,15},{1,2},{2,1},{3,4},{4,3},{5,6},{6,5},{7,8},{8,7},{9,10},{10,... | collective-permute-start | bytes 135176 | tf_op jit(solution)/shard_map/ppermute | solution.py:493
  18.8 4.3 %collective-permute-start.5 = (f32[15,8,128]{2,1,0:T(8,128)S(1)}, f32[15,8,128]{2,1,0:T(8,128)S(1)}, u32[]{:S(2)}, u32[]{:S(2)}) collective-permute-start(f32[15,8,128]{2,1,0:T(8,128)S(1)} %get-tuple-element.136), channel_id=1, source_target_pairs={{0,16},{16,0},{32,48},{48,32},{64,80},{80,64},{96,112},{112,96},{1... | collective-permute-start | bytes 184328 | tf_op jit(solution)/shard_map/ppermute | solution.py:492
  22.2 3.6 %collective-permute-start.4 = (f32[15,8,128]{2,1,0:T(8,128)S(1)}, f32[15,8,128]{2,1,0:T(8,128)S(1)}, u32[]{:S(2)}, u32[]{:S(2)}) collective-permute-start(f32[15,8,128]{2,1,0:T(8,128)S(1)} %get-tuple-element.137), channel_id=1, source_target_pairs={{0,240},{16,32},{32,16},{48,64},{64,48},{80,96},{96,80},{112,128},... | collective-permute-start | bytes 184328 | tf_op jit(solution)/shard_map/ppermute | solution.py:493
  26.1 8.1 %collective-permute-start.7 = (f32[10,8,128]{2,1,0:T(8,128)S(1)}, f32[10,8,128]{2,1,0:T(8,128)S(1)}, u32[]{:S(2)}, u32[]{:S(2)}) collective-permute-start(f32[10,8,128]{2,1,0:T(8,128)S(1)} %get-tuple-element.148), channel_id=1, source_target_pairs={{0,1},{1,0},{2,3},{3,2},{4,5},{5,4},{6,7},{7,6},{8,9},{9,8},{10,11... | collective-permute-start | bytes 122888 | tf_op jit(solution)/shard_map/ppermute | solution.py:492
  26.2 8.0 %collective-permute-start.6 = (f32[10,8,128]{2,1,0:T(8,128)S(1)}, f32[10,8,128]{2,1,0:T(8,128)S(1)}, u32[]{:S(2)}, u32[]{:S(2)}) collective-permute-start(f32[10,8,128]{2,1,0:T(8,128)S(1)} %get-tuple-element.149), channel_id=1, source_target_pairs={{0,15},{1,2},{2,1},{3,4},{4,3},{5,6},{6,5},{7,8},{8,7},{9,10},{10,... | collective-permute-start | bytes 122888 | tf_op jit(solution)/shard_map/ppermute | solution.py:493
  38.4 6.0 %collective-permute-start.9 = (f32[15,8,128]{2,1,0:T(8,128)S(1)}, f32[15,8,128]{2,1,0:T(8,128)S(1)}, u32[]{:S(2)}, u32[]{:S(2)}) collective-permute-start(f32[15,8,128]{2,1,0:T(8,128)S(1)} %get-tuple-element.132), channel_id=1, source_target_pairs={{0,16},{16,0},{32,48},{48,32},{64,80},{80,64},{96,112},{112,96},{1... | collective-permute-start | bytes 184328 | tf_op jit(solution)/shard_map/ppermute | solution.py:492
  41.0 3.6 %collective-permute-start.8 = (f32[15,8,128]{2,1,0:T(8,128)S(1)}, f32[15,8,128]{2,1,0:T(8,128)S(1)}, u32[]{:S(2)}, u32[]{:S(2)}) collective-permute-start(f32[15,8,128]{2,1,0:T(8,128)S(1)} %get-tuple-element.133), channel_id=1, source_target_pairs={{0,240},{16,32},{32,16},{48,64},{64,48},{80,96},{96,80},{112,128},... | collective-permute-start | bytes 184328 | tf_op jit(solution)/shard_map/ppermute | solution.py:493
  46.6 3.3 %collective-permute-start.10 = (f32[24,128]{1,0:T(8,128)S(1)}, f32[24,128]{1,0:T(8,128)S(1)}, u32[]{:S(2)}, u32[]{:S(2)}) collective-permute-start(f32[24,128]{1,0:T(8,128)S(1)} %slice_select_fusion), channel_id=1, source_target_pairs={{0,16},{1,17},{2,18},{3,19},{4,20},{5,21},{6,22},{7,23},{8,24},{9,... | collective-permute-start | bytes 36872 | tf_op jit(solution)/shard_map/ppermute | solution.py:531
  50.0 10.3 %collective-permute-start.12 = (f32[10,8,128]{2,1,0:T(8,128)S(1)}, f32[10,8,128]{2,1,0:T(8,128)S(1)}, u32[]{:S(2)}, u32[]{:S(2)}) collective-permute-start(f32[10,8,128]{2,1,0:T(8,128)S(1)} %get-tuple-element.144), channel_id=1, source_target_pairs={{0,1},{1,0},{2,3},{3,2},{4,5},{5,4},{6,7},{7,6},{8,9},{9,8},{10,11... | collective-permute-start | bytes 122888 | tf_op jit(solution)/shard_map/ppermute | solution.py:492
  50.1 10.2 %collective-permute-start.11 = (f32[10,8,128]{2,1,0:T(8,128)S(1)}, f32[10,8,128]{2,1,0:T(8,128)S(1)}, u32[]{:S(2)}, u32[]{:S(2)}) collective-permute-start(f32[10,8,128]{2,1,0:T(8,128)S(1)} %get-tuple-element.145), channel_id=1, source_target_pairs={{0,15},{1,2},{2,1},{3,4},{4,3},{5,6},{6,5},{7,8},{8,7},{9,10},{10,... | collective-permute-start | bytes 122888 | tf_op jit(solution)/shard_map/ppermute | solution.py:493
  56.8 11.0 %all-to-all-start = ((f32[16,24,128]{2,1,0:T(8,128)}), f32[16,24,128]{2,1,0:T(8,128)S(1)}, u32[]{:S(2)}, u32[]{:S(2)}) async-start(f32[16,24,128]{2,1,0:T(8,128)} %broadcast_in_dim.4), calls=%async_computation | async-start | bytes 393216 | tf_op jit(solution)/shard_map/all_to_all | solution.py:514
  77.1 3.9 %collective-permute-start.13 = (f32[24,128]{1,0:T(8,128)S(1)}, f32[24,128]{1,0:T(8,128)S(1)}, u32[]{:S(2)}, u32[]{:S(2)}) collective-permute-start(f32[24,128]{1,0:T(8,128)S(1)} %reduce_sum.19), channel_id=1, source_target_pairs={{0,16},{1,17},{2,18},{3,19},{4,20},{5,21},{6,22},{7,23},{8,24},{9,... | collective-permute-start | bytes 36872 | tf_op jit(solution)/shard_map/ppermute | solution.py:540

commit v6 on v5

--- a/solution.py
+++ b/solution.py
@@ -363,8 +363,8 @@
 
 def second_body(
     w_ref, yl_ref, yr_ref, mk_ref, im_ref, sa_ref, c0_ref, p_ref, k_ref,
-    part_ref, m1_ref, w2_ref, up_ref, dn_ref, x_ref, c_ref, hh_ref, dd_ref,
-    o_ref, b_ref,
+    part_ref, m1_ref, w2_ref, up_ref, dn_ref, x_ref, c_ref, ha_ref, hb_ref, dd_ref,
+    b_ref,
 ):
     im = im_ref[...] * STEP
     mass = quad((64, 128)) * mk_ref[0:1]
@@ -379,9 +379,8 @@
     def chunk(i, carry):
         n0 = i * CH
         h1, h1h, h1l, h2, h2h, h2l = forward(load8(x_ref, n0), w, ones)
-        put4(hh_ref, i, (h1h, h1l, h2h, h2l))
-        out = mm(w["lo"], jnp.concatenate([h2h, h2l, h2h, ones], axis=0))
-        store8(o_ref, n0, out[0:8])
+        put4(ha_ref, i, (h1h, h1l))
+        put4(hb_ref, i, (h2h, h2l))
         back, *ds = backward(load8(c_ref, n0), 1.0 - h1 * h1, 1.0 - h2 * h2, w)
         put4(dd_ref, i, ds)
         store8(b_ref, n0, back)
@@ -391,7 +390,7 @@
     back = b_ref[0 : F * 64].reshape(F, 64, 128)
     a1 = a2 - v[F:] + (STEP / mass)[None] * back
     m1_ref[...] = a1 * mass[None]
-    part_ref[0:F] = s1 + STEP * o_ref[0 : F * 64].reshape(F, 64, 128)
+    part_ref[0:F] = s1
     part_ref[F:] = a1
     wz = zsum(stiffness(jnp.concatenate([s1, a1], axis=0), k_ref[...], mk_ref[8:9]))
     w2_ref[...] = wz
@@ -412,10 +411,10 @@
     back_ref[...] = b_ref[0 : F * 64].reshape(F, 64, 128)
 
 
-def grads_body(x_ref, c_ref, hh_ref, dd_ref, gw_ref, gb_ref, pay_ref):
+def grads_body(x_ref, c_ref, ha_ref, hb_ref, dd_ref, gw_ref, gb_ref, pay_ref):
     g, gb = add_grads(
         (gw_ref[...], gb_ref[...]), load8(x_ref, 0, 64), load8(c_ref, 0, 64),
-        hh_ref[0:128], hh_ref[128:256], dd_ref[0:128], dd_ref[128:256],
+        ha_ref[...], hb_ref[...], dd_ref[0:128], dd_ref[128:256],
     )
 
     def fold(t):
@@ -435,12 +434,24 @@
 
 
 def finish_body(
-    w_ref, yl_ref, yr_ref, mk_ref, im_ref, part_ref, back_ref, g_ref, s_ref, a_ref
+    w_ref, yl_ref, yr_ref, mk_ref, im_ref, part_ref, back_ref, g_ref, hb_ref, p_ref, s_ref, a_ref, o_ref
 ):
     im = im_ref[...] * STEP
     mass = quad((64, 128)) * mk_ref[0:1]
     v = zfill(yadd(w_ref[...], yl_ref[...], yr_ref[...])) * im[None]
-    s2 = part_ref[0:F] - v[0:F]
+    w = weights(p_ref)
+    ones = bias_rows()
+
+    def chunk(i, carry):
+        at = lanes_of(i)
+        h2h, h2l = hb_ref[0:64, at], hb_ref[64:128, at]
+        out = mm(w["lo"], jnp.concatenate([h2h, h2l, h2h, ones], axis=0))
+        store8(o_ref, i * CH, out[0:8])
+        return carry
+
+    lax.fori_loop(0, 64 // CH, chunk, 0)
+    forcing = o_ref[0 : F * 64].reshape(F, 64, 128)
+    s2 = part_ref[0:F] + STEP * forcing - v[0:F]
     a0 = (part_ref[F:] - v[F:]) * mass[None] + STEP * back_ref[...]
     x = jnp.concatenate([s2.reshape(320, 128), a0.reshape(320, 128)], axis=0)
     y = permute_nn(x, g_ref[...])
@@ -557,6 +568,7 @@
     flags = (even_at("sub"), even_at("col"), element_weight)
     even_s, even_c, element_weight = lax.optimization_barrier(flags)
     hot = jax.ShapeDtypeStruct((128, 128), bf16)
+    half = jax.ShapeDtypeStruct((128, 8192), bf16)
     wide = jax.ShapeDtypeStruct((256, 8192), bf16)
     khot = jax.ShapeDtypeStruct((64, 192), bf16)
 
@@ -617,11 +629,11 @@
         trans=1000000,
     )
     w, yl, yr = faces(w, up, dn, 10)
-    part, m1, w, up, dn, x1, c1, hh1, dd1 = call(
+    part, m1, w, up, dn, x1, c1, ha1, hb1, dd1 = call(
         second_body,
-        [(10, 64, 128), (F, 64, 128)] + ten + [(512, 128), (512, 128), wide, wide],
+        [(10, 64, 128), (F, 64, 128)] + ten + [(512, 128), (512, 128), half, half, wide],
         [w, yl, yr, mk, im, sa, c0, pw, kmat],
-        [(512, 128)] * 2,
+        [(512, 128)],
         flops=900000000,
         trans=1000000,
     )
@@ -634,7 +646,7 @@
     )
     rp, rm = both_ways(up, dn, "sub", even_s)
     gw, rp, rm = lax.optimization_barrier((gw, rp, rm))
-    (pay,) = call(grads_body, [(48, 128)], [x1, c1, hh1, dd1, gw, gb], flops=300000000)
+    (pay,) = call(grads_body, [(48, 128)], [x1, c1, ha1, hb1, dd1, gw, gb], flops=300000000)
     w, yu, yd = in_device(w, rp, rm, 10)
     if grid_is_whole():
         pay = chip_sum(pay, even_s)
@@ -643,7 +655,8 @@
         out_state, out_adj = call(
             finish_body,
             [(F, 64, 128), (F, 64, 128)],
-            [w, yl, yr, mk, im, part, back, g],
+            [w, yl, yr, mk, im, part, back, g, hb1, pw],
+            [(512, 128)],
             flops=20000000,
         )
         pay = plane_sum(pay)
@@ -655,7 +668,8 @@
         out_state, out_adj = call(
             finish_body,
             [(F, 64, 128), (F, 64, 128)],
-            [w, yl, yr, mk, im, part, back, g],
+            [w, yl, yr, mk, im, part, back, g, hb1, pw],
+            [(512, 128)],
             flops=20000000,
         )
         terms = [pay[:24], pay[24:]]

time: 82 us -> 81.4 us (level)
  transfers between devices with their start and end apart: 15 -> 15, of which waited for: 9 -> 9; matrix products, arithmetic and copies ran while one was open for 1% -> 1% of each run, Pallas kernels for 9% -> 10%
where the time goes in v6:
time: 81.4 us; the launch traced here: 81.1 us
  starting transfers between devices  37.8 us (46%)
  Pallas kernels  17.2 us (21%)
  waiting for transfers between devices  15.1 us (19%)
  blocking collectives  9.29 us (11%)
  between operations  0.91 us (1%)
    ppermute x6, starting transfers between devices, both_ways(): lax.ppermute(jnp.where(even, dn, up), axis, [(i, (i + 1 if i % 2 else i -...  19.1 us
    pallas_call x12, Pallas kernels, call(): pl.pallas_call(body, out_shape=shapes, in_specs=[pl.BlockSpec(memory_spac...  17.2 us
    ppermute x6, starting transfers between devices, both_ways(): lax.ppermute(jnp.where(even, up, dn), axis, [(i, i ^ 1) for i in range(n)])  9.63 us
    all_to_all x1, blocking collectives, send_to_all(): lax.all_to_all(y, ('sub', 'col'), 0, 0, axis_index_groups=groups, tiled=T...  9.29 us
    ppermute x6, waiting for transfers between devices, both_ways(): lax.ppermute(jnp.where(even, dn, up), axis, [(i, (i + 1 if i % 2 else i -...  6.24 us
    all_to_all x1, waiting for transfers between devices, send_to_all(): lax.all_to_all(y, ('sub', 'col'), 0, 0, axis_index_groups=groups, tiled=T...  5.55 us
    all_to_all x1, starting transfers between devices, send_to_all(): lax.all_to_all(y, ('sub', 'col'), 0, 0, axis_index_groups=groups, tiled=T...  3.52 us
    ppermute x1, starting transfers between devices, rest_sum(): other = lax.ppermute(x, ('sub', 'col'), SWAP)  3.06 us
  transfers between devices with their start and end apart: 15, of which 9 were waited for; matrix products, arithmetic and copies ran while one was open for 1% of the time, Pallas kernels for 10%

profile of v6, /device:TPU:1, one launch (start us, length us, event | category | flops | bytes accessed | tf_op | source)
XLA Modules:
  0.0 81.1 jit_solution(6448400133727596423)
XLA Ops:
  0.7 1.6 %shard_map.179 = (f32[12,48,128]{2,1,0:T(8,128)S(1)}, f32[18,8,128]{2,1,0:T(8,128)S(1)}, f32[18,8,128]{2,1,0:T(8,128)S(1)}, f32[16,128]{1,0:T(8,128)S(1)}, bf16[...) custom-call(f32[5,64,128]{2,1,0:T(8,128)} %s_in.1, f32[5,64,128]{2,1,0:T(8,128)} %c_in.1, s32[1,128]{1,0:T(1,128)} %o_in.1, ...), custom_call_target="tpu_custom_call" | custom-call | bytes 2000000 | tf_op jit(solution)/shard_map/pallas_call | solution.py:483
  2.3 3.3 %collective-permute-start.1 = (f32[18,8,128]{2,1,0:T(8,128)S(1)}, f32[18,8,128]{2,1,0:T(8,128)S(1)}, u32[]{:S(2)}, u32[]{:S(2)}) collective-permute-start(f32[18,8,128]{2,1,0:T(8,128)S(1)} %get-tuple-element.130), channel_id=1, source_target_pairs={{0,16},{16,0},{32,48},{48,32},{64,80},{80,64},{96,112},{112,96},{1... | collective-permute-start | bytes 221192 | tf_op jit(solution)/shard_map/ppermute | solution.py:503
  5.6 0.9 %collective-permute-done.1 = f32[18,8,128]{2,1,0:T(8,128)S(1)} collective-permute-done((f32[18,8,128]{2,1,0:T(8,128)S(1)}, f32[18,8,128]{2,1,0:T(8,128)S(1)}, u32[]{:S(2)}, u32[]{:S(2)}) %collective-permute-start.1) | collective-permute-done | bytes 73760 | tf_op jit(solution)/shard_map/ppermute | solution.py:503
  6.5 2.9 %collective-permute-done = f32[18,8,128]{2,1,0:T(8,128)S(1)} collective-permute-done((f32[18,8,128]{2,1,0:T(8,128)S(1)}, f32[18,8,128]{2,1,0:T(8,128)S(1)}, u32[]{:S(2)}, u32[]{:S(2)}) %collective-permute-start) | collective-permute-done | bytes 73760 | tf_op jit(solution)/shard_map/ppermute | solution.py:504
  9.8 7.0 %collective-permute-start.2 = (f32[11,8,128]{2,1,0:T(8,128)S(1)}, f32[11,8,128]{2,1,0:T(8,128)S(1)}, u32[]{:S(2)}, u32[]{:S(2)}) collective-permute-start(f32[11,8,128]{2,1,0:T(8,128)S(1)} %get-tuple-element.143), channel_id=1, source_target_pairs={{0,15},{1,2},{2,1},{3,4},{4,3},{5,6},{6,5},{7,8},{8,7},{9,10},{10,... | collective-permute-start | bytes 135176 | tf_op jit(solution)/shard_map/ppermute | solution.py:504
  16.8 1.1 %shard_map.181.p_ref = bf16[272,256]{1,0:T(8,128)(2,1)S(1)} custom-call(f32[5,64]{1,0:T(8,128)} %bitcast.10, f32[1,64]{1,0:T(1,128)} %bitcast.13, f32[64,64]{1,0:T(8,128)} %w2_in.1, f32[1,64]{1,0:T(1,128)} %bitcast.14, f32[5,64]{1,0:T(8,128)} %wo_in.1, f32[1,5]{1,0:T(1,128)} %bitcast.15), custom_call_target="tpu_custom_call" | custom-call | flops 2000000 | bytes 2000000 | tf_op jit(solution)/shard_map/pallas_call | solution.py:483
  18.8 3.4 %collective-permute-start.5 = (f32[15,8,128]{2,1,0:T(8,128)S(1)}, f32[15,8,128]{2,1,0:T(8,128)S(1)}, u32[]{:S(2)}, u32[]{:S(2)}) collective-permute-start(f32[15,8,128]{2,1,0:T(8,128)S(1)} %get-tuple-element.138), channel_id=1, source_target_pairs={{0,16},{16,0},{32,48},{48,32},{64,80},{80,64},{96,112},{112,96},{1... | collective-permute-start | bytes 184328 | tf_op jit(solution)/shard_map/ppermute | solution.py:503
  22.2 0.9 %collective-permute-done.5 = f32[15,8,128]{2,1,0:T(8,128)S(1)} collective-permute-done((f32[15,8,128]{2,1,0:T(8,128)S(1)}, f32[15,8,128]{2,1,0:T(8,128)S(1)}, u32[]{:S(2)}, u32[]{:S(2)}) %collective-permute-start.5) | collective-permute-done | bytes 61472 | tf_op jit(solution)/shard_map/ppermute | solution.py:503
  23.1 2.7 %collective-permute-done.4 = f32[15,8,128]{2,1,0:T(8,128)S(1)} collective-permute-done((f32[15,8,128]{2,1,0:T(8,128)S(1)}, f32[15,8,128]{2,1,0:T(8,128)S(1)}, u32[]{:S(2)}, u32[]{:S(2)}) %collective-permute-start.4) | collective-permute-done | bytes 61472 | tf_op jit(solution)/shard_map/ppermute | solution.py:504
  26.2 6.0 %collective-permute-start.6 = (f32[10,8,128]{2,1,0:T(8,128)S(1)}, f32[10,8,128]{2,1,0:T(8,128)S(1)}, u32[]{:S(2)}, u32[]{:S(2)}) collective-permute-start(f32[10,8,128]{2,1,0:T(8,128)S(1)} %get-tuple-element.151), channel_id=1, source_target_pairs={{0,15},{1,2},{2,1},{3,4},{4,3},{5,6},{6,5},{7,8},{8,7},{9,10},{10,... | collective-permute-start | bytes 122888 | tf_op jit(solution)/shard_map/ppermute | solution.py:504
  32.2 2.0 %shard_map.184 = (f32[5,64,128]{2,1,0:T(8,128)S(1)}, f32[512,128]{1,0:T(8,128)S(1)}, bf16[256,8192]{1,0:T(8,128)(2,1)S(1)}, f32[128,8192]{1,0:T(8,128)S(1)}) custom-call(f32[10,64,128]{2,1,0:T(8,128)S(1)} %get-tuple-element.88.sa_ref, bf16[272,256]{1,0:T(8,128)(2,1)S(1)} %shard_map.181.p_ref), custom_call_target="tpu_custom_call" | custom-call | flops 300000000 | bytes 2000000 | tf_op jit(solution)/shard_map/pallas_call | solution.py:483
  34.3 3.5 %shard_map.185 = (f32[10,64,128]{2,1,0:T(8,128)S(1)}, f32[5,64,128]{2,1,0:T(8,128)S(1)}, f32[10,48,128]{2,1,0:T(8,128)S(1)}, f32[15,8,128]{2,1,0:T(8,128)S(1)}, ...) custom-call(f32[10,3,2,8,128]{4,3,2,1,0:T(8,128)S(1)} %get-tuple-ele, ...), custom_call_target="tpu_custom_call" | custom-call | flops 900000000 | bytes 2000000 | tf_op jit(solution)/shard_map/pallas_call | solution.py:483
  37.8 2.6 %collective-permute-start.9 = (f32[15,8,128]{2,1,0:T(8,128)S(1)}, f32[15,8,128]{2,1,0:T(8,128)S(1)}, u32[]{:S(2)}, u32[]{:S(2)}) collective-permute-start(f32[15,8,128]{2,1,0:T(8,128)S(1)} %get-tuple-element.134), channel_id=1, source_target_pairs={{0,16},{16,0},{32,48},{48,32},{64,80},{80,64},{96,112},{112,96},{1... | collective-permute-start | bytes 184328 | tf_op jit(solution)/shard_map/ppermute | solution.py:503
  40.4 3.4 %shard_map.186 = (f32[5,64,128]{2,1,0:T(8,128)S(1)}, f32[384,160]{1,0:T(8,128)S(1)}, f32[8,128]{1,0:T(8,128)S(1)}) custom-call(f32[512,128]{1,0:T(8,128)S(1)} %get-tuple-element.96.x_ref, f32[5,64,128]{2,1,0:T(8,128)S(1)} %get-tuple-element.97.m1_ref, bf16[256,8192]{1,0:T(8,128)(2,1)S(1)} %get-tuple-element.98.hh_ref, ...), custom_call_target="tpu_custom_call" | custom-call | flops 600000000 | bytes 2000000 | tf_op jit(solution)/shard_map/pallas_call | solution.py:483
  44.0 2.0 %shard_map.187 = f32[48,128]{1,0:T(8,128)S(1)} custom-call(f32[512,128]{1,0:T(8,128)S(1)} %get-tuple-element.91.x_ref, f32[512,128]{1,0:T(8,128)S(1)} %get-tuple-element.92.c_ref, bf16[128,8192]{1,0:T(8,128)(2,1)S(1)} %get-tuple-element.93.ha_ref, bf16[128,8192]{1,0:T(8,128)(2,1)S(1)} %get-tuple-element.94.hb_ref, ...), custom_call_target="tpu_custom_call" | custom-call | flops 300000000 | bytes 2000000 | tf_op jit(solution)/shard_map/pallas_call | solution.py:483
  46.0 2.5 %collective-permute-start.10 = (f32[24,128]{1,0:T(8,128)S(1)}, f32[24,128]{1,0:T(8,128)S(1)}, u32[]{:S(2)}, u32[]{:S(2)}) collective-permute-start(f32[24,128]{1,0:T(8,128)S(1)} %slice_select_fusion), channel_id=1, source_target_pairs={{0,16},{1,17},{2,18},{3,19},{4,20},{5,21},{6,22},{7,23},{8,24},{9,... | collective-permute-start | bytes 36872 | tf_op jit(solution)/shard_map/ppermute | solution.py:542
  49.5 6.0 %collective-permute-start.11 = (f32[10,8,128]{2,1,0:T(8,128)S(1)}, f32[10,8,128]{2,1,0:T(8,128)S(1)}, u32[]{:S(2)}, u32[]{:S(2)}) collective-permute-start(f32[10,8,128]{2,1,0:T(8,128)S(1)} %get-tuple-element.147), channel_id=1, source_target_pairs={{0,15},{1,2},{2,1},{3,4},{4,3},{5,6},{6,5},{7,8},{8,7},{9,10},{10,... | collective-permute-start | bytes 122888 | tf_op jit(solution)/shard_map/ppermute | solution.py:504
  56.2 3.5 %all-to-all-start = ((f32[16,24,128]{2,1,0:T(8,128)}), f32[16,24,128]{2,1,0:T(8,128)S(1)}, u32[]{:S(2)}, u32[]{:S(2)}) async-start(f32[16,24,128]{2,1,0:T(8,128)} %broadcast_in_dim.4), calls=%async_computation | async-start | bytes 393216 | tf_op jit(solution)/shard_map/all_to_all | solution.py:525
  59.7 1.9 %shard_map.189 = (f32[5,64,128]{2,1,0:T(8,128)}, f32[5,64,128]{2,1,0:T(8,128)}) custom-call(f32[10,3,2,8,128]{4,3,2,1,0:T(8,128)S(1)} %get-tuple-element.111.w_ref, f32[10,8,128]{2,1,0:T(8,128)S(1)} %get-tuple-element.145.yl_ref, f32[10,8,128]{2,1,0:T(8,128)S(1)} %get-tuple-element.144.yr_ref, f32[16,128]{1,0:T(8,128)S(1)} %get-tuple-element.79.mk_ref, ...), custom_call_target="tpu_custom_call" | custom-call | flops 20000000 | bytes 2000000 | tf_op jit(solution)/shard_map/pallas_call | solution.py:483
  61.6 5.5 %all-to-all-done = f32[16,24,128]{2,1,0:T(8,128)S(1)} async-done(((f32[16,24,128]{2,1,0:T(8,128)}), f32[16,24,128]{2,1,0:T(8,128)S(1)}, u32[]{:S(2)}, u32[]{:S(2)}) %all-to-all-start) | async-done | bytes 196640 | tf_op jit(solution)/shard_map/all_to_all | solution.py:525
  67.2 9.3 %all_to_all.10 = f32[8,24,128]{2,1,0:T(8,128)S(1)} all-to-all(f32[8,24,128]{2,1,0:T(8,128)S(1)} %broadcast_in_dim.5), channel_id=1, replica_groups={{0,4,8,12,128,132,136,140},{1,5,9,13,129,133,137,141},{2,6,10,14,130,13..., dimensions={0} | all-to-all | bytes 196608 | tf_op jit(solution)/shard_map/all_to_all | solution.py:525
  76.5 3.1 %collective-permute-start.13 = (f32[24,128]{1,0:T(8,128)S(1)}, f32[24,128]{1,0:T(8,128)S(1)}, u32[]{:S(2)}, u32[]{:S(2)}) collective-permute-start(f32[24,128]{1,0:T(8,128)S(1)} %reduce_sum.19), channel_id=1, source_target_pairs={{0,16},{1,17},{2,18},{3,19},{4,20},{5,21},{6,22},{7,23},{8,24},{9,... | collective-permute-start | bytes 36872 | tf_op jit(solution)/shard_map/ppermute | solution.py:551
  79.5 0.8 %collective-permute-done.13 = f32[24,128]{1,0:T(8,128)S(1)} collective-permute-done((f32[24,128]{1,0:T(8,128)S(1)}, f32[24,128]{1,0:T(8,128)S(1)}, u32[]{:S(2)}, u32[]{:S(2)}) %collective-permute-start.13) | collective-permute-done | bytes 12320 | tf_op jit(solution)/shard_map/ppermute | solution.py:551
  80.4 0.7 shard_map.190
  (38 shorter events, 3.6 us)
Async XLA Ops:
  2.3 4.2 %collective-permute-start.1 = (f32[18,8,128]{2,1,0:T(8,128)S(1)}, f32[18,8,128]{2,1,0:T(8,128)S(1)}, u32[]{:S(2)}, u32[]{:S(2)}) collective-permute-start(f32[18,8,128]{2,1,0:T(8,128)S(1)} %get-tuple-element.130), channel_id=1, source_target_pairs={{0,16},{16,0},{32,48},{48,32},{64,80},{80,64},{96,112},{112,96},{1... | collective-permute-start | bytes 221192 | tf_op jit(solution)/shard_map/ppermute | solution.py:503
  5.6 3.8 %collective-permute-start = (f32[18,8,128]{2,1,0:T(8,128)S(1)}, f32[18,8,128]{2,1,0:T(8,128)S(1)}, u32[]{:S(2)}, u32[]{:S(2)}) collective-permute-start(f32[18,8,128]{2,1,0:T(8,128)S(1)} %get-tuple-element.131), channel_id=1, source_target_pairs={{0,240},{16,32},{32,16},{48,64},{64,48},{80,96},{96,80},{112,128},... | collective-permute-start | bytes 221192 | tf_op jit(solution)/shard_map/ppermute | solution.py:504
  9.7 8.2 %collective-permute-start.3 = (f32[11,8,128]{2,1,0:T(8,128)S(1)}, f32[11,8,128]{2,1,0:T(8,128)S(1)}, u32[]{:S(2)}, u32[]{:S(2)}) collective-permute-start(f32[11,8,128]{2,1,0:T(8,128)S(1)} %get-tuple-element.142), channel_id=1, source_target_pairs={{0,1},{1,0},{2,3},{3,2},{4,5},{5,4},{6,7},{7,6},{8,9},{9,8},{10,11... | collective-permute-start | bytes 135176 | tf_op jit(solution)/shard_map/ppermute | solution.py:503
  9.8 8.5 %collective-permute-start.2 = (f32[11,8,128]{2,1,0:T(8,128)S(1)}, f32[11,8,128]{2,1,0:T(8,128)S(1)}, u32[]{:S(2)}, u32[]{:S(2)}) collective-permute-start(f32[11,8,128]{2,1,0:T(8,128)S(1)} %get-tuple-element.143), channel_id=1, source_target_pairs={{0,15},{1,2},{2,1},{3,4},{4,3},{5,6},{6,5},{7,8},{8,7},{9,10},{10,... | collective-permute-start | bytes 135176 | tf_op jit(solution)/shard_map/ppermute | solution.py:504
  18.8 4.3 %collective-permute-start.5 = (f32[15,8,128]{2,1,0:T(8,128)S(1)}, f32[15,8,128]{2,1,0:T(8,128)S(1)}, u32[]{:S(2)}, u32[]{:S(2)}) collective-permute-start(f32[15,8,128]{2,1,0:T(8,128)S(1)} %get-tuple-element.138), channel_id=1, source_target_pairs={{0,16},{16,0},{32,48},{48,32},{64,80},{80,64},{96,112},{112,96},{1... | collective-permute-start | bytes 184328 | tf_op jit(solution)/shard_map/ppermute | solution.py:503
  22.2 3.6 %collective-permute-start.4 = (f32[15,8,128]{2,1,0:T(8,128)S(1)}, f32[15,8,128]{2,1,0:T(8,128)S(1)}, u32[]{:S(2)}, u32[]{:S(2)}) collective-permute-start(f32[15,8,128]{2,1,0:T(8,128)S(1)} %get-tuple-element.139), channel_id=1, source_target_pairs={{0,240},{16,32},{32,16},{48,64},{64,48},{80,96},{96,80},{112,128},... | collective-permute-start | bytes 184328 | tf_op jit(solution)/shard_map/ppermute | solution.py:504
  26.1 8.1 %collective-permute-start.7 = (f32[10,8,128]{2,1,0:T(8,128)S(1)}, f32[10,8,128]{2,1,0:T(8,128)S(1)}, u32[]{:S(2)}, u32[]{:S(2)}) collective-permute-start(f32[10,8,128]{2,1,0:T(8,128)S(1)} %get-tuple-element.150), channel_id=1, source_target_pairs={{0,1},{1,0},{2,3},{3,2},{4,5},{5,4},{6,7},{7,6},{8,9},{9,8},{10,11... | collective-permute-start | bytes 122888 | tf_op jit(solution)/shard_map/ppermute | solution.py:503
  26.2 8.0 %collective-permute-start.6 = (f32[10,8,128]{2,1,0:T(8,128)S(1)}, f32[10,8,128]{2,1,0:T(8,128)S(1)}, u32[]{:S(2)}, u32[]{:S(2)}) collective-permute-start(f32[10,8,128]{2,1,0:T(8,128)S(1)} %get-tuple-element.151), channel_id=1, source_target_pairs={{0,15},{1,2},{2,1},{3,4},{4,3},{5,6},{6,5},{7,8},{8,7},{9,10},{10,... | collective-permute-start | bytes 122888 | tf_op jit(solution)/shard_map/ppermute | solution.py:504
  37.8 6.0 %collective-permute-start.9 = (f32[15,8,128]{2,1,0:T(8,128)S(1)}, f32[15,8,128]{2,1,0:T(8,128)S(1)}, u32[]{:S(2)}, u32[]{:S(2)}) collective-permute-start(f32[15,8,128]{2,1,0:T(8,128)S(1)} %get-tuple-element.134), channel_id=1, source_target_pairs={{0,16},{16,0},{32,48},{48,32},{64,80},{80,64},{96,112},{112,96},{1... | collective-permute-start | bytes 184328 | tf_op jit(solution)/shard_map/ppermute | solution.py:503
  40.4 3.6 %collective-permute-start.8 = (f32[15,8,128]{2,1,0:T(8,128)S(1)}, f32[15,8,128]{2,1,0:T(8,128)S(1)}, u32[]{:S(2)}, u32[]{:S(2)}) collective-permute-start(f32[15,8,128]{2,1,0:T(8,128)S(1)} %get-tuple-element.135), channel_id=1, source_target_pairs={{0,240},{16,32},{32,16},{48,64},{64,48},{80,96},{96,80},{112,128},... | collective-permute-start | bytes 184328 | tf_op jit(solution)/shard_map/ppermute | solution.py:504
  46.0 3.3 %collective-permute-start.10 = (f32[24,128]{1,0:T(8,128)S(1)}, f32[24,128]{1,0:T(8,128)S(1)}, u32[]{:S(2)}, u32[]{:S(2)}) collective-permute-start(f32[24,128]{1,0:T(8,128)S(1)} %slice_select_fusion), channel_id=1, source_target_pairs={{0,16},{1,17},{2,18},{3,19},{4,20},{5,21},{6,22},{7,23},{8,24},{9,... | collective-permute-start | bytes 36872 | tf_op jit(solution)/shard_map/ppermute | solution.py:542
  49.4 10.3 %collective-permute-start.12 = (f32[10,8,128]{2,1,0:T(8,128)S(1)}, f32[10,8,128]{2,1,0:T(8,128)S(1)}, u32[]{:S(2)}, u32[]{:S(2)}) collective-permute-start(f32[10,8,128]{2,1,0:T(8,128)S(1)} %get-tuple-element.146), channel_id=1, source_target_pairs={{0,1},{1,0},{2,3},{3,2},{4,5},{5,4},{6,7},{7,6},{8,9},{9,8},{10,11... | collective-permute-start | bytes 122888 | tf_op jit(solution)/shard_map/ppermute | solution.py:503
  49.5 10.2 %collective-permute-start.11 = (f32[10,8,128]{2,1,0:T(8,128)S(1)}, f32[10,8,128]{2,1,0:T(8,128)S(1)}, u32[]{:S(2)}, u32[]{:S(2)}) collective-permute-start(f32[10,8,128]{2,1,0:T(8,128)S(1)} %get-tuple-element.147), channel_id=1, source_target_pairs={{0,15},{1,2},{2,1},{3,4},{4,3},{5,6},{6,5},{7,8},{8,7},{9,10},{10,... | collective-permute-start | bytes 122888 | tf_op jit(solution)/shard_map/ppermute | solution.py:504
  56.2 11.0 %all-to-all-start = ((f32[16,24,128]{2,1,0:T(8,128)}), f32[16,24,128]{2,1,0:T(8,128)S(1)}, u32[]{:S(2)}, u32[]{:S(2)}) async-start(f32[16,24,128]{2,1,0:T(8,128)} %broadcast_in_dim.4), calls=%async_computation | async-start | bytes 393216 | tf_op jit(solution)/shard_map/all_to_all | solution.py:525
  76.5 3.9 %collective-permute-start.13 = (f32[24,128]{1,0:T(8,128)S(1)}, f32[24,128]{1,0:T(8,128)S(1)}, u32[]{:S(2)}, u32[]{:S(2)}) collective-permute-start(f32[24,128]{1,0:T(8,128)S(1)} %reduce_sum.19), channel_id=1, source_target_pairs={{0,16},{1,17},{2,18},{3,19},{4,20},{5,21},{6,22},{7,23},{8,24},{9,... | collective-permute-start | bytes 36872 | tf_op jit(solution)/shard_map/ppermute | solution.py:551

commit v7 on v6

--- a/solution.py
+++ b/solution.py
@@ -542,12 +542,12 @@
     return mine + lax.ppermute(jnp.where(core, high, low), ("sub", "col"), SWAP)
 
 
-def plane_sum(x):
-    return send_to_all(x, together((0, 2, 3))).sum(0)
+def column_sum(x):
+    return send_to_all(x, together((1, 2, 4))).sum(0)
 
 
 def rest_sum(x, core):
-    x = send_to_all(x, together((1, 2, 4))).sum(0)
+    x = send_to_all(x, together((0, 2, 3))).sum(0)
     other = lax.ppermute(x, ("sub", "col"), SWAP)
     return jnp.where(core, x, other), jnp.where(core, other, x)
 
@@ -659,7 +659,7 @@
             [(512, 128)],
             flops=20000000,
         )
-        pay = plane_sum(pay)
+        pay = column_sum(pay)
         pay, out_state, out_adj = lax.optimization_barrier((pay, out_state, out_adj))
         terms = list(rest_sum(pay, even_s))
     else:

time: 81.4 us -> 81.2 us (level)
  no operation moved by 1% of the time
where the time goes in v7:
time: 81.2 us; the launch traced here: 80.9 us
  starting transfers between devices  37.7 us (46%)
  Pallas kernels  17.2 us (21%)
  waiting for transfers between devices  14.4 us (18%)
  blocking collectives  9.84 us (12%)
  between operations  0.91 us (1%)
    ppermute x6, starting transfers between devices, both_ways(): lax.ppermute(jnp.where(even, dn, up), axis, [(i, (i + 1 if i % 2 else i -...  19.1 us
    pallas_call x12, Pallas kernels, call(): pl.pallas_call(body, out_shape=shapes, in_specs=[pl.BlockSpec(memory_spac...  17.2 us
    all_to_all x1, blocking collectives, send_to_all(): lax.all_to_all(y, ('sub', 'col'), 0, 0, axis_index_groups=groups, tiled=T...  9.84 us
    ppermute x6, starting transfers between devices, both_ways(): lax.ppermute(jnp.where(even, up, dn), axis, [(i, i ^ 1) for i in range(n)])  9.63 us
    ppermute x6, waiting for transfers between devices, both_ways(): lax.ppermute(jnp.where(even, dn, up), axis, [(i, (i + 1 if i % 2 else i -...  6.24 us
    all_to_all x1, waiting for transfers between devices, send_to_all(): lax.all_to_all(y, ('sub', 'col'), 0, 0, axis_index_groups=groups, tiled=T...  4.94 us
    all_to_all x1, starting transfers between devices, send_to_all(): lax.all_to_all(y, ('sub', 'col'), 0, 0, axis_index_groups=groups, tiled=T...  3.36 us
    ppermute x1, starting transfers between devices, rest_sum(): other = lax.ppermute(x, ('sub', 'col'), SWAP)  3.16 us
  transfers between devices with their start and end apart: 15, of which 9 were waited for; matrix products, arithmetic and copies ran while one was open for 1% of the time, Pallas kernels for 10%

profile of v7, /device:TPU:1, one launch (start us, length us, event | category | flops | bytes accessed | tf_op | source)
XLA Modules:
  0.0 80.9 jit_solution(4633658904738788446)
XLA Ops:
  0.7 1.6 %shard_map.179 = (f32[12,48,128]{2,1,0:T(8,128)S(1)}, f32[18,8,128]{2,1,0:T(8,128)S(1)}, f32[18,8,128]{2,1,0:T(8,128)S(1)}, f32[16,128]{1,0:T(8,128)S(1)}, bf16[...) custom-call(f32[5,64,128]{2,1,0:T(8,128)} %s_in.1, f32[5,64,128]{2,1,0:T(8,128)} %c_in.1, s32[1,128]{1,0:T(1,128)} %o_in.1, ...), custom_call_target="tpu_custom_call" | custom-call | bytes 2000000 | tf_op jit(solution)/shard_map/pallas_call | solution.py:483
  2.3 3.3 %collective-permute-start.1 = (f32[18,8,128]{2,1,0:T(8,128)S(1)}, f32[18,8,128]{2,1,0:T(8,128)S(1)}, u32[]{:S(2)}, u32[]{:S(2)}) collective-permute-start(f32[18,8,128]{2,1,0:T(8,128)S(1)} %get-tuple-element.130), channel_id=1, source_target_pairs={{0,16},{16,0},{32,48},{48,32},{64,80},{80,64},{96,112},{112,96},{1... | collective-permute-start | bytes 221192 | tf_op jit(solution)/shard_map/ppermute | solution.py:503
  5.6 0.9 %collective-permute-done.1 = f32[18,8,128]{2,1,0:T(8,128)S(1)} collective-permute-done((f32[18,8,128]{2,1,0:T(8,128)S(1)}, f32[18,8,128]{2,1,0:T(8,128)S(1)}, u32[]{:S(2)}, u32[]{:S(2)}) %collective-permute-start.1) | collective-permute-done | bytes 73760 | tf_op jit(solution)/shard_map/ppermute | solution.py:503
  6.5 2.9 %collective-permute-done = f32[18,8,128]{2,1,0:T(8,128)S(1)} collective-permute-done((f32[18,8,128]{2,1,0:T(8,128)S(1)}, f32[18,8,128]{2,1,0:T(8,128)S(1)}, u32[]{:S(2)}, u32[]{:S(2)}) %collective-permute-start) | collective-permute-done | bytes 73760 | tf_op jit(solution)/shard_map/ppermute | solution.py:504
  9.8 7.0 %collective-permute-start.2 = (f32[11,8,128]{2,1,0:T(8,128)S(1)}, f32[11,8,128]{2,1,0:T(8,128)S(1)}, u32[]{:S(2)}, u32[]{:S(2)}) collective-permute-start(f32[11,8,128]{2,1,0:T(8,128)S(1)} %get-tuple-element.143), channel_id=1, source_target_pairs={{0,15},{1,2},{2,1},{3,4},{4,3},{5,6},{6,5},{7,8},{8,7},{9,10},{10,... | collective-permute-start | bytes 135176 | tf_op jit(solution)/shard_map/ppermute | solution.py:504
  16.8 1.1 %shard_map.181.p_ref = bf16[272,256]{1,0:T(8,128)(2,1)S(1)} custom-call(f32[5,64]{1,0:T(8,128)} %bitcast.10, f32[1,64]{1,0:T(1,128)} %bitcast.13, f32[64,64]{1,0:T(8,128)} %w2_in.1, f32[1,64]{1,0:T(1,128)} %bitcast.14, f32[5,64]{1,0:T(8,128)} %wo_in.1, f32[1,5]{1,0:T(1,128)} %bitcast.15), custom_call_target="tpu_custom_call" | custom-call | flops 2000000 | bytes 2000000 | tf_op jit(solution)/shard_map/pallas_call | solution.py:483
  18.8 3.4 %collective-permute-start.5 = (f32[15,8,128]{2,1,0:T(8,128)S(1)}, f32[15,8,128]{2,1,0:T(8,128)S(1)}, u32[]{:S(2)}, u32[]{:S(2)}) collective-permute-start(f32[15,8,128]{2,1,0:T(8,128)S(1)} %get-tuple-element.138), channel_id=1, source_target_pairs={{0,16},{16,0},{32,48},{48,32},{64,80},{80,64},{96,112},{112,96},{1... | collective-permute-start | bytes 184328 | tf_op jit(solution)/shard_map/ppermute | solution.py:503
  22.2 0.9 %collective-permute-done.5 = f32[15,8,128]{2,1,0:T(8,128)S(1)} collective-permute-done((f32[15,8,128]{2,1,0:T(8,128)S(1)}, f32[15,8,128]{2,1,0:T(8,128)S(1)}, u32[]{:S(2)}, u32[]{:S(2)}) %collective-permute-start.5) | collective-permute-done | bytes 61472 | tf_op jit(solution)/shard_map/ppermute | solution.py:503
  23.1 2.7 %collective-permute-done.4 = f32[15,8,128]{2,1,0:T(8,128)S(1)} collective-permute-done((f32[15,8,128]{2,1,0:T(8,128)S(1)}, f32[15,8,128]{2,1,0:T(8,128)S(1)}, u32[]{:S(2)}, u32[]{:S(2)}) %collective-permute-start.4) | collective-permute-done | bytes 61472 | tf_op jit(solution)/shard_map/ppermute | solution.py:504
  26.2 6.0 %collective-permute-start.6 = (f32[10,8,128]{2,1,0:T(8,128)S(1)}, f32[10,8,128]{2,1,0:T(8,128)S(1)}, u32[]{:S(2)}, u32[]{:S(2)}) collective-permute-start(f32[10,8,128]{2,1,0:T(8,128)S(1)} %get-tuple-element.151), channel_id=1, source_target_pairs={{0,15},{1,2},{2,1},{3,4},{4,3},{5,6},{6,5},{7,8},{8,7},{9,10},{10,... | collective-permute-start | bytes 122888 | tf_op jit(solution)/shard_map/ppermute | solution.py:504
  32.2 2.0 %shard_map.184 = (f32[5,64,128]{2,1,0:T(8,128)S(1)}, f32[512,128]{1,0:T(8,128)S(1)}, bf16[256,8192]{1,0:T(8,128)(2,1)S(1)}, f32[128,8192]{1,0:T(8,128)S(1)}) custom-call(f32[10,64,128]{2,1,0:T(8,128)S(1)} %get-tuple-element.88.sa_ref, bf16[272,256]{1,0:T(8,128)(2,1)S(1)} %shard_map.181.p_ref), custom_call_target="tpu_custom_call" | custom-call | flops 300000000 | bytes 2000000 | tf_op jit(solution)/shard_map/pallas_call | solution.py:483
  34.3 3.5 %shard_map.185 = (f32[10,64,128]{2,1,0:T(8,128)S(1)}, f32[5,64,128]{2,1,0:T(8,128)S(1)}, f32[10,48,128]{2,1,0:T(8,128)S(1)}, f32[15,8,128]{2,1,0:T(8,128)S(1)}, ...) custom-call(f32[10,3,2,8,128]{4,3,2,1,0:T(8,128)S(1)} %get-tuple-ele, ...), custom_call_target="tpu_custom_call" | custom-call | flops 900000000 | bytes 2000000 | tf_op jit(solution)/shard_map/pallas_call | solution.py:483
  37.8 2.6 %collective-permute-start.9 = (f32[15,8,128]{2,1,0:T(8,128)S(1)}, f32[15,8,128]{2,1,0:T(8,128)S(1)}, u32[]{:S(2)}, u32[]{:S(2)}) collective-permute-start(f32[15,8,128]{2,1,0:T(8,128)S(1)} %get-tuple-element.134), channel_id=1, source_target_pairs={{0,16},{16,0},{32,48},{48,32},{64,80},{80,64},{96,112},{112,96},{1... | collective-permute-start | bytes 184328 | tf_op jit(solution)/shard_map/ppermute | solution.py:503
  40.4 3.4 %shard_map.186 = (f32[5,64,128]{2,1,0:T(8,128)S(1)}, f32[384,160]{1,0:T(8,128)S(1)}, f32[8,128]{1,0:T(8,128)S(1)}) custom-call(f32[512,128]{1,0:T(8,128)S(1)} %get-tuple-element.96.x_ref, f32[5,64,128]{2,1,0:T(8,128)S(1)} %get-tuple-element.97.m1_ref, bf16[256,8192]{1,0:T(8,128)(2,1)S(1)} %get-tuple-element.98.hh_ref, ...), custom_call_target="tpu_custom_call" | custom-call | flops 600000000 | bytes 2000000 | tf_op jit(solution)/shard_map/pallas_call | solution.py:483
  44.0 2.0 %shard_map.187 = f32[48,128]{1,0:T(8,128)S(1)} custom-call(f32[512,128]{1,0:T(8,128)S(1)} %get-tuple-element.91.x_ref, f32[512,128]{1,0:T(8,128)S(1)} %get-tuple-element.92.c_ref, bf16[128,8192]{1,0:T(8,128)(2,1)S(1)} %get-tuple-element.93.ha_ref, bf16[128,8192]{1,0:T(8,128)(2,1)S(1)} %get-tuple-element.94.hb_ref, ...), custom_call_target="tpu_custom_call" | custom-call | flops 300000000 | bytes 2000000 | tf_op jit(solution)/shard_map/pallas_call | solution.py:483
  46.0 2.5 %collective-permute-start.10 = (f32[24,128]{1,0:T(8,128)S(1)}, f32[24,128]{1,0:T(8,128)S(1)}, u32[]{:S(2)}, u32[]{:S(2)}) collective-permute-start(f32[24,128]{1,0:T(8,128)S(1)} %slice_select_fusion), channel_id=1, source_target_pairs={{0,16},{1,17},{2,18},{3,19},{4,20},{5,21},{6,22},{7,23},{8,24},{9,... | collective-permute-start | bytes 36872 | tf_op jit(solution)/shard_map/ppermute | solution.py:542
  49.5 6.0 %collective-permute-start.11 = (f32[10,8,128]{2,1,0:T(8,128)S(1)}, f32[10,8,128]{2,1,0:T(8,128)S(1)}, u32[]{:S(2)}, u32[]{:S(2)}) collective-permute-start(f32[10,8,128]{2,1,0:T(8,128)S(1)} %get-tuple-element.147), channel_id=1, source_target_pairs={{0,15},{1,2},{2,1},{3,4},{4,3},{5,6},{6,5},{7,8},{8,7},{9,10},{10,... | collective-permute-start | bytes 122888 | tf_op jit(solution)/shard_map/ppermute | solution.py:504
  56.1 3.4 %all-to-all-start = ((f32[8,24,128]{2,1,0:T(8,128)}), f32[8,24,128]{2,1,0:T(8,128)S(1)}, u32[]{:S(2)}, u32[]{:S(2)}) async-start(f32[8,24,128]{2,1,0:T(8,128)} %broadcast_in_dim.4), calls=%async_computation | async-start | bytes 196608 | tf_op jit(solution)/shard_map/all_to_all | solution.py:525
  59.5 1.9 %shard_map.189 = (f32[5,64,128]{2,1,0:T(8,128)}, f32[5,64,128]{2,1,0:T(8,128)}) custom-call(f32[10,3,2,8,128]{4,3,2,1,0:T(8,128)S(1)} %get-tuple-element.111.w_ref, f32[10,8,128]{2,1,0:T(8,128)S(1)} %get-tuple-element.145.yl_ref, f32[10,8,128]{2,1,0:T(8,128)S(1)} %get-tuple-element.144.yr_ref, f32[16,128]{1,0:T(8,128)S(1)} %get-tuple-element.79.mk_ref, ...), custom_call_target="tpu_custom_call" | custom-call | flops 20000000 | bytes 2000000 | tf_op jit(solution)/shard_map/pallas_call | solution.py:483
  61.4 4.9 %all-to-all-done = f32[8,24,128]{2,1,0:T(8,128)S(1)} async-done(((f32[8,24,128]{2,1,0:T(8,128)}), f32[8,24,128]{2,1,0:T(8,128)S(1)}, u32[]{:S(2)}, u32[]{:S(2)}) %all-to-all-start) | async-done | bytes 98336 | tf_op jit(solution)/shard_map/all_to_all | solution.py:525
  66.4 9.8 %all_to_all.10 = f32[16,24,128]{2,1,0:T(8,128)S(1)} all-to-all(f32[16,24,128]{2,1,0:T(8,128)S(1)} %broadcast_in_dim.5), channel_id=1, replica_groups={{0,1,2,3,32,33,34,35,64,65,66,67,96,97,98,99},{4,5,6,7,36,37,38,39,68,6..., dimensions={0} | all-to-all | bytes 393216 | tf_op jit(solution)/shard_map/all_to_all | solution.py:525
  76.2 3.2 %collective-permute-start.13 = (f32[24,128]{1,0:T(8,128)S(1)}, f32[24,128]{1,0:T(8,128)S(1)}, u32[]{:S(2)}, u32[]{:S(2)}) collective-permute-start(f32[24,128]{1,0:T(8,128)S(1)} %reduce_sum.19), channel_id=1, source_target_pairs={{0,16},{1,17},{2,18},{3,19},{4,20},{5,21},{6,22},{7,23},{8,24},{9,... | collective-permute-start | bytes 36872 | tf_op jit(solution)/shard_map/ppermute | solution.py:551
  79.4 0.8 %collective-permute-done.13 = f32[24,128]{1,0:T(8,128)S(1)} collective-permute-done((f32[24,128]{1,0:T(8,128)S(1)}, f32[24,128]{1,0:T(8,128)S(1)}, u32[]{:S(2)}, u32[]{:S(2)}) %collective-permute-start.13) | collective-permute-done | bytes 12320 | tf_op jit(solution)/shard_map/ppermute | solution.py:551
  80.2 0.7 shard_map.190
  (38 shorter events, 3.5 us)
Async XLA Ops:
  2.3 4.2 %collective-permute-start.1 = (f32[18,8,128]{2,1,0:T(8,128)S(1)}, f32[18,8,128]{2,1,0:T(8,128)S(1)}, u32[]{:S(2)}, u32[]{:S(2)}) collective-permute-start(f32[18,8,128]{2,1,0:T(8,128)S(1)} %get-tuple-element.130), channel_id=1, source_target_pairs={{0,16},{16,0},{32,48},{48,32},{64,80},{80,64},{96,112},{112,96},{1... | collective-permute-start | bytes 221192 | tf_op jit(solution)/shard_map/ppermute | solution.py:503
  5.6 3.8 %collective-permute-start = (f32[18,8,128]{2,1,0:T(8,128)S(1)}, f32[18,8,128]{2,1,0:T(8,128)S(1)}, u32[]{:S(2)}, u32[]{:S(2)}) collective-permute-start(f32[18,8,128]{2,1,0:T(8,128)S(1)} %get-tuple-element.131), channel_id=1, source_target_pairs={{0,240},{16,32},{32,16},{48,64},{64,48},{80,96},{96,80},{112,128},... | collective-permute-start | bytes 221192 | tf_op jit(solution)/shard_map/ppermute | solution.py:504
  9.7 8.2 %collective-permute-start.3 = (f32[11,8,128]{2,1,0:T(8,128)S(1)}, f32[11,8,128]{2,1,0:T(8,128)S(1)}, u32[]{:S(2)}, u32[]{:S(2)}) collective-permute-start(f32[11,8,128]{2,1,0:T(8,128)S(1)} %get-tuple-element.142), channel_id=1, source_target_pairs={{0,1},{1,0},{2,3},{3,2},{4,5},{5,4},{6,7},{7,6},{8,9},{9,8},{10,11... | collective-permute-start | bytes 135176 | tf_op jit(solution)/shard_map/ppermute | solution.py:503
  9.8 8.5 %collective-permute-start.2 = (f32[11,8,128]{2,1,0:T(8,128)S(1)}, f32[11,8,128]{2,1,0:T(8,128)S(1)}, u32[]{:S(2)}, u32[]{:S(2)}) collective-permute-start(f32[11,8,128]{2,1,0:T(8,128)S(1)} %get-tuple-element.143), channel_id=1, source_target_pairs={{0,15},{1,2},{2,1},{3,4},{4,3},{5,6},{6,5},{7,8},{8,7},{9,10},{10,... | collective-permute-start | bytes 135176 | tf_op jit(solution)/shard_map/ppermute | solution.py:504
  18.8 4.3 %collective-permute-start.5 = (f32[15,8,128]{2,1,0:T(8,128)S(1)}, f32[15,8,128]{2,1,0:T(8,128)S(1)}, u32[]{:S(2)}, u32[]{:S(2)}) collective-permute-start(f32[15,8,128]{2,1,0:T(8,128)S(1)} %get-tuple-element.138), channel_id=1, source_target_pairs={{0,16},{16,0},{32,48},{48,32},{64,80},{80,64},{96,112},{112,96},{1... | collective-permute-start | bytes 184328 | tf_op jit(solution)/shard_map/ppermute | solution.py:503
  22.2 3.6 %collective-permute-start.4 = (f32[15,8,128]{2,1,0:T(8,128)S(1)}, f32[15,8,128]{2,1,0:T(8,128)S(1)}, u32[]{:S(2)}, u32[]{:S(2)}) collective-permute-start(f32[15,8,128]{2,1,0:T(8,128)S(1)} %get-tuple-element.139), channel_id=1, source_target_pairs={{0,240},{16,32},{32,16},{48,64},{64,48},{80,96},{96,80},{112,128},... | collective-permute-start | bytes 184328 | tf_op jit(solution)/shard_map/ppermute | solution.py:504
  26.1 8.1 %collective-permute-start.7 = (f32[10,8,128]{2,1,0:T(8,128)S(1)}, f32[10,8,128]{2,1,0:T(8,128)S(1)}, u32[]{:S(2)}, u32[]{:S(2)}) collective-permute-start(f32[10,8,128]{2,1,0:T(8,128)S(1)} %get-tuple-element.150), channel_id=1, source_target_pairs={{0,1},{1,0},{2,3},{3,2},{4,5},{5,4},{6,7},{7,6},{8,9},{9,8},{10,11... | collective-permute-start | bytes 122888 | tf_op jit(solution)/shard_map/ppermute | solution.py:503
  26.2 8.0 %collective-permute-start.6 = (f32[10,8,128]{2,1,0:T(8,128)S(1)}, f32[10,8,128]{2,1,0:T(8,128)S(1)}, u32[]{:S(2)}, u32[]{:S(2)}) collective-permute-start(f32[10,8,128]{2,1,0:T(8,128)S(1)} %get-tuple-element.151), channel_id=1, source_target_pairs={{0,15},{1,2},{2,1},{3,4},{4,3},{5,6},{6,5},{7,8},{8,7},{9,10},{10,... | collective-permute-start | bytes 122888 | tf_op jit(solution)/shard_map/ppermute | solution.py:504
  37.8 6.0 %collective-permute-start.9 = (f32[15,8,128]{2,1,0:T(8,128)S(1)}, f32[15,8,128]{2,1,0:T(8,128)S(1)}, u32[]{:S(2)}, u32[]{:S(2)}) collective-permute-start(f32[15,8,128]{2,1,0:T(8,128)S(1)} %get-tuple-element.134), channel_id=1, source_target_pairs={{0,16},{16,0},{32,48},{48,32},{64,80},{80,64},{96,112},{112,96},{1... | collective-permute-start | bytes 184328 | tf_op jit(solution)/shard_map/ppermute | solution.py:503
  40.4 3.6 %collective-permute-start.8 = (f32[15,8,128]{2,1,0:T(8,128)S(1)}, f32[15,8,128]{2,1,0:T(8,128)S(1)}, u32[]{:S(2)}, u32[]{:S(2)}) collective-permute-start(f32[15,8,128]{2,1,0:T(8,128)S(1)} %get-tuple-element.135), channel_id=1, source_target_pairs={{0,240},{16,32},{32,16},{48,64},{64,48},{80,96},{96,80},{112,128},... | collective-permute-start | bytes 184328 | tf_op jit(solution)/shard_map/ppermute | solution.py:504
  46.0 3.3 %collective-permute-start.10 = (f32[24,128]{1,0:T(8,128)S(1)}, f32[24,128]{1,0:T(8,128)S(1)}, u32[]{:S(2)}, u32[]{:S(2)}) collective-permute-start(f32[24,128]{1,0:T(8,128)S(1)} %slice_select_fusion), channel_id=1, source_target_pairs={{0,16},{1,17},{2,18},{3,19},{4,20},{5,21},{6,22},{7,23},{8,24},{9,... | collective-permute-start | bytes 36872 | tf_op jit(solution)/shard_map/ppermute | solution.py:542
  49.4 10.1 %collective-permute-start.12 = (f32[10,8,128]{2,1,0:T(8,128)S(1)}, f32[10,8,128]{2,1,0:T(8,128)S(1)}, u32[]{:S(2)}, u32[]{:S(2)}) collective-permute-start(f32[10,8,128]{2,1,0:T(8,128)S(1)} %get-tuple-element.146), channel_id=1, source_target_pairs={{0,1},{1,0},{2,3},{3,2},{4,5},{5,4},{6,7},{7,6},{8,9},{9,8},{10,11... | collective-permute-start | bytes 122888 | tf_op jit(solution)/shard_map/ppermute | solution.py:503
  49.5 10.0 %collective-permute-start.11 = (f32[10,8,128]{2,1,0:T(8,128)S(1)}, f32[10,8,128]{2,1,0:T(8,128)S(1)}, u32[]{:S(2)}, u32[]{:S(2)}) collective-permute-start(f32[10,8,128]{2,1,0:T(8,128)S(1)} %get-tuple-element.147), channel_id=1, source_target_pairs={{0,15},{1,2},{2,1},{3,4},{4,3},{5,6},{6,5},{7,8},{8,7},{9,10},{10,... | collective-permute-start | bytes 122888 | tf_op jit(solution)/shard_map/ppermute | solution.py:504
  56.1 10.2 %all-to-all-start = ((f32[8,24,128]{2,1,0:T(8,128)}), f32[8,24,128]{2,1,0:T(8,128)S(1)}, u32[]{:S(2)}, u32[]{:S(2)}) async-start(f32[8,24,128]{2,1,0:T(8,128)} %broadcast_in_dim.4), calls=%async_computation | async-start | bytes 196608 | tf_op jit(solution)/shard_map/all_to_all | solution.py:525
  76.2 4.0 %collective-permute-start.13 = (f32[24,128]{1,0:T(8,128)S(1)}, f32[24,128]{1,0:T(8,128)S(1)}, u32[]{:S(2)}, u32[]{:S(2)}) collective-permute-start(f32[24,128]{1,0:T(8,128)S(1)} %reduce_sum.19), channel_id=1, source_target_pairs={{0,16},{1,17},{2,18},{3,19},{4,20},{5,21},{6,22},{7,23},{8,24},{9,... | collective-permute-start | bytes 36872 | tf_op jit(solution)/shard_map/ppermute | solution.py:551
